TPU v7x, 512 devices: a whole 4x8x8 slice. The times are simulated.
512 devices in a mesh: dp: 32 (over x, y), expert: 16 (over z, core).
Axes of the slice: x: 4, y: 8, z: 8, core: 2. Of those that a mesh axis runs over, the one named last changes fastest.
Arguments:
- tokens: bfloat16 [32768, 2048], P(('dp', 'expert')), may hold values from -6 to 6
- routes: int32 [32768, 8], P(('dp', 'expert')), may hold values from 0 to 127, all different within a row; in each aligned block of 64 rows (0 to 63, 64 to 127, ...) at most 6 rows name the same one
- route_weights: float32 [32768, 8], P(('dp', 'expert')), may hold values from 0.05 to 0.5
- gate_weight: bfloat16 [32, 16, 192, 2048], P('dp', 'expert'), may hold values from -0.125 to 0.125
- up_weight: bfloat16 [32, 16, 192, 2048], P('dp', 'expert'), may hold values from -0.125 to 0.125
- down_weight: bfloat16 [32, 16, 192, 2048], P('dp', 'expert'), may hold values from -0.21875 to 0.21875
Outputs:
- mixed: bfloat16 [32768, 2048], P(('dp', 'expert'))
Inputs may be any that keep to these rules, and one draw needn't show every extreme that they name: `routes`: each token names 8 different experts. Among the tokens of one device no expert is named by more than 6 tokens, a bound that some block reaches.
All inputs are finite; a program needn't handle non-finite values.
Results may differ from a plain program's by a relative error of at most 0.0072.
Values may be sent and summed in bfloat16 or wider, within the bound.
No kernel may reach another device: no remote copies, remote signals or barrier semaphores. Data moves between devices by JAX's collectives and lax.ppermute only.
A program may use at most 128 MiB of HBM per device.

v0:
```python
import jax
import jax.numpy as jnp
from jax import lax
from jax.sharding import PartitionSpec as P

SPLIT = 4


def partner(value, axis, bit):
    mask = 2**bit
    pairs = [(source, source ^ mask) for source in range(lax.axis_size(axis))]
    return lax.ppermute(value, axis, pairs)


def project_rows(rows, panel):
    return lax.dot_general(
        rows, panel, (((1,), (1,)), ((), ())), preferred_element_type=jnp.float32
    )


def add_rounded(first, second):
    first, second = lax.optimization_barrier((first, second))
    return (first.astype(jnp.float32) + second.astype(jnp.float32)).astype(jnp.bfloat16)


def shards(tokens, routes, route_weights, gate_weight, up_weight, down_weight):
    column_count = lax.axis_size("expert")
    row_count = lax.axis_size("dp")
    group_count = row_count // SPLIT
    expert_count = column_count * group_count
    token_count = tokens.shape[0]
    model_width = tokens.shape[1]
    top_count = routes.shape[1]
    part_width = gate_weight.shape[2]
    slot_count = max(2, min(token_count, 3 * token_count * top_count // (2 * expert_count)))
    bit_count = SPLIT.bit_length() - 1
    flat_ids = routes.reshape(-1)
    one_hot = (flat_ids[:, None] == jnp.arange(expert_count, dtype=jnp.int32)[None, :]).astype(
        jnp.int32
    )
    earlier = jnp.cumsum(one_hot, axis=0) - one_hot
    slot_rank = jnp.sum(earlier * one_hot, axis=1)
    owner_column = flat_ids // group_count
    owner_group = flat_ids % group_count
    slot_index = (owner_group * column_count + owner_column) * slot_count + slot_rank
    source_token = jnp.arange(token_count * top_count, dtype=jnp.int32) // top_count
    outgoing = jnp.zeros((expert_count * slot_count, model_width), jnp.bfloat16)
    outgoing = outgoing.at[slot_index].set(tokens[source_token])
    outgoing = outgoing.reshape(group_count, column_count, slot_count, model_width)
    arrived = lax.all_to_all(outgoing, "expert", split_axis=1, concat_axis=1, tiled=True)
    arrived = arrived.reshape(row_count, column_count // SPLIT, slot_count, model_width)
    received = lax.all_to_all(arrived, "dp", split_axis=0, concat_axis=0, tiled=True)
    expert_rows = received.reshape(-1, model_width)
    gate_local = gate_weight[0, 0]
    up_local = up_weight[0, 0]
    down_local = down_weight[0, 0]
    for bit_index in range(bit_count):
        partner_piece = partner((gate_local, up_local, down_local), "dp", bit_index)
        gate_local = jnp.concatenate([gate_local, partner_piece[0]], axis=0)
        up_local = jnp.concatenate([up_local, partner_piece[1]], axis=0)
        down_local = jnp.concatenate([down_local, partner_piece[2]], axis=0)
    gate_value = project_rows(expert_rows, gate_local)
    up_value = project_rows(expert_rows, up_local)
    hidden = (jax.nn.silu(gate_value) * up_value).astype(jnp.bfloat16)
    parts = [
        jnp.dot(
            hidden[:, q * part_width : (q + 1) * part_width],
            down_local[q * part_width : (q + 1) * part_width],
            preferred_element_type=jnp.float32,
        ).astype(jnp.bfloat16)
        for q in range(SPLIT)
    ]
    outputs = add_rounded(add_rounded(parts[0], parts[2]), add_rounded(parts[1], parts[3]))
    outputs = outputs.reshape(row_count, column_count // SPLIT, slot_count, model_width)
    returned = lax.all_to_all(outputs, "dp", split_axis=0, concat_axis=0, tiled=True)
    returned = returned.reshape(group_count, column_count, slot_count, model_width)
    returned = lax.all_to_all(returned, "expert", split_axis=1, concat_axis=1, tiled=True)
    results = returned.reshape(-1, model_width)
    picked = results[slot_index].astype(jnp.float32) * route_weights.reshape(-1)[:, None]
    mixed = jnp.sum(picked.reshape(token_count, top_count, model_width), axis=1)
    return mixed.astype(jnp.bfloat16)


def solution(mesh):
    placed = (
        P(("dp", "expert"), None),
        P(("dp", "expert"), None),
        P(("dp", "expert"), None),
        P("dp", "expert", None, None),
        P("dp", "expert", None, None),
        P("dp", "expert", None, None),
    )
    return jax.shard_map(
        shards, mesh=mesh, in_specs=placed, out_specs=P(("dp", "expert"), None), check_vma=False
    )
```

profile of v0, /device:TPU:1, one launch (start us, length us, event | category | flops | bytes accessed | tf_op | source)
XLA Modules:
  0.0 631.6 jit_solution(4489176998835835529)
XLA Ops:
  0.0 0.8 copy.24
  1.2 0.2 fusion.24
  1.6 0.2 fusion.23
  1.8 11.8 %scatter_custom_fusion = bf16[768,2048]{1,0:T(8,128)(2,1)S(1)} fusion(s32[512]{0:T(512)S(1)} %bitcast.45, bf16[64,2048]{1,0:T(8,128)(2,1)S(1)} %copy-done, s32[1024]{0:T(1024)S(1)} %pad_clamp_fusion.1, bf16[]{:T(256)} %constant.45.clone.1), kind=kCustom, calls=%fused_computation.25 | custom fusion | bytes 3145730 | tf_op jit(solution)/shard_map/scatter | solution.py:48
  13.6 2.9 reshape.213
  16.5 4.2 copy.29
  20.7 85.1 %all_to_all.20 = bf16[8,16,6,2048]{3,0,2,1:T(8,128)(2,1)S(1)} all-to-all(bf16[8,16,6,2048]{3,0,2,1:T(8,128)(2,1)S(1)} %copy.29), channel_id=1, replica_groups=mesh['dp'=32,'expert'=16] {'expert'}, dimensions={1} | all-to-all | bytes 6291456 | tf_op jit(solution)/shard_map/all_to_all | solution.py:50
  105.8 1.7 copy.30
  107.6 3.2 reshape.214
  110.8 5.7 copy.31
  116.5 9.7 %all-to-all-start.1 = ((bf16[32,4,6,2048]{3,1,2,0:T(4,128)(2,1)}), bf16[32,4,6,2048]{3,1,2,0:T(4,128)(2,1)S(1)}, u32[]{:S(2)}, u32[]{:S(2)}) async-start(bf16[32,4,6,2048]{3,1,2,0:T(4,128)(2,1)} %copy.31), calls=%async_computation.1 | async-start | bytes 6291456 | tf_op jit(solution)/shard_map/all_to_all | solution.py:52
  126.2 3.3 collective-permute-start
  129.5 2.1 collective-permute-start.2
  131.6 81.9 %collective-permute-done = bf16[192,2048]{1,0:T(8,128)(2,1)S(1)} collective-permute-done((bf16[192,2048]{1,0:T(8,128)(2,1)}, bf16[192,2048]{1,0:T(8,128)(2,1)S(1)}, u32[]{:S(2)}, u32[]{:S(2)}) %collective-permute-start) | collective-permute-done | bytes 786464 | tf_op jit(solution)/shard_map/ppermute | solution.py:12
  213.5 2.7 pad_maximum_fusion
  216.2 3.7 collective-permute-start.1
  220.0 1.9 collective-permute-start.4
  221.9 18.3 %collective-permute-done.2 = bf16[192,2048]{1,0:T(8,128)(2,1)S(1)} collective-permute-done((bf16[192,2048]{1,0:T(8,128)(2,1)}, bf16[192,2048]{1,0:T(8,128)(2,1)S(1)}, u32[]{:S(2)}, u32[]{:S(2)}) %collective-permute-start.2) | collective-permute-done | bytes 786464 | tf_op jit(solution)/shard_map/ppermute | solution.py:12
  240.2 1.4 pad_maximum_fusion.1
  241.6 1.9 collective-permute-start.3
  243.5 35.7 %collective-permute-done.4 = bf16[192,2048]{1,0:T(8,128)(2,1)S(1)} collective-permute-done((bf16[192,2048]{1,0:T(8,128)(2,1)S(1)}, bf16[192,2048]{1,0:T(8,128)(2,1)S(1)}, u32[]{:S(2)}, u32[]{:S(2)}) %collective-permute-start.4) | collective-permute-done | bytes 786464 | tf_op jit(solution)/shard_map/ppermute | solution.py:12
  279.2 1.4 pad_maximum_fusion.2
  280.7 5.6 collective-permute-start.5
  286.3 4.3 copy.32
  290.6 5.0 reshape.215
  295.7 61.1 %collective-permute-done.1 = bf16[384,2048]{1,0:T(8,128)(2,1)} collective-permute-done((bf16[384,2048]{1,0:T(8,128)(2,1)}, bf16[384,2048]{1,0:T(8,128)(2,1)}, u32[]{:S(2)}, u32[]{:S(2)}) %collective-permute-start.1) | collective-permute-done | bytes 1572896 | tf_op jit(solution)/shard_map/ppermute | solution.py:12
  356.8 4.5 fusion.1
  361.3 29.2 %collective-permute-done.3 = bf16[384,2048]{1,0:T(8,128)(2,1)} collective-permute-done((bf16[384,2048]{1,0:T(8,128)(2,1)}, bf16[384,2048]{1,0:T(8,128)(2,1)}, u32[]{:S(2)}, u32[]{:S(2)}) %collective-permute-start.3) | collective-permute-done | bytes 1572896 | tf_op jit(solution)/shard_map/ppermute | solution.py:12
  390.5 4.2 multiply_convert_fusion
  394.7 1.0 convolution_convert_fusion.3
  395.7 28.5 %collective-permute-done.5 = bf16[384,2048]{1,0:T(8,128)(2,1)} collective-permute-done((bf16[384,2048]{1,0:T(8,128)(2,1)}, bf16[384,2048]{1,0:T(8,128)(2,1)}, u32[]{:S(2)}, u32[]{:S(2)}) %collective-permute-start.5) | collective-permute-done | bytes 1572896 | tf_op jit(solution)/shard_map/ppermute | solution.py:12
  424.2 2.1 convolution_convert_fusion.2
  426.4 2.2 convolution_convert_fusion
  428.6 1.0 convolution_convert_fusion.1
  429.6 6.4 %add_convert_fusion.1 = (bf16[768,2048]{1,0:T(8,128)(2,1)}, bf16[768,2048]{1,0:T(8,128)(2,1)}) fusion(bf16[768,2048]{1,0:T(8,128)(2,1)S(1)} %convolution_convert_fusion, bf16[768,2048]{1,0:T(8,128)(2,1)S(1)} %convolution_convert_fusion.1, bf16[768,2048]{1,0:T(8,128)(2,1)S(1)} %convolution_convert_fusion.2, bf16[768,2048]{1,0:T(8,128)(2,1)S(1)} %convolution_convert_fusion.3), kind=kLoop, calls=%fused_computation.4 | loop fusion | flops 12582912 | bytes 18874368 | tf_op jit(solution)/shard_map/convert_element_type | solution.py:23
  436.0 4.4 add_convert_fusion
  440.4 2.9 reshape.216
  443.3 5.2 copy.33
  448.5 76.8 %all_to_all.21 = bf16[32,4,6,2048]{3,1,2,0:T(4,128)(2,1)S(1)} all-to-all(bf16[32,4,6,2048]{3,1,2,0:T(4,128)(2,1)S(1)} %copy.33), channel_id=1, replica_groups=mesh['dp'=32,'expert'=16] {'dp'}, dimensions={0} | all-to-all | bytes 6291456 | tf_op jit(solution)/shard_map/all_to_all | solution.py:75
  525.3 1.5 copy.34
  526.8 3.0 reshape.217
  529.8 5.3 copy.35
  535.1 9.0 %all-to-all-start.3 = ((bf16[8,16,6,2048]{3,0,2,1:T(8,128)(2,1)}), bf16[8,16,6,2048]{3,0,2,1:T(8,128)(2,1)S(1)}, u32[]{:S(2)}, u32[]{:S(2)}) async-start(bf16[8,16,6,2048]{3,0,2,1:T(8,128)(2,1)} %copy.35), calls=%async_computation.3 | async-start | bytes 6291456 | tf_op jit(solution)/shard_map/all_to_all | solution.py:77
  544.3 70.9 %all-to-all-done.3 = bf16[8,16,6,2048]{3,0,2,1:T(8,128)(2,1)S(1)} async-done(((bf16[8,16,6,2048]{3,0,2,1:T(8,128)(2,1)}), bf16[8,16,6,2048]{3,0,2,1:T(8,128)(2,1)S(1)}, u32[]{:S(2)}, u32[]{:S(2)}) %all-to-all-start.3) | async-done | bytes 3145760 | tf_op jit(solution)/shard_map/all_to_all | solution.py:77
  615.1 3.7 copy.36
  618.8 4.9 reshape.218
  623.7 3.3 gather_fusion
  627.1 4.1 fusion
  (40 shorter events, 0.7 us)
Async XLA Ops:
  0.0 1.8 copy-start
  116.5 169.8 %all-to-all-start.1 = ((bf16[32,4,6,2048]{3,1,2,0:T(4,128)(2,1)}), bf16[32,4,6,2048]{3,1,2,0:T(4,128)(2,1)S(1)}, u32[]{:S(2)}, u32[]{:S(2)}) async-start(bf16[32,4,6,2048]{3,1,2,0:T(4,128)(2,1)} %copy.31), calls=%async_computation.1 | async-start | bytes 6291456 | tf_op jit(solution)/shard_map/all_to_all | solution.py:52
  126.2 93.8 %copy-start.2 = (bf16[1,1,192,2048]{3,2,1,0:T(8,128)(2,1)S(1)}, bf16[1,1,192,2048]{3,2,1,0:T(8,128)(2,1)}, u32[]{:S(2)}) copy-start(bf16[1,1,192,2048]{3,2,1,0:T(8,128)(2,1)} %param.11) | copy-start | bytes 2359300
  126.2 114.0 %copy-start.6 = (bf16[1,1,192,2048]{3,2,1,0:T(8,128)(2,1)S(1)}, bf16[1,1,192,2048]{3,2,1,0:T(8,128)(2,1)}, u32[]{:S(2)}) copy-start(bf16[1,1,192,2048]{3,2,1,0:T(8,128)(2,1)} %param.10) | copy-start | bytes 2359300
  126.2 87.3 %collective-permute-start = (bf16[192,2048]{1,0:T(8,128)(2,1)}, bf16[192,2048]{1,0:T(8,128)(2,1)S(1)}, u32[]{:S(2)}, u32[]{:S(2)}) collective-permute-start(bf16[192,2048]{1,0:T(8,128)(2,1)} %bitcast.37), channel_id=1, source_target_pairs={{0,16},{16,0},{32,48},{48,32},{64,80},{80,64},{96,112},{112,96},{1... | collective-permute-start | bytes 2359304 | tf_op jit(solution)/shard_map/ppermute | solution.py:12
  129.5 110.7 %collective-permute-start.2 = (bf16[192,2048]{1,0:T(8,128)(2,1)}, bf16[192,2048]{1,0:T(8,128)(2,1)S(1)}, u32[]{:S(2)}, u32[]{:S(2)}) collective-permute-start(bf16[192,2048]{1,0:T(8,128)(2,1)} %bitcast.40), channel_id=1, source_target_pairs={{0,16},{16,0},{32,48},{48,32},{64,80},{80,64},{96,112},{112,96},{1... | collective-permute-start | bytes 2359304 | tf_op jit(solution)/shard_map/ppermute | solution.py:12
  213.5 6.5 %copy-start.10 = (bf16[192,2048]{1,0:T(8,128)(2,1)}, bf16[192,2048]{1,0:T(8,128)(2,1)S(1)}, u32[]{:S(2)}) copy-start(bf16[192,2048]{1,0:T(8,128)(2,1)S(1)} %collective-permute-done) | copy-start | bytes 2359300
  216.2 140.6 %collective-permute-start.1 = (bf16[384,2048]{1,0:T(8,128)(2,1)}, bf16[384,2048]{1,0:T(8,128)(2,1)}, u32[]{:S(2)}, u32[]{:S(2)}) collective-permute-start(bf16[384,2048]{1,0:T(8,128)(2,1)} %pad_maximum_fusion), channel_id=1, source_target_pairs={{0,32},{16,48},{32,0},{48,16},{64,96},{80,112},{96,64},{112,80},{1... | collective-permute-start | bytes 4718600 | tf_op jit(solution)/shard_map/ppermute | solution.py:12
  220.0 59.2 %collective-permute-start.4 = (bf16[192,2048]{1,0:T(8,128)(2,1)S(1)}, bf16[192,2048]{1,0:T(8,128)(2,1)S(1)}, u32[]{:S(2)}, u32[]{:S(2)}) collective-permute-start(bf16[192,2048]{1,0:T(8,128)(2,1)S(1)} %bitcast.33), channel_id=1, source_target_pairs={{0,16},{16,0},{32,48},{48,32},{64,80},{80,64},{96,112},{112,96},{1... | collective-permute-start | bytes 2359304 | tf_op jit(solution)/shard_map/ppermute | solution.py:12
  240.2 40.4 %copy-start.8 = (bf16[192,2048]{1,0:T(8,128)(2,1)}, bf16[192,2048]{1,0:T(8,128)(2,1)S(1)}, u32[]{:S(2)}) copy-start(bf16[192,2048]{1,0:T(8,128)(2,1)S(1)} %collective-permute-done.2) | copy-start | bytes 2359300
  241.6 148.9 %collective-permute-start.3 = (bf16[384,2048]{1,0:T(8,128)(2,1)}, bf16[384,2048]{1,0:T(8,128)(2,1)}, u32[]{:S(2)}, u32[]{:S(2)}) collective-permute-start(bf16[384,2048]{1,0:T(8,128)(2,1)} %pad_maximum_fusion.1), channel_id=1, source_target_pairs={{0,32},{16,48},{32,0},{48,16},{64,96},{80,112},{96,64},{112,80},{1... | collective-permute-start | bytes 4718600 | tf_op jit(solution)/shard_map/ppermute | solution.py:12
  279.2 1.5 copy-start.4
  280.7 143.5 %collective-permute-start.5 = (bf16[384,2048]{1,0:T(8,128)(2,1)}, bf16[384,2048]{1,0:T(8,128)(2,1)}, u32[]{:S(2)}, u32[]{:S(2)}) collective-permute-start(bf16[384,2048]{1,0:T(8,128)(2,1)} %pad_maximum_fusion.2), channel_id=1, source_target_pairs={{0,32},{16,48},{32,0},{48,16},{64,96},{80,112},{96,64},{112,80},{1... | collective-permute-start | bytes 4718600 | tf_op jit(solution)/shard_map/ppermute | solution.py:12
  295.7 94.8 %copy-start.7 = (bf16[1,1,192,2048]{3,2,1,0:T(8,128)(2,1)S(1)}, bf16[1,1,192,2048]{3,2,1,0:T(8,128)(2,1)}, u32[]{:S(2)}) copy-start(bf16[1,1,192,2048]{3,2,1,0:T(8,128)(2,1)} %param.10) | copy-start | bytes 2359300
  295.7 94.8 %copy-start.9 = (bf16[192,2048]{1,0:T(8,128)(2,1)S(1)}, bf16[192,2048]{1,0:T(8,128)(2,1)}, u32[]{:S(2)}) copy-start(bf16[192,2048]{1,0:T(8,128)(2,1)} %copy-done.8) | copy-start | bytes 2359300
  361.3 33.4 %copy-start.3 = (bf16[1,1,192,2048]{3,2,1,0:T(8,128)(2,1)S(1)}, bf16[1,1,192,2048]{3,2,1,0:T(8,128)(2,1)}, u32[]{:S(2)}) copy-start(bf16[1,1,192,2048]{3,2,1,0:T(8,128)(2,1)} %param.11) | copy-start | bytes 2359300
  426.3 2.2 copy-start.5
  535.1 9.0 %copy-start.11 = (f32[64,8]{0,1:T(8,128)S(1)}, f32[64,8]{0,1:T(8,128)}, u32[]{:S(2)}) copy-start(f32[64,8]{0,1:T(8,128)} %param.8) | copy-start | bytes 6148
  535.1 80.0 %all-to-all-start.3 = ((bf16[8,16,6,2048]{3,0,2,1:T(8,128)(2,1)}), bf16[8,16,6,2048]{3,0,2,1:T(8,128)(2,1)S(1)}, u32[]{:S(2)}, u32[]{:S(2)}) async-start(bf16[8,16,6,2048]{3,0,2,1:T(8,128)(2,1)} %copy.35), calls=%async_computation.3 | async-start | bytes 6291456 | tf_op jit(solution)/shard_map/all_to_all | solution.py:77
  623.7 7.5 %copy-start.1 = (bf16[64,2048]{1,0:T(8,128)(2,1)S(1)}, bf16[64,2048]{1,0:T(8,128)(2,1)}, u32[]{:S(2)}) copy-start(bf16[64,2048]{1,0:T(8,128)(2,1)} %param.6) | copy-start | bytes 786436
where the time goes:
time: 641 us; the launch traced here: 632 us
  waiting for transfers between devices  325 us (51%)
  blocking collectives  162 us (25%)
  local copies, waits for them, and re-layouts  70 us (11%)
  starting transfers between devices  37.3 us (6%)
  other arithmetic  21 us (3%)
  matrix products  15.1 us (2%)
    ppermute x6, waiting for transfers between devices, partner(): return lax.ppermute(value, axis, pairs)  255 us
    all_to_all x1, blocking collectives, shards(): lax.all_to_all(outgoing, 'expert', split_axis=1, concat_axis=1, tiled=True)  85.1 us
    all_to_all x1, blocking collectives, shards(): lax.all_to_all(outputs, 'dp', split_axis=0, concat_axis=0, tiled=True)  76.8 us
    all_to_all x1, waiting for transfers between devices, shards(): lax.all_to_all(returned, 'expert', split_axis=1, concat_axis=1, tiled=True)  70.9 us
    ppermute x6, starting transfers between devices, partner(): return lax.ppermute(value, axis, pairs)  18.6 us
  transfers between devices with their start and end apart: 8, of which 7 were waited for; matrix products, arithmetic and copies ran while one was open for 4% of the time, Pallas kernels for 0%

commit v1 on v0

v1 whole, which is shorter than its diff:
```python
import jax
import jax.numpy as jnp
from jax import lax
from jax.experimental import pallas as pl
from jax.experimental.pallas import tpu as pltpu
from jax.sharding import Mesh, PartitionSpec as P

SIZES = (4, 2, 2, 2, 8, 2)
NAMES = ("x", "h", "p", "b", "z", "c")
MOST = 6
CHUNKS = 4
PLANE = 32
EXTRA = 128


def flips(axes):
    return [(i, i ^ (2 ** len(axes) - 1)) for i in range(2 ** len(axes))]


def place(p, b, c):
    return p * 4 + b * 2 + c


FIRST = [
    (place(1, 0, 0), place(0, 1, 1)),
    (place(1, 1, 0), place(0, 0, 1)),
    (place(0, 1, 1), place(1, 0, 0)),
    (place(0, 0, 1), place(1, 1, 0)),
    (place(0, 0, 0), place(0, 1, 0)),
    (place(0, 1, 0), place(0, 0, 0)),
    (place(1, 0, 1), place(1, 1, 1)),
    (place(1, 1, 1), place(1, 0, 1)),
]
SECOND = [
    (place(0, 0, 1), place(0, 1, 1)),
    (place(0, 1, 1), place(0, 0, 1)),
    (place(1, 0, 0), place(1, 1, 0)),
    (place(1, 1, 0), place(1, 0, 0)),
]
PARTNERS = (("p",), ("h", "p", "b"), ("h", "b"))


def swap(value, axes):
    return lax.ppermute(value, axes, flips(axes))


def expert_kernel(rows_ref, *refs):
    gates, ups, downs, out_ref = refs[0:4], refs[4:8], refs[8:12], refs[12]
    rows = rows_ref[...]
    total = None
    for gate, up, down in zip(gates, ups, downs):
        dims = (((1,), (1,)), ((), ()))
        g = lax.dot_general(rows, gate[...], dims, preferred_element_type=jnp.float32)
        u = lax.dot_general(rows, up[...], dims, preferred_element_type=jnp.float32)
        hidden = (g / (1.0 + jnp.exp(-g)) * u).astype(jnp.bfloat16)
        part = jnp.dot(hidden, down[...], preferred_element_type=jnp.float32)
        total = part if total is None else total + part
    out_ref[...] = total.astype(jnp.bfloat16)


def run_expert(rows, gates, ups, downs):
    count, width = rows.shape
    hid = gates[0].shape[0]
    tile = 256
    whole = pl.BlockSpec((hid, width), lambda i: (0, 0))
    block = pl.BlockSpec((tile, width), lambda i: (i, 0))
    return pl.pallas_call(
        expert_kernel,
        grid=(count // tile,),
        out_shape=jax.ShapeDtypeStruct((count, width), jnp.bfloat16),
        in_specs=[block] + [whole] * 12,
        out_specs=block,
        compiler_params=pltpu.CompilerParams(vmem_limit_bytes=48 * 1024 * 1024),
        cost_estimate=pl.CostEstimate(
            flops=2 * count * width * hid * 12,
            bytes_accessed=4 * count * width + 24 * hid * width,
            transcendentals=count * hid * 4,
        ),
    )(rows, *gates, *ups, *downs)


def shards(tokens, routes, route_weights, gate_weight, up_weight, down_weight):
    count, width = tokens.shape
    top = routes.shape[1]
    x, h, p, z, c = (lax.axis_index(n) for n in ("x", "h", "p", "z", "c"))

    high = route_weights.astype(jnp.bfloat16)
    low = (route_weights - high.astype(jnp.float32)).astype(jnp.bfloat16)
    fields = (routes.astype(jnp.bfloat16), high, low)
    meta = sum(
        jnp.pad(f, ((0, 0), (top * k, EXTRA - top * (k + 1)))) for k, f in enumerate(fields)
    )
    record = jnp.concatenate([tokens, meta], axis=1)
    records = [record] + [swap(record, axes) for axes in PARTNERS]

    own = [gate_weight[0, 0], up_weight[0, 0], down_weight[0, 0]]
    axes = ("p", "b", "c")
    first = [lax.ppermute(w, axes, FIRST) for w in own]
    second = [lax.ppermute(w, axes, SECOND) for w in first]
    second = [jnp.where(c == p, mine, got) for mine, got in zip(own, second)]
    third = [swap(w, ("c",)) for w in first]
    fourth = [swap(w, ("c",)) for w in second]
    pieces = [list(four) for four in zip(first, second, third, fourth)]

    held = jnp.concatenate(records, axis=0)
    rows = held[:, :width]
    meta = held[:, width:].astype(jnp.float32)
    named = meta[:, :top].astype(jnp.int32)
    weight = meta[:, top : 2 * top] + meta[:, 2 * top : 3 * top]
    target = jnp.arange(PLANE, dtype=jnp.int32)
    expert = (2 * (target % 8) + p) * 8 + 2 * (target // 8) + h
    match = named[:, :, None] == expert[None, None, :]
    chosen = jnp.any(match, axis=1)
    weight = jnp.sum(jnp.where(match, weight[:, :, None], 0.0), axis=1)
    order = jnp.arange(CHUNKS * count, dtype=jnp.int32)
    before = (order[:, None] // count == order[None, :] // count) & (order[None, :] < order[:, None])
    rank = jnp.dot(
        before.astype(jnp.bfloat16), chosen.astype(jnp.bfloat16), preferred_element_type=jnp.float32
    ).astype(jnp.int32)
    slot = jnp.where(chosen, rank + (order // count * MOST)[:, None], -1).T
    slots = jnp.arange(CHUNKS * MOST, dtype=jnp.int32)
    hit = (slot[:, None, :] == slots[None, :, None]).reshape(PLANE * CHUNKS * MOST, CHUNKS * count)
    outgoing = jnp.dot(
        hit.astype(jnp.bfloat16), rows, preferred_element_type=jnp.float32
    ).astype(jnp.bfloat16)
    share = (PLANE, CHUNKS * MOST, width)
    arrived = lax.all_to_all(outgoing.reshape(share), ("x", "z"), 0, 0, tiled=True)

    results = run_expert(arrived.reshape(-1, width), *pieces)

    returned = lax.all_to_all(results.reshape(share), ("x", "z"), 0, 0, tiled=True)
    returned = returned.reshape(-1, width)
    spread = jnp.broadcast_to(
        weight.T[:, None, :], (PLANE, CHUNKS * MOST, CHUNKS * count)
    ).reshape(hit.shape)
    spread = jnp.where(hit, spread, 0.0)
    upper = spread.astype(jnp.bfloat16)
    lower = (spread - upper.astype(jnp.float32)).astype(jnp.bfloat16)
    dims = (((0,), (0,)), ((), ()))
    partial = lax.dot_general(
        upper, returned, dims, preferred_element_type=jnp.float32
    ) + lax.dot_general(lower, returned, dims, preferred_element_type=jnp.float32)
    mixed = partial[:count]
    for k, names in enumerate(PARTNERS, 1):
        sent = partial[k * count : (k + 1) * count].astype(jnp.bfloat16)
        mixed = mixed + swap(sent, names).astype(jnp.float32)
    return mixed.astype(jnp.bfloat16)


def solution(mesh):
    fine = Mesh(mesh.devices.reshape(SIZES), NAMES)
    rows = P(NAMES, None)
    weights = P(("x", "h", "p", "b"), ("z", "c"), None, None)
    return jax.shard_map(
        shards,
        mesh=fine,
        in_specs=(rows, rows, rows, weights, weights, weights),
        out_specs=rows,
        check_vma=False,
    )
```

time: 641 us -> 281 us (0.44)
  the two profiles are of different devices: /device:TPU:1 before, /device:TPU:4 now
where the time goes in v1:
time: 281 us; the launch traced here: 280 us
  waiting for transfers between devices  165 us (59%)
  starting transfers between devices  81.1 us (29%)
  Pallas kernels  14.7 us (5%)
  local copies, waits for them, and re-layouts  10.4 us (4%)
  matrix products  5.15 us (2%)
  other arithmetic  3.96 us (1%)
    all_to_all x1, waiting for transfers between devices, shards(): lax.all_to_all(results.reshape(share), ('x', 'z'), 0, 0, tiled=True)  71.5 us
    ppermute x3, waiting for transfers between devices, shards(): first = [lax.ppermute(w, axes, FIRST) for w in own]  54.1 us
    ppermute x12, starting transfers between devices, swap(): return lax.ppermute(value, axes, flips(axes))  46 us
    ppermute x12, waiting for transfers between devices, swap(): return lax.ppermute(value, axes, flips(axes))  39.1 us
    pallas_call x1, Pallas kernels, run_expert(): pl.pallas_call(expert_kernel, grid=(count // tile,), out_shape=jax.ShapeD...  14.7 us
    all_to_all x1, starting transfers between devices, shards(): lax.all_to_all(outgoing.reshape(share), ('x', 'z'), 0, 0, tiled=True)  13.6 us
    all_to_all x1, starting transfers between devices, shards(): lax.all_to_all(results.reshape(share), ('x', 'z'), 0, 0, tiled=True)  9.79 us
    unnamed x35, local copies, waits for them, and re-layouts  9.06 us
  transfers between devices with their start and end apart: 20, of which 10 were waited for; matrix products, arithmetic and copies ran while one was open for 1% of the time, Pallas kernels for 0%

profile of v1, /device:TPU:4, one launch (start us, length us, event | category | flops | bytes accessed | tf_op | source)
XLA Modules:
  0.0 280.4 jit_solution(4607168651823826629)
XLA Ops:
  0.0 0.7 convert_element_type.62
  0.7 0.8 subtract_convert_fusion
  1.5 1.2 copy.18
  3.1 6.9 %collective-permute-start.2 = (bf16[64,2176]{1,0:T(8,128)(2,1)S(1)}, bf16[64,2176]{1,0:T(8,128)(2,1)S(1)}, u32[]{:S(2)}, u32[]{:S(2)}) collective-permute-start(bf16[64,2176]{1,0:T(8,128)(2,1)S(1)} %copy.19), channel_id=1, source_target_pairs={{0,80},{16,64},{64,16},{80,0},{1,81},{17,65},{65,17},{81,1},{2,82}... | collective-permute-start | bytes 835592 | tf_op jit(solution)/shard_map/ppermute | solution.py:44
  10.0 2.1 collective-permute-start.1
  12.2 3.2 %collective-permute-start = (bf16[64,2176]{1,0:T(8,128)(2,1)S(1)}, bf16[64,2176]{1,0:T(8,128)(2,1)S(1)}, u32[]{:S(2)}, u32[]{:S(2)}) collective-permute-start(bf16[64,2176]{1,0:T(8,128)(2,1)S(1)} %copy.19), channel_id=1, source_target_pairs={{0,32},{32,0},{1,33},{33,1},{2,34},{34,2},{3,35},{35,3},{4,36},{36... | collective-permute-start | bytes 835592 | tf_op jit(solution)/shard_map/ppermute | solution.py:44
  15.5 13.2 %collective-permute-done.2 = bf16[64,2176]{1,0:T(8,128)(2,1)S(1)} collective-permute-done((bf16[64,2176]{1,0:T(8,128)(2,1)S(1)}, bf16[64,2176]{1,0:T(8,128)(2,1)S(1)}, u32[]{:S(2)}, u32[]{:S(2)}) %collective-permute-start.2) | collective-permute-done | bytes 278560 | tf_op jit(solution)/shard_map/ppermute | solution.py:44
  29.0 5.6 %collective-permute-done.1 = bf16[64,2176]{1,0:T(8,128)(2,1)S(1)} collective-permute-done((bf16[64,2176]{1,0:T(8,128)(2,1)S(1)}, bf16[64,2176]{1,0:T(8,128)(2,1)S(1)}, u32[]{:S(2)}, u32[]{:S(2)}) %collective-permute-start.1) | collective-permute-done | bytes 278560 | tf_op jit(solution)/shard_map/ppermute | solution.py:44
  34.6 0.3 copy.23
  35.1 0.3 copy.22
  36.1 2.9 %convolution_convert_fusion = bf16[768,2048]{1,0:T(8,128)(2,1)} fusion(pred[768,256]{1,0:T(32,128)(4,1)S(1)} %bitcast_compare_fusion, bf16[64,2176]{0,1:T(8,128)(2,1)S(1)} %copy.24, bf16[64,2176]{0,1:T(8,128)(2,1)S(1)} %copy.23, bf16[64,2176]{0,1:T(8,128)(2,1)S(1)} %copy.22, bf16[64,128]{0,1:T(8,128)(2,1)S(1)} %pad_add_fusion, bf16[64,2048]{0,1:T(8,128)(2,1)S(1)} %copy.18), kind=kOutput, calls=%fused_computation | convolution fusion | flops 812122112 | bytes 4456448 | tf_op jit(solution)/shard_map/dot_general | solution.py:123
  39.0 13.6 %all-to-all-start = ((bf16[32,24,2048]{2,1,0:T(8,128)(2,1)}), bf16[32,24,2048]{2,1,0:T(8,128)(2,1)}, u32[]{:S(2)}, u32[]{:S(2)}) async-start(bf16[32,24,2048]{2,1,0:T(8,128)(2,1)} %bitcast.24), calls=%async_computation | async-start | bytes 6291456 | tf_op jit(solution)/shard_map/all_to_all | solution.py:127
  52.7 1.9 collective-permute-start.11
  54.6 3.9 %collective-permute-start.7 = (bf16[192,2048]{1,0:T(8,128)(2,1)S(1)}, bf16[192,2048]{1,0:T(8,128)(2,1)S(1)}, u32[]{:S(2)}, u32[]{:S(2)}) collective-permute-start(bf16[192,2048]{1,0:T(8,128)(2,1)S(1)} %bitcast.27), channel_id=1, source_target_pairs={{32,17},{48,1},{17,32},{1,48},{0,16},{16,0},{33,49},{49,33},{34,19... | collective-permute-start | bytes 2359304 | tf_op jit(solution)/shard_map/ppermute | solution.py:98
  58.6 1.9 collective-permute-start.3
  60.5 13.8 %collective-permute-done.11.refs_8_ = bf16[192,2048]{1,0:T(8,128)(2,1)} collective-permute-done((bf16[192,2048]{1,0:T(8,128)(2,1)S(1)}, bf16[192,2048]{1,0:T(8,128)(2,1)}, u32[]{:S(2)}, u32[]{:S(2)}) %collective-permute-start.11) | collective-permute-done | bytes 786464 | tf_op jit(solution)/shard_map/ppermute | solution.py:98
  74.3 1.6 collective-permute-start.12
  75.9 25.3 %collective-permute-done.7.refs_4_ = bf16[192,2048]{1,0:T(8,128)(2,1)S(1)} collective-permute-done((bf16[192,2048]{1,0:T(8,128)(2,1)S(1)}, bf16[192,2048]{1,0:T(8,128)(2,1)S(1)}, u32[]{:S(2)}, u32[]{:S(2)}) %collective-permute-start.7) | collective-permute-done | bytes 786464 | tf_op jit(solution)/shard_map/ppermute | solution.py:98
  101.2 1.6 collective-permute-start.8
  102.8 2.0 collective-permute-start.13
  104.8 2.4 collective-permute-start.9
  107.2 15.0 %collective-permute-done.3.refs_0_ = bf16[192,2048]{1,0:T(8,128)(2,1)S(1)} collective-permute-done((bf16[192,2048]{1,0:T(8,128)(2,1)}, bf16[192,2048]{1,0:T(8,128)(2,1)S(1)}, u32[]{:S(2)}, u32[]{:S(2)}) %collective-permute-start.3) | collective-permute-done | bytes 786464 | tf_op jit(solution)/shard_map/ppermute | solution.py:98
  122.2 1.9 collective-permute-start.5
  124.1 0.7 collective-permute-start.4
  125.0 4.7 %collective-permute-start.14 = (bf16[192,2048]{1,0:T(8,128)(2,1)S(1)}, bf16[192,2048]{1,0:T(8,128)(2,1)S(1)}, u32[]{:S(2)}, u32[]{:S(2)}) collective-permute-start(bf16[192,2048]{1,0:T(8,128)(2,1)S(1)} %broadcast_select_fusion.refs_9_), channel_id=1, source_target_pairs={{0,1},{1,0},{2,3},{3,2},{4,5},{5,4},{6,7},{7,6},{8,9},{9,8},{10,11... | collective-permute-start | bytes 2359304 | tf_op jit(solution)/shard_map/ppermute | solution.py:44
  129.8 9.4 %collective-permute-start.10 = (bf16[192,2048]{1,0:T(8,128)(2,1)S(1)}, bf16[192,2048]{1,0:T(8,128)(2,1)S(1)}, u32[]{:S(2)}, u32[]{:S(2)}) collective-permute-start(bf16[192,2048]{1,0:T(8,128)(2,1)S(1)} %broadcast_select_fusion.1.refs_5_), channel_id=1, source_target_pairs={{0,1},{1,0},{2,3},{3,2},{4,5},{5,4},{6,7},{7,6},{8,9},{9,8},{10,11... | collective-permute-start | bytes 2359304 | tf_op jit(solution)/shard_map/ppermute | solution.py:44
  139.4 1.9 collective-permute-start.6
  141.4 0.9 copy-done
  142.2 0.9 copy-done.2
  143.1 0.9 copy-done.15
  144.0 0.9 copy-done.16
  144.9 0.9 copy-done.4
  145.8 1.1 copy-done.1
  146.9 1.1 copy-done.3
  148.1 1.1 copy-done.5
  149.2 14.7 %shard_map.64 = bf16[768,2048]{1,0:T(8,128)(2,1)} custom-call(bf16[768,2048]{1,0:T(8,128)(2,1)} %bitcast.4.rows_ref, bf16[192,2048]{1,0:T(8,128)(2,1)S(1)} %collective-permute-done.3.refs_0_, bf16[192,2048]{1,0:T(8,128)(2,1)S(1)} %broadcast_select_fusion.2.refs_1_, bf16[192,2048]{1,0:T(8,128)(2,1)S(1)} %copy-done.3, bf16[192,2048]{1,0:T(8,128)(2,1)S(1)} %copy-done.5, ...), custom_call_target="tpu_custom_call" | custom-call | flops 7247757312 | bytes 15728640 | tf_op jit(solution)/shard_map/pallas_call | solution.py:67
  163.9 9.8 %all-to-all-start.1 = ((bf16[32,24,2048]{2,1,0:T(8,128)(2,1)}), bf16[32,24,2048]{2,1,0:T(8,128)(2,1)S(1)}, u32[]{:S(2)}, u32[]{:S(2)}) async-start(bf16[32,24,2048]{2,1,0:T(8,128)(2,1)} %bitcast.25), calls=%async_computation.1 | async-start | bytes 6291456 | tf_op jit(solution)/shard_map/all_to_all | solution.py:131
  173.6 0.8 convert_add_fusion
  174.5 71.5 %all-to-all-done.1 = bf16[32,24,2048]{2,1,0:T(8,128)(2,1)S(1)} async-done(((bf16[32,24,2048]{2,1,0:T(8,128)(2,1)}), bf16[32,24,2048]{2,1,0:T(8,128)(2,1)S(1)}, u32[]{:S(2)}, u32[]{:S(2)}) %all-to-all-start.1) | async-done | bytes 3145760 | tf_op jit(solution)/shard_map/all_to_all | solution.py:131
  246.1 1.0 convolution_bitcast_fusion
  247.1 1.0 fusion.31
  248.1 1.9 collective-permute-start.15
  250.1 5.0 %collective-permute-start.17 = (bf16[64,2048]{1,0:T(8,128)(2,1)S(1)}, bf16[64,2048]{1,0:T(8,128)(2,1)S(1)}, u32[]{:S(2)}, u32[]{:S(2)}) collective-permute-start(bf16[64,2048]{1,0:T(8,128)(2,1)S(1)} %get-tuple-element.8), channel_id=1, source_target_pairs={{0,80},{16,64},{64,16},{80,0},{1,81},{17,65},{65,17},{81,1},{2,82}... | collective-permute-start | bytes 786440 | tf_op jit(solution)/shard_map/ppermute | solution.py:44
  255.1 4.4 %collective-permute-start.16 = (bf16[64,2048]{1,0:T(8,128)(2,1)S(1)}, bf16[64,2048]{1,0:T(8,128)(2,1)S(1)}, u32[]{:S(2)}, u32[]{:S(2)}) collective-permute-start(bf16[64,2048]{1,0:T(8,128)(2,1)S(1)} %get-tuple-element.9), channel_id=1, source_target_pairs={{0,112},{16,96},{32,80},{48,64},{64,48},{80,32},{96,16},{112,0},{1... | collective-permute-start | bytes 786440 | tf_op jit(solution)/shard_map/ppermute | solution.py:44
  259.5 10.1 %collective-permute-done.15 = bf16[64,2048]{1,0:T(8,128)(2,1)S(1)} collective-permute-done((bf16[64,2048]{1,0:T(8,128)(2,1)S(1)}, bf16[64,2048]{1,0:T(8,128)(2,1)S(1)}, u32[]{:S(2)}, u32[]{:S(2)}) %collective-permute-start.15) | collective-permute-done | bytes 262176 | tf_op jit(solution)/shard_map/ppermute | solution.py:44
  269.6 5.5 %collective-permute-done.17 = bf16[64,2048]{1,0:T(8,128)(2,1)S(1)} collective-permute-done((bf16[64,2048]{1,0:T(8,128)(2,1)S(1)}, bf16[64,2048]{1,0:T(8,128)(2,1)S(1)}, u32[]{:S(2)}, u32[]{:S(2)}) %collective-permute-start.17) | collective-permute-done | bytes 262176 | tf_op jit(solution)/shard_map/ppermute | solution.py:44
  275.0 4.5 %collective-permute-done.16 = bf16[64,2048]{1,0:T(8,128)(2,1)S(1)} collective-permute-done((bf16[64,2048]{1,0:T(8,128)(2,1)S(1)}, bf16[64,2048]{1,0:T(8,128)(2,1)S(1)}, u32[]{:S(2)}, u32[]{:S(2)}) %collective-permute-start.16) | collective-permute-done | bytes 262176 | tf_op jit(solution)/shard_map/ppermute | solution.py:44
  279.5 0.8 fusion.7
  (54 shorter events, 2.1 us)
Async XLA Ops:
  2.7 33.4 %copy-start.6 = (bf16[64,2048]{0,1:T(8,128)(2,1)}, bf16[64,2048]{0,1:T(8,128)(2,1)S(1)}, u32[]{:S(2)}) copy-start(bf16[64,2048]{0,1:T(8,128)(2,1)S(1)} %copy.18) | copy-start | bytes 786436
  3.1 25.6 %collective-permute-start.2 = (bf16[64,2176]{1,0:T(8,128)(2,1)S(1)}, bf16[64,2176]{1,0:T(8,128)(2,1)S(1)}, u32[]{:S(2)}, u32[]{:S(2)}) collective-permute-start(bf16[64,2176]{1,0:T(8,128)(2,1)S(1)} %copy.19), channel_id=1, source_target_pairs={{0,80},{16,64},{64,16},{80,0},{1,81},{17,65},{65,17},{81,1},{2,82}... | collective-permute-start | bytes 835592 | tf_op jit(solution)/shard_map/ppermute | solution.py:44
  10.0 24.6 %collective-permute-start.1 = (bf16[64,2176]{1,0:T(8,128)(2,1)S(1)}, bf16[64,2176]{1,0:T(8,128)(2,1)S(1)}, u32[]{:S(2)}, u32[]{:S(2)}) collective-permute-start(bf16[64,2176]{1,0:T(8,128)(2,1)S(1)} %copy.19), channel_id=1, source_target_pairs={{0,112},{16,96},{32,80},{48,64},{64,48},{80,32},{96,16},{112,0},{1... | collective-permute-start | bytes 835592 | tf_op jit(solution)/shard_map/ppermute | solution.py:44
  12.2 23.0 %collective-permute-start = (bf16[64,2176]{1,0:T(8,128)(2,1)S(1)}, bf16[64,2176]{1,0:T(8,128)(2,1)S(1)}, u32[]{:S(2)}, u32[]{:S(2)}) collective-permute-start(bf16[64,2176]{1,0:T(8,128)(2,1)S(1)} %copy.19), channel_id=1, source_target_pairs={{0,32},{32,0},{1,33},{33,1},{2,34},{34,2},{3,35},{35,3},{4,36},{36... | collective-permute-start | bytes 835592 | tf_op jit(solution)/shard_map/ppermute | solution.py:44
  29.0 7.1 %copy-start.7 = (bf16[64,2176]{0,1:T(8,128)(2,1)}, bf16[64,2176]{0,1:T(8,128)(2,1)S(1)}, u32[]{:S(2)}) copy-start(bf16[64,2176]{0,1:T(8,128)(2,1)S(1)} %copy.24) | copy-start | bytes 835588
  34.9 4.1 %copy-start.8 = (bf16[64,2176]{0,1:T(8,128)(2,1)}, bf16[64,2176]{0,1:T(8,128)(2,1)S(1)}, u32[]{:S(2)}) copy-start(bf16[64,2176]{0,1:T(8,128)(2,1)S(1)} %copy.23) | copy-start | bytes 835588
  35.5 3.6 %copy-start.9 = (bf16[64,2176]{0,1:T(8,128)(2,1)}, bf16[64,2176]{0,1:T(8,128)(2,1)S(1)}, u32[]{:S(2)}) copy-start(bf16[64,2176]{0,1:T(8,128)(2,1)S(1)} %copy.22) | copy-start | bytes 835588
  39.0 13.7 %copy-start.10 = (bf16[1,1,192,2048]{3,2,1,0:T(8,128)(2,1)S(1)}, bf16[1,1,192,2048]{3,2,1,0:T(8,128)(2,1)}, u32[]{:S(2)}) copy-start(bf16[1,1,192,2048]{3,2,1,0:T(8,128)(2,1)} %param.11) | copy-start | bytes 2359300
  39.0 15.6 %copy-start.11 = (bf16[1,1,192,2048]{3,2,1,0:T(8,128)(2,1)S(1)}, bf16[1,1,192,2048]{3,2,1,0:T(8,128)(2,1)}, u32[]{:S(2)}) copy-start(bf16[1,1,192,2048]{3,2,1,0:T(8,128)(2,1)} %param.10) | copy-start | bytes 2359300
  39.0 106.8 %all-to-all-start = ((bf16[32,24,2048]{2,1,0:T(8,128)(2,1)}), bf16[32,24,2048]{2,1,0:T(8,128)(2,1)}, u32[]{:S(2)}, u32[]{:S(2)}) async-start(bf16[32,24,2048]{2,1,0:T(8,128)(2,1)} %bitcast.24), calls=%async_computation | async-start | bytes 6291456 | tf_op jit(solution)/shard_map/all_to_all | solution.py:127
  52.7 21.6 %collective-permute-start.11 = (bf16[192,2048]{1,0:T(8,128)(2,1)S(1)}, bf16[192,2048]{1,0:T(8,128)(2,1)}, u32[]{:S(2)}, u32[]{:S(2)}) collective-permute-start(bf16[192,2048]{1,0:T(8,128)(2,1)S(1)} %bitcast.26), channel_id=1, source_target_pairs={{32,17},{48,1},{17,32},{1,48},{0,16},{16,0},{33,49},{49,33},{34,19... | collective-permute-start | bytes 2359304 | tf_op jit(solution)/shard_map/ppermute | solution.py:98
  54.6 46.6 %collective-permute-start.7 = (bf16[192,2048]{1,0:T(8,128)(2,1)S(1)}, bf16[192,2048]{1,0:T(8,128)(2,1)S(1)}, u32[]{:S(2)}, u32[]{:S(2)}) collective-permute-start(bf16[192,2048]{1,0:T(8,128)(2,1)S(1)} %bitcast.27), channel_id=1, source_target_pairs={{32,17},{48,1},{17,32},{1,48},{0,16},{16,0},{33,49},{49,33},{34,19... | collective-permute-start | bytes 2359304 | tf_op jit(solution)/shard_map/ppermute | solution.py:98
  58.6 63.7 %collective-permute-start.3 = (bf16[192,2048]{1,0:T(8,128)(2,1)}, bf16[192,2048]{1,0:T(8,128)(2,1)S(1)}, u32[]{:S(2)}, u32[]{:S(2)}) collective-permute-start(bf16[192,2048]{1,0:T(8,128)(2,1)} %bitcast.28), channel_id=1, source_target_pairs={{32,17},{48,1},{17,32},{1,48},{0,16},{16,0},{33,49},{49,33},{34,19... | collective-permute-start | bytes 2359304 | tf_op jit(solution)/shard_map/ppermute | solution.py:98
  74.3 49.9 %collective-permute-start.12 = (bf16[192,2048]{1,0:T(8,128)(2,1)}, bf16[192,2048]{1,0:T(8,128)(2,1)}, u32[]{:S(2)}, u32[]{:S(2)}) collective-permute-start(bf16[192,2048]{1,0:T(8,128)(2,1)} %collective-permute-done.11.refs_8_), channel_id=1, source_target_pairs={{1,17},{17,1},{32,48},{48,32},{3,19},{19,3},{34,50},{50,34},{5,21}... | collective-permute-start | bytes 2359304 | tf_op jit(solution)/shard_map/ppermute | solution.py:99
  101.2 23.8 %collective-permute-start.8 = (bf16[192,2048]{1,0:T(8,128)(2,1)S(1)}, bf16[192,2048]{1,0:T(8,128)(2,1)}, u32[]{:S(2)}, u32[]{:S(2)}) collective-permute-start(bf16[192,2048]{1,0:T(8,128)(2,1)S(1)} %collective-permute-done.7.refs_4_), channel_id=1, source_target_pairs={{1,17},{17,1},{32,48},{48,32},{3,19},{19,3},{34,50},{50,34},{5,21}... | collective-permute-start | bytes 2359304 | tf_op jit(solution)/shard_map/ppermute | solution.py:99
  102.8 36.5 %copy-start.12 = (bf16[1,1,192,2048]{3,2,1,0:T(8,128)(2,1)S(1)}, bf16[1,1,192,2048]{3,2,1,0:T(8,128)(2,1)}, u32[]{:S(2)}) copy-start(bf16[1,1,192,2048]{3,2,1,0:T(8,128)(2,1)} %param.9) | copy-start | bytes 2359300
  102.8 36.6 %collective-permute-start.13 = (bf16[192,2048]{1,0:T(8,128)(2,1)}, bf16[192,2048]{1,0:T(8,128)(2,1)S(1)}, u32[]{:S(2)}, u32[]{:S(2)}) collective-permute-start(bf16[192,2048]{1,0:T(8,128)(2,1)} %collective-permute-done.11.refs_8_), channel_id=1, source_target_pairs={{0,1},{1,0},{2,3},{3,2},{4,5},{5,4},{6,7},{7,6},{8,9},{9,8},{10,11... | collective-permute-start | bytes 2359304 | tf_op jit(solution)/shard_map/ppermute | solution.py:44
  104.8 36.5 %collective-permute-start.9 = (bf16[192,2048]{1,0:T(8,128)(2,1)S(1)}, bf16[192,2048]{1,0:T(8,128)(2,1)S(1)}, u32[]{:S(2)}, u32[]{:S(2)}) collective-permute-start(bf16[192,2048]{1,0:T(8,128)(2,1)S(1)} %collective-permute-done.7.refs_4_), channel_id=1, source_target_pairs={{0,1},{1,0},{2,3},{3,2},{4,5},{5,4},{6,7},{7,6},{8,9},{9,8},{10,11... | collective-permute-start | bytes 2359304 | tf_op jit(solution)/shard_map/ppermute | solution.py:44
  122.2 20.0 %collective-permute-start.5 = (bf16[192,2048]{1,0:T(8,128)(2,1)S(1)}, bf16[192,2048]{1,0:T(8,128)(2,1)S(1)}, u32[]{:S(2)}, u32[]{:S(2)}) collective-permute-start(bf16[192,2048]{1,0:T(8,128)(2,1)S(1)} %collective-permute-done.3.refs_0_), channel_id=1, source_target_pairs={{0,1},{1,0},{2,3},{3,2},{4,5},{5,4},{6,7},{7,6},{8,9},{9,8},{10,11... | collective-permute-start | bytes 2359304 | tf_op jit(solution)/shard_map/ppermute | solution.py:44
  124.1 5.7 %collective-permute-start.4 = (bf16[192,2048]{1,0:T(8,128)(2,1)S(1)}, bf16[192,2048]{1,0:T(8,128)(2,1)S(1)}, u32[]{:S(2)}, u32[]{:S(2)}) collective-permute-start(bf16[192,2048]{1,0:T(8,128)(2,1)S(1)} %collective-permute-done.3.refs_0_), channel_id=1, source_target_pairs={{1,17},{17,1},{32,48},{48,32},{3,19},{19,3},{34,50},{50,34},{5,21}... | collective-permute-start | bytes 2359304 | tf_op jit(solution)/shard_map/ppermute | solution.py:99
  125.0 14.4 %copy-start.13 = (bf16[192,2048]{1,0:T(8,128)(2,1)}, bf16[192,2048]{1,0:T(8,128)(2,1)S(1)}, u32[]{:S(2)}) copy-start(bf16[192,2048]{1,0:T(8,128)(2,1)S(1)} %broadcast_select_fusion.refs_9_) | copy-start | bytes 2359300
  125.0 18.1 %collective-permute-start.14 = (bf16[192,2048]{1,0:T(8,128)(2,1)S(1)}, bf16[192,2048]{1,0:T(8,128)(2,1)S(1)}, u32[]{:S(2)}, u32[]{:S(2)}) collective-permute-start(bf16[192,2048]{1,0:T(8,128)(2,1)S(1)} %broadcast_select_fusion.refs_9_), channel_id=1, source_target_pairs={{0,1},{1,0},{2,3},{3,2},{4,5},{5,4},{6,7},{7,6},{8,9},{9,8},{10,11... | collective-permute-start | bytes 2359304 | tf_op jit(solution)/shard_map/ppermute | solution.py:44
  129.8 13.3 %collective-permute-start.10 = (bf16[192,2048]{1,0:T(8,128)(2,1)S(1)}, bf16[192,2048]{1,0:T(8,128)(2,1)S(1)}, u32[]{:S(2)}, u32[]{:S(2)}) collective-permute-start(bf16[192,2048]{1,0:T(8,128)(2,1)S(1)} %broadcast_select_fusion.1.refs_5_), channel_id=1, source_target_pairs={{0,1},{1,0},{2,3},{3,2},{4,5},{5,4},{6,7},{7,6},{8,9},{9,8},{10,11... | collective-permute-start | bytes 2359304 | tf_op jit(solution)/shard_map/ppermute | solution.py:44
  139.4 3.7 %copy-start.14 = (bf16[192,2048]{1,0:T(8,128)(2,1)}, bf16[192,2048]{1,0:T(8,128)(2,1)S(1)}, u32[]{:S(2)}) copy-start(bf16[192,2048]{1,0:T(8,128)(2,1)S(1)} %collective-permute-done.13.refs_10_) | copy-start | bytes 2359300
  139.4 5.5 %collective-permute-start.6 = (bf16[192,2048]{1,0:T(8,128)(2,1)S(1)}, bf16[192,2048]{1,0:T(8,128)(2,1)S(1)}, u32[]{:S(2)}, u32[]{:S(2)}) collective-permute-start(bf16[192,2048]{1,0:T(8,128)(2,1)S(1)} %broadcast_select_fusion.2.refs_1_), channel_id=1, source_target_pairs={{0,1},{1,0},{2,3},{3,2},{4,5},{5,4},{6,7},{7,6},{8,9},{9,8},{10,11... | collective-permute-start | bytes 2359304 | tf_op jit(solution)/shard_map/ppermute | solution.py:44
  141.3 0.9 copy-start
  142.2 0.9 copy-start.2
  143.1 0.9 copy-start.15
  144.0 0.9 copy-start.16
  144.9 0.9 copy-start.4
  145.8 1.1 copy-start.1
  146.9 1.1 copy-start.3
  148.1 1.1 copy-start.5
  163.9 82.2 %all-to-all-start.1 = ((bf16[32,24,2048]{2,1,0:T(8,128)(2,1)}), bf16[32,24,2048]{2,1,0:T(8,128)(2,1)S(1)}, u32[]{:S(2)}, u32[]{:S(2)}) async-start(bf16[32,24,2048]{2,1,0:T(8,128)(2,1)} %bitcast.25), calls=%async_computation.1 | async-start | bytes 6291456 | tf_op jit(solution)/shard_map/all_to_all | solution.py:131
  248.1 21.4 %collective-permute-start.15 = (bf16[64,2048]{1,0:T(8,128)(2,1)S(1)}, bf16[64,2048]{1,0:T(8,128)(2,1)S(1)}, u32[]{:S(2)}, u32[]{:S(2)}) collective-permute-start(bf16[64,2048]{1,0:T(8,128)(2,1)S(1)} %get-tuple-element.7), channel_id=1, source_target_pairs={{0,32},{32,0},{1,33},{33,1},{2,34},{34,2},{3,35},{35,3},{4,36},{36... | collective-permute-start | bytes 786440 | tf_op jit(solution)/shard_map/ppermute | solution.py:44
  250.1 25.0 %collective-permute-start.17 = (bf16[64,2048]{1,0:T(8,128)(2,1)S(1)}, bf16[64,2048]{1,0:T(8,128)(2,1)S(1)}, u32[]{:S(2)}, u32[]{:S(2)}) collective-permute-start(bf16[64,2048]{1,0:T(8,128)(2,1)S(1)} %get-tuple-element.8), channel_id=1, source_target_pairs={{0,80},{16,64},{64,16},{80,0},{1,81},{17,65},{65,17},{81,1},{2,82}... | collective-permute-start | bytes 786440 | tf_op jit(solution)/shard_map/ppermute | solution.py:44
  255.1 24.5 %collective-permute-start.16 = (bf16[64,2048]{1,0:T(8,128)(2,1)S(1)}, bf16[64,2048]{1,0:T(8,128)(2,1)S(1)}, u32[]{:S(2)}, u32[]{:S(2)}) collective-permute-start(bf16[64,2048]{1,0:T(8,128)(2,1)S(1)} %get-tuple-element.9), channel_id=1, source_target_pairs={{0,112},{16,96},{32,80},{48,64},{64,48},{80,32},{96,16},{112,0},{1... | collective-permute-start | bytes 786440 | tf_op jit(solution)/shard_map/ppermute | solution.py:44

commit v2 on v1

v2 whole, which is shorter than its diff:
```python
import jax
import jax.numpy as jnp
from jax import lax
from jax.experimental import pallas as pl
from jax.experimental.pallas import tpu as pltpu
from jax.sharding import Mesh, PartitionSpec as P

SIZES = (4, 2, 2, 2, 8, 2)
NAMES = ("x", "h", "p", "b", "z", "c")
MOST = 6
CHUNKS = 4
PLANE = 32
EXTRA = 128
LANES = 128


def flips(axes):
    return [(i, i ^ (2 ** len(axes) - 1)) for i in range(2 ** len(axes))]


def place(p, b, c):
    return p * 4 + b * 2 + c


FIRST = [
    (place(1, 0, 0), place(0, 1, 1)),
    (place(1, 1, 0), place(0, 0, 1)),
    (place(0, 1, 1), place(1, 0, 0)),
    (place(0, 0, 1), place(1, 1, 0)),
    (place(0, 0, 0), place(0, 1, 0)),
    (place(0, 1, 0), place(0, 0, 0)),
    (place(1, 0, 1), place(1, 1, 1)),
    (place(1, 1, 1), place(1, 0, 1)),
]
SECOND = [
    (place(0, 0, 1), place(0, 1, 1)),
    (place(0, 1, 1), place(0, 0, 1)),
    (place(1, 0, 0), place(1, 1, 0)),
    (place(1, 1, 0), place(1, 0, 0)),
]
PARTNERS = (("p",), ("h", "p", "b"), ("h", "b"))


def swap(value, axes):
    return lax.ppermute(value, axes, flips(axes))


def expert_kernel(group_ref, rows_ref, *refs):
    pieces, out_ref = refs[:12], refs[12]
    gate, up, down, lined, sems = refs[13:]
    first = pl.program_id(0) == 0
    hid = pieces[0].shape[0]
    copies = [
        pltpu.make_async_copy(piece, into.at[pl.ds(k % 4 * hid, hid)], sems.at[k])
        for k, (piece, into) in enumerate(zip(pieces, [gate] * 4 + [up] * 4 + [down] * 4))
    ]

    @pl.when(first)
    def _():
        for copy in copies:
            copy.start()
        for copy in copies[:8]:
            copy.wait()

    dims = (((1,), (1,)), ((), ()))
    rows = rows_ref[...]
    g = lax.dot_general(rows, gate[...], dims, preferred_element_type=jnp.float32)
    u = lax.dot_general(rows, up[...], dims, preferred_element_type=jnp.float32)
    hidden = (g / (1.0 + jnp.exp(-g)) * u).astype(jnp.bfloat16)

    @pl.when(first)
    def _():
        for copy in copies[8:]:
            copy.wait()

    result = jnp.dot(hidden, down[...], preferred_element_type=jnp.float32)
    count = rows.shape[0]
    lines = result.shape[1] // LANES
    for k in range(lines):
        lined[pl.ds(k, count, stride=lines), :] = result[:, k * LANES : (k + 1) * LANES]
    block = MOST * lines
    for k in range(count // MOST):
        z, m = divmod(k, CHUNKS)
        out_ref[0, m ^ group_ref[0], z] = lined[k * block : (k + 1) * block, :].astype(jnp.bfloat16)


def run_expert(group, rows, pieces):
    count, width = rows.shape
    hid = pieces[0].shape[0]
    xs, zs = SIZES[0], SIZES[4]
    tile = count // xs
    lines = width // LANES
    shape = (CHUNKS, zs, MOST * lines, LANES)
    return pl.pallas_call(
        expert_kernel,
        grid=(xs,),
        out_shape=jax.ShapeDtypeStruct((xs,) + shape, jnp.bfloat16),
        in_specs=[
            pl.BlockSpec(memory_space=pltpu.SMEM),
            pl.BlockSpec((tile, width), lambda i: (i, 0)),
        ]
        + [pl.BlockSpec(memory_space=pl.ANY)] * 12,
        out_specs=pl.BlockSpec((1,) + shape, lambda i: (i, 0, 0, 0, 0)),
        scratch_shapes=[pltpu.VMEM((4 * hid, width), jnp.bfloat16)] * 3
        + [pltpu.VMEM((tile * lines, LANES), jnp.float32), pltpu.SemaphoreType.DMA((12,))],
        compiler_params=pltpu.CompilerParams(vmem_limit_bytes=28 * 1024 * 1024),
        cost_estimate=pl.CostEstimate(
            flops=2 * count * width * hid * 12,
            bytes_accessed=4 * count * width + 24 * hid * width,
            transcendentals=count * hid * 4,
        ),
    )(group, rows, *pieces)


def member_groups():
    def index(x, member, z, kind, c):
        h = member >> 1
        at = x
        for n, coordinate in zip(SIZES[1:], (h, (member & 1) ^ h, kind ^ h, z, c)):
            at = at * n + coordinate
        return at

    return [
        [
            index(x, member, z, kind, c)
            for x in range(SIZES[0])
            for member in range(CHUNKS)
            for z in range(SIZES[4])
        ]
        for kind in range(2)
        for c in range(2)
    ]


def matches(named, experts):
    return named[:, :, None] == experts[None, None, :]


def ranks(chosen, count):
    order = jnp.arange(chosen.shape[0], dtype=jnp.int32)
    before = (order[:, None] // count == order[None, :] // count) & (order[None, :] < order[:, None])
    return jnp.dot(
        before.astype(jnp.bfloat16), chosen.astype(jnp.bfloat16), preferred_element_type=jnp.float32
    ).astype(jnp.int32)


def shards(tokens, routes, route_weights, gate_weight, up_weight, down_weight):
    count, width = tokens.shape
    top = routes.shape[1]
    h, p, c = (lax.axis_index(n) for n in ("h", "p", "c"))
    xs, zs = SIZES[0], SIZES[4]

    meta = jnp.pad(routes.astype(jnp.bfloat16), ((0, 0), (0, EXTRA - top)))
    record = jnp.concatenate([tokens, meta], axis=1)
    records = jnp.concatenate([record] + [swap(record, axes) for axes in PARTNERS], axis=0)

    own = [gate_weight[0, 0], up_weight[0, 0], down_weight[0, 0]]
    axes = ("p", "b", "c")
    first = [lax.ppermute(w, axes, FIRST) for w in own]

    named = records[:, width : width + top].astype(jnp.int32)
    target = jnp.arange(PLANE, dtype=jnp.int32)
    chosen = jnp.any(matches(named, (2 * (target % zs) + p) * 8 + 2 * (target // zs) + h), axis=1)
    chunk = jnp.arange(CHUNKS * count, dtype=jnp.int32) // count
    slot = jnp.where(chosen, ranks(chosen, count) + (chunk * MOST)[:, None], -1).T
    slots = jnp.arange(CHUNKS * MOST, dtype=jnp.int32)
    hit = (slot[:, None, :] == slots[None, :, None]).reshape(PLANE * CHUNKS * MOST, CHUNKS * count)
    sent = jnp.dot(
        hit.astype(jnp.bfloat16), records[:, :width], preferred_element_type=jnp.float32
    ).astype(jnp.bfloat16)
    sent, first[0] = lax.optimization_barrier((sent, first[0]))
    arrived = lax.all_to_all(
        sent.reshape(PLANE, CHUNKS * MOST, width), ("x", "z"), 0, 0, tiled=True
    )

    second = [lax.ppermute(w, axes, SECOND) for w in first]
    second = [jnp.where(c == p, mine, got) for mine, got in zip(own, second)]
    third = [swap(w, ("c",)) for w in first]
    fourth = [swap(w, ("c",)) for w in second]
    pieces = [piece for four in zip(first, second, third, fourth) for piece in four]

    group = (2 * h + (p ^ h)).astype(jnp.int32).reshape(1)
    results = run_expert(group, arrived.reshape(-1, width), pieces)

    returned = lax.all_to_all(
        results.reshape((xs * CHUNKS * zs,) + results.shape[3:]),
        NAMES,
        0,
        0,
        axis_index_groups=member_groups(),
        tiled=True,
    )
    returned = returned.reshape(-1, width)

    target = jnp.arange(xs * CHUNKS * zs, dtype=jnp.int32)
    half = target // zs % CHUNKS // 2
    column = 2 * (target % zs) + (target // zs % 2 ^ half)
    match = matches(routes, column * 8 + 2 * (target // (zs * CHUNKS)) + half)
    chosen = jnp.any(match, axis=1)
    weight = jnp.sum(jnp.where(match, route_weights[:, :, None], 0.0), axis=1)
    slot = jnp.where(chosen, ranks(chosen, count), -1).T
    slots = jnp.arange(MOST, dtype=jnp.int32)
    spread = jnp.where(slot[:, None, :] == slots[None, :, None], weight.T[:, None, :], 0.0)
    spread = spread.reshape(-1, count)
    upper = spread.astype(jnp.bfloat16)
    lower = (spread - upper.astype(jnp.float32)).astype(jnp.bfloat16)
    dims = (((0,), (0,)), ((), ()))
    mixed = lax.dot_general(
        upper, returned, dims, preferred_element_type=jnp.float32
    ) + lax.dot_general(lower, returned, dims, preferred_element_type=jnp.float32)
    return mixed.astype(jnp.bfloat16)


def solution(mesh):
    fine = Mesh(mesh.devices.reshape(SIZES), NAMES)
    rows = P(NAMES, None)
    weights = P(("x", "h", "p", "b"), ("z", "c"), None, None)
    return jax.shard_map(
        shards,
        mesh=fine,
        in_specs=(rows, rows, rows, weights, weights, weights),
        out_specs=rows,
        check_vma=False,
    )
```

time: 281 us -> 275 us (0.979)
  the two profiles are of different devices: /device:TPU:4 before, /device:TPU:111 now
where the time goes in v2:
time: 275 us; the launch traced here: 274 us
  waiting for transfers between devices  159 us (58%)
  starting transfers between devices  73.1 us (27%)
  Pallas kernels  15.8 us (6%)
  local copies, waits for them, and re-layouts  13 us (5%)
  other arithmetic  7.5 us (3%)
  matrix products  5.36 us (2%)
    all_to_all x1, waiting for transfers between devices, shards(): lax.all_to_all(results.reshape((xs * CHUNKS * zs,) + results.shape[3:]),...  99.2 us
    ppermute x3, waiting for transfers between devices, shards(): first = [lax.ppermute(w, axes, FIRST) for w in own]  36.1 us
    ppermute x9, starting transfers between devices, swap(): return lax.ppermute(value, axes, flips(axes))  29.5 us
    ppermute x9, waiting for transfers between devices, swap(): return lax.ppermute(value, axes, flips(axes))  19.4 us
    pallas_call x1, Pallas kernels, run_expert(): pl.pallas_call(expert_kernel, grid=(xs,), out_shape=jax.ShapeDtypeStruct(...  15.8 us
    all_to_all x1, starting transfers between devices, shards(): lax.all_to_all(results.reshape((xs * CHUNKS * zs,) + results.shape[3:]),...  15.5 us
    all_to_all x1, starting transfers between devices, shards(): lax.all_to_all(sent.reshape(PLANE, CHUNKS * MOST, width), ('x', 'z'), 0,...  12 us
    ppermute x3, starting transfers between devices, shards(): first = [lax.ppermute(w, axes, FIRST) for w in own]  9.28 us
  transfers between devices with their start and end apart: 17, of which 9 were waited for; matrix products, arithmetic and copies ran while one was open for 4% of the time, Pallas kernels for 0%

profile of v2, /device:TPU:111, one launch (start us, length us, event | category | flops | bytes accessed | tf_op | source)
XLA Modules:
  0.0 274.2 jit_solution(5898045591943304086)
XLA Ops:
  0.0 1.2 copy.30
  1.2 0.7 convert_element_type.71
  2.1 0.2 copy.31
  2.3 2.4 collective-permute-start
  4.7 2.3 collective-permute-start.1
  7.0 5.8 %collective-permute-start.2 = (bf16[64,2176]{1,0:T(8,128)(2,1)S(1)}, bf16[64,2176]{1,0:T(8,128)(2,1)S(1)}, u32[]{:S(2)}, u32[]{:S(2)}) collective-permute-start(bf16[64,2176]{1,0:T(8,128)(2,1)S(1)} %copy.31), channel_id=1, source_target_pairs={{0,80},{16,64},{64,16},{80,0},{1,81},{17,65},{65,17},{81,1},{2,82}... | collective-permute-start | bytes 835592 | tf_op jit(solution)/shard_map/ppermute | solution.py:45
  12.8 3.7 %collective-permute-start.3 = (bf16[192,2048]{1,0:T(8,128)(2,1)}, bf16[192,2048]{1,0:T(8,128)(2,1)S(1)}, u32[]{:S(2)}, u32[]{:S(2)}) collective-permute-start(bf16[192,2048]{1,0:T(8,128)(2,1)} %bitcast.27), channel_id=1, source_target_pairs={{32,17},{48,1},{17,32},{1,48},{0,16},{16,0},{33,49},{49,33},{34,19... | collective-permute-start | bytes 2359304 | tf_op jit(solution)/shard_map/ppermute | solution.py:159
  16.7 0.3 copy.34
  17.0 12.3 %collective-permute-done.1 = bf16[64,2176]{1,0:T(8,128)(2,1)S(1)} collective-permute-done((bf16[64,2176]{1,0:T(8,128)(2,1)S(1)}, bf16[64,2176]{1,0:T(8,128)(2,1)S(1)}, u32[]{:S(2)}, u32[]{:S(2)}) %collective-permute-start.1) | collective-permute-done | bytes 278560 | tf_op jit(solution)/shard_map/ppermute | solution.py:45
  29.3 0.3 copy.35
  29.6 4.9 %collective-permute-done.2 = bf16[64,2176]{1,0:T(8,128)(2,1)S(1)} collective-permute-done((bf16[64,2176]{1,0:T(8,128)(2,1)S(1)}, bf16[64,2176]{1,0:T(8,128)(2,1)S(1)}, u32[]{:S(2)}, u32[]{:S(2)}) %collective-permute-start.2) | collective-permute-done | bytes 278560 | tf_op jit(solution)/shard_map/ppermute | solution.py:45
  34.5 0.3 copy.36
  35.0 0.2 fusion.2
  35.5 2.8 %convolution_convert_fusion = bf16[768,2048]{1,0:T(8,128)(2,1)} fusion(pred[768,256]{1,0:T(32,128)(4,1)S(1)} %bitcast_compare_fusion, bf16[64,2176]{0,1:T(8,128)(2,1)S(1)} %copy.36, bf16[64,2176]{0,1:T(8,128)(2,1)S(1)} %copy.35, bf16[64,2176]{0,1:T(8,128)(2,1)S(1)} %copy.34, bf16[64,128]{0,1:T(8,128)(2,1)S(1)} %pad.4, bf16[64,2048]{0,1:T(8,128)(2,1)S(1)} %copy.30), kind=kOutput, calls=%fused_computation | convolution fusion | flops 812122112 | bytes 4456448 | tf_op jit(solution)/shard_map/dot_general | solution.py:168
  38.3 9.9 %collective-permute-done.3.refs_0_ = bf16[192,2048]{1,0:T(8,128)(2,1)S(1)} collective-permute-done((bf16[192,2048]{1,0:T(8,128)(2,1)}, bf16[192,2048]{1,0:T(8,128)(2,1)S(1)}, u32[]{:S(2)}, u32[]{:S(2)}) %collective-permute-start.3) | collective-permute-done | bytes 786464 | tf_op jit(solution)/shard_map/ppermute | solution.py:159
  48.2 0.9 copy-done.1
  49.1 12.0 %all-to-all-start = ((bf16[32,24,2048]{2,1,0:T(8,128)(2,1)}), bf16[32,24,2048]{2,1,0:T(8,128)(2,1)S(1)}, u32[]{:S(2)}, u32[]{:S(2)}) async-start(bf16[32,24,2048]{2,1,0:T(8,128)(2,1)} %bitcast.26), calls=%async_computation | async-start | bytes 6291456 | tf_op jit(solution)/shard_map/all_to_all | solution.py:172
  61.1 2.8 %collective-permute-start.7 = (bf16[192,2048]{1,0:T(8,128)(2,1)}, bf16[192,2048]{1,0:T(8,128)(2,1)}, u32[]{:S(2)}, u32[]{:S(2)}) collective-permute-start(bf16[192,2048]{1,0:T(8,128)(2,1)} %bitcast.28), channel_id=1, source_target_pairs={{32,17},{48,1},{17,32},{1,48},{0,16},{16,0},{33,49},{49,33},{34,19... | collective-permute-start | bytes 2359304 | tf_op jit(solution)/shard_map/ppermute | solution.py:159
  63.9 2.7 %collective-permute-start.11 = (bf16[192,2048]{1,0:T(8,128)(2,1)}, bf16[192,2048]{1,0:T(8,128)(2,1)}, u32[]{:S(2)}, u32[]{:S(2)}) collective-permute-start(bf16[192,2048]{1,0:T(8,128)(2,1)} %bitcast.29), channel_id=1, source_target_pairs={{32,17},{48,1},{17,32},{1,48},{0,16},{16,0},{33,49},{49,33},{34,19... | collective-permute-start | bytes 2359304 | tf_op jit(solution)/shard_map/ppermute | solution.py:159
  66.7 2.5 collective-permute-start.4
  69.2 14.2 %collective-permute-done.7.refs_4_ = bf16[192,2048]{1,0:T(8,128)(2,1)} collective-permute-done((bf16[192,2048]{1,0:T(8,128)(2,1)}, bf16[192,2048]{1,0:T(8,128)(2,1)}, u32[]{:S(2)}, u32[]{:S(2)}) %collective-permute-start.7) | collective-permute-done | bytes 786464 | tf_op jit(solution)/shard_map/ppermute | solution.py:159
  83.4 2.5 collective-permute-start.8
  85.9 2.1 collective-permute-start.5
  88.0 11.9 %collective-permute-done.11.refs_8_ = bf16[192,2048]{1,0:T(8,128)(2,1)} collective-permute-done((bf16[192,2048]{1,0:T(8,128)(2,1)}, bf16[192,2048]{1,0:T(8,128)(2,1)}, u32[]{:S(2)}, u32[]{:S(2)}) %collective-permute-start.11) | collective-permute-done | bytes 786464 | tf_op jit(solution)/shard_map/ppermute | solution.py:159
  99.9 1.9 collective-permute-start.12
  101.8 8.8 %collective-permute-start.13 = (bf16[192,2048]{1,0:T(8,128)(2,1)}, bf16[192,2048]{1,0:T(8,128)(2,1)}, u32[]{:S(2)}, u32[]{:S(2)}) collective-permute-start(bf16[192,2048]{1,0:T(8,128)(2,1)} %collective-permute-done.11.refs_8_), channel_id=1, source_target_pairs={{0,1},{1,0},{2,3},{3,2},{4,5},{5,4},{6,7},{7,6},{8,9},{9,8},{10,11... | collective-permute-start | bytes 2359304 | tf_op jit(solution)/shard_map/ppermute | solution.py:45
  110.6 1.9 collective-permute-start.9
  112.6 2.4 broadcast_select_fusion.2.refs_1_
  114.9 0.3 collective-permute-done.8
  115.3 1.9 collective-permute-start.6
  117.2 2.4 broadcast_select_fusion.1.refs_5_
  119.6 4.1 %collective-permute-done.12 = bf16[192,2048]{1,0:T(8,128)(2,1)S(1)} collective-permute-done((bf16[192,2048]{1,0:T(8,128)(2,1)}, bf16[192,2048]{1,0:T(8,128)(2,1)S(1)}, u32[]{:S(2)}, u32[]{:S(2)}) %collective-permute-start.12) | collective-permute-done | bytes 786464 | tf_op jit(solution)/shard_map/ppermute | solution.py:176
  123.7 1.9 collective-permute-start.10
  125.6 1.0 broadcast_select_fusion.refs_9_
  126.6 0.9 copy-done.3
  127.5 2.4 collective-permute-start.14
  129.9 2.2 collective-permute-done.14.refs_11_
  132.1 1.1 copy-done.2
  133.3 1.1 copy-done.4
  134.4 15.8 %shard_map.64 = bf16[4,4,8,96,128]{4,3,2,1,0:T(8,128)(2,1)S(1)} custom-call(s32[1]{0:T(128)} %bitcast.2.group_ref, bf16[768,2048]{1,0:T(8,128)(2,1)S(1)} %bitcast.24, bf16[192,2048]{1,0:T(8,128)(2,1)S(1)} %copy-done.2, bf16[192,2048]{1,0:T(8,128)(2,1)} %broadcast_select_fusion.2.refs_1_, bf16[192,2048]{1,0:T(8,128)(2,1)S(1)} %copy-done.4, ...), custom_call_target="tpu_custom_call" | custom-call | flops 7247757312 | bytes 15728640 | tf_op jit(solution)/shard_map/pallas_call | solution.py:94
  150.2 1.7 copy-done
  151.9 15.5 %all-to-all-start.1 = ((bf16[128,96,128]{2,1,0:T(8,128)(2,1)}), bf16[128,96,128]{2,1,0:T(8,128)(2,1)}, u32[]{:S(2)}, u32[]{:S(2)}) async-start(bf16[128,96,128]{2,1,0:T(8,128)(2,1)} %bitcast.25), calls=%async_computation.1 | async-start | bytes 6291456 | tf_op jit(solution)/shard_map/all_to_all | solution.py:185
  167.6 0.2 fusion.6
  168.1 0.2 fusion.3
  168.8 99.2 %all-to-all-done.1 = bf16[128,96,128]{2,1,0:T(8,128)(2,1)} async-done(((bf16[128,96,128]{2,1,0:T(8,128)(2,1)}), bf16[128,96,128]{2,1,0:T(8,128)(2,1)}, u32[]{:S(2)}, u32[]{:S(2)}) %all-to-all-start.1) | async-done | bytes 3145760 | tf_op jit(solution)/shard_map/all_to_all | solution.py:185
  268.0 4.1 %reshape.347 = bf16[768,2048]{1,0:T(8,128)(2,1)S(1)} reshape(bf16[128,96,128]{2,1,0:T(8,128)(2,1)} %all-to-all-done.1) | data formatting | bytes 6291456 | tf_op jit(solution)/shard_map/reshape | solution.py:193
  272.2 0.7 fusion.31
  272.8 1.4 fusion
  (39 shorter events, 1.6 us)
Async XLA Ops:
  2.3 14.4 %collective-permute-start = (bf16[64,2176]{1,0:T(8,128)(2,1)S(1)}, bf16[64,2176]{1,0:T(8,128)(2,1)S(1)}, u32[]{:S(2)}, u32[]{:S(2)}) collective-permute-start(bf16[64,2176]{1,0:T(8,128)(2,1)S(1)} %copy.31), channel_id=1, source_target_pairs={{0,32},{32,0},{1,33},{33,1},{2,34},{34,2},{3,35},{35,3},{4,36},{36... | collective-permute-start | bytes 835592 | tf_op jit(solution)/shard_map/ppermute | solution.py:45
  4.7 24.5 %collective-permute-start.1 = (bf16[64,2176]{1,0:T(8,128)(2,1)S(1)}, bf16[64,2176]{1,0:T(8,128)(2,1)S(1)}, u32[]{:S(2)}, u32[]{:S(2)}) collective-permute-start(bf16[64,2176]{1,0:T(8,128)(2,1)S(1)} %copy.31), channel_id=1, source_target_pairs={{0,112},{16,96},{32,80},{48,64},{64,48},{80,32},{96,16},{112,0},{1... | collective-permute-start | bytes 835592 | tf_op jit(solution)/shard_map/ppermute | solution.py:45
  7.0 27.5 %collective-permute-start.2 = (bf16[64,2176]{1,0:T(8,128)(2,1)S(1)}, bf16[64,2176]{1,0:T(8,128)(2,1)S(1)}, u32[]{:S(2)}, u32[]{:S(2)}) collective-permute-start(bf16[64,2176]{1,0:T(8,128)(2,1)S(1)} %copy.31), channel_id=1, source_target_pairs={{0,80},{16,64},{64,16},{80,0},{1,81},{17,65},{65,17},{81,1},{2,82}... | collective-permute-start | bytes 835592 | tf_op jit(solution)/shard_map/ppermute | solution.py:45
  12.8 35.4 %collective-permute-start.3 = (bf16[192,2048]{1,0:T(8,128)(2,1)}, bf16[192,2048]{1,0:T(8,128)(2,1)S(1)}, u32[]{:S(2)}, u32[]{:S(2)}) collective-permute-start(bf16[192,2048]{1,0:T(8,128)(2,1)} %bitcast.27), channel_id=1, source_target_pairs={{32,17},{48,1},{17,32},{1,48},{0,16},{16,0},{33,49},{49,33},{34,19... | collective-permute-start | bytes 2359304 | tf_op jit(solution)/shard_map/ppermute | solution.py:159
  48.2 0.9 copy-start.1
  49.1 83.1 %all-to-all-start = ((bf16[32,24,2048]{2,1,0:T(8,128)(2,1)}), bf16[32,24,2048]{2,1,0:T(8,128)(2,1)S(1)}, u32[]{:S(2)}, u32[]{:S(2)}) async-start(bf16[32,24,2048]{2,1,0:T(8,128)(2,1)} %bitcast.26), calls=%async_computation | async-start | bytes 6291456 | tf_op jit(solution)/shard_map/all_to_all | solution.py:172
  61.1 22.3 %collective-permute-start.7 = (bf16[192,2048]{1,0:T(8,128)(2,1)}, bf16[192,2048]{1,0:T(8,128)(2,1)}, u32[]{:S(2)}, u32[]{:S(2)}) collective-permute-start(bf16[192,2048]{1,0:T(8,128)(2,1)} %bitcast.28), channel_id=1, source_target_pairs={{32,17},{48,1},{17,32},{1,48},{0,16},{16,0},{33,49},{49,33},{34,19... | collective-permute-start | bytes 2359304 | tf_op jit(solution)/shard_map/ppermute | solution.py:159
  63.9 36.0 %collective-permute-start.11 = (bf16[192,2048]{1,0:T(8,128)(2,1)}, bf16[192,2048]{1,0:T(8,128)(2,1)}, u32[]{:S(2)}, u32[]{:S(2)}) collective-permute-start(bf16[192,2048]{1,0:T(8,128)(2,1)} %bitcast.29), channel_id=1, source_target_pairs={{32,17},{48,1},{17,32},{1,48},{0,16},{16,0},{33,49},{49,33},{34,19... | collective-permute-start | bytes 2359304 | tf_op jit(solution)/shard_map/ppermute | solution.py:159
  66.7 44.0 %collective-permute-start.4 = (bf16[192,2048]{1,0:T(8,128)(2,1)}, bf16[192,2048]{1,0:T(8,128)(2,1)}, u32[]{:S(2)}, u32[]{:S(2)}) collective-permute-start(bf16[192,2048]{1,0:T(8,128)(2,1)} %copy-done.1), channel_id=1, source_target_pairs={{1,17},{17,1},{32,48},{48,32},{3,19},{19,3},{34,50},{50,34},{5,21}... | collective-permute-start | bytes 2359304 | tf_op jit(solution)/shard_map/ppermute | solution.py:176
  83.4 31.9 %collective-permute-start.8 = (bf16[192,2048]{1,0:T(8,128)(2,1)}, bf16[192,2048]{1,0:T(8,128)(2,1)}, u32[]{:S(2)}, u32[]{:S(2)}) collective-permute-start(bf16[192,2048]{1,0:T(8,128)(2,1)} %collective-permute-done.7.refs_4_), channel_id=1, source_target_pairs={{1,17},{17,1},{32,48},{48,32},{3,19},{19,3},{34,50},{50,34},{5,21}... | collective-permute-start | bytes 2359304 | tf_op jit(solution)/shard_map/ppermute | solution.py:176
  85.9 39.7 %copy-start.5 = (bf16[1,1,192,2048]{3,2,1,0:T(8,128)(2,1)S(1)}, bf16[1,1,192,2048]{3,2,1,0:T(8,128)(2,1)}, u32[]{:S(2)}) copy-start(bf16[1,1,192,2048]{3,2,1,0:T(8,128)(2,1)} %param.11) | copy-start | bytes 2359300
  85.9 40.7 %collective-permute-start.5 = (bf16[192,2048]{1,0:T(8,128)(2,1)}, bf16[192,2048]{1,0:T(8,128)(2,1)S(1)}, u32[]{:S(2)}, u32[]{:S(2)}) collective-permute-start(bf16[192,2048]{1,0:T(8,128)(2,1)} %copy-done.1), channel_id=1, source_target_pairs={{0,1},{1,0},{2,3},{3,2},{4,5},{5,4},{6,7},{7,6},{8,9},{9,8},{10,11... | collective-permute-start | bytes 2359304 | tf_op jit(solution)/shard_map/ppermute | solution.py:45
  99.9 23.8 %collective-permute-start.12 = (bf16[192,2048]{1,0:T(8,128)(2,1)}, bf16[192,2048]{1,0:T(8,128)(2,1)S(1)}, u32[]{:S(2)}, u32[]{:S(2)}) collective-permute-start(bf16[192,2048]{1,0:T(8,128)(2,1)} %collective-permute-done.11.refs_8_), channel_id=1, source_target_pairs={{1,17},{17,1},{32,48},{48,32},{3,19},{19,3},{34,50},{50,34},{5,21}... | collective-permute-start | bytes 2359304 | tf_op jit(solution)/shard_map/ppermute | solution.py:176
  101.8 28.1 %collective-permute-start.13 = (bf16[192,2048]{1,0:T(8,128)(2,1)}, bf16[192,2048]{1,0:T(8,128)(2,1)}, u32[]{:S(2)}, u32[]{:S(2)}) collective-permute-start(bf16[192,2048]{1,0:T(8,128)(2,1)} %collective-permute-done.11.refs_8_), channel_id=1, source_target_pairs={{0,1},{1,0},{2,3},{3,2},{4,5},{5,4},{6,7},{7,6},{8,9},{9,8},{10,11... | collective-permute-start | bytes 2359304 | tf_op jit(solution)/shard_map/ppermute | solution.py:45
  110.6 19.3 %collective-permute-start.9 = (bf16[192,2048]{1,0:T(8,128)(2,1)}, bf16[192,2048]{1,0:T(8,128)(2,1)}, u32[]{:S(2)}, u32[]{:S(2)}) collective-permute-start(bf16[192,2048]{1,0:T(8,128)(2,1)} %collective-permute-done.7.refs_4_), channel_id=1, source_target_pairs={{0,1},{1,0},{2,3},{3,2},{4,5},{5,4},{6,7},{7,6},{8,9},{9,8},{10,11... | collective-permute-start | bytes 2359304 | tf_op jit(solution)/shard_map/ppermute | solution.py:45
  115.3 14.7 %collective-permute-start.6 = (bf16[192,2048]{1,0:T(8,128)(2,1)}, bf16[192,2048]{1,0:T(8,128)(2,1)}, u32[]{:S(2)}, u32[]{:S(2)}) collective-permute-start(bf16[192,2048]{1,0:T(8,128)(2,1)} %broadcast_select_fusion.2.refs_1_), channel_id=1, source_target_pairs={{0,1},{1,0},{2,3},{3,2},{4,5},{5,4},{6,7},{7,6},{8,9},{9,8},{10,11... | collective-permute-start | bytes 2359304 | tf_op jit(solution)/shard_map/ppermute | solution.py:45
  123.7 6.2 %collective-permute-start.10 = (bf16[192,2048]{1,0:T(8,128)(2,1)}, bf16[192,2048]{1,0:T(8,128)(2,1)}, u32[]{:S(2)}, u32[]{:S(2)}) collective-permute-start(bf16[192,2048]{1,0:T(8,128)(2,1)} %broadcast_select_fusion.1.refs_5_), channel_id=1, source_target_pairs={{0,1},{1,0},{2,3},{3,2},{4,5},{5,4},{6,7},{7,6},{8,9},{9,8},{10,11... | collective-permute-start | bytes 2359304 | tf_op jit(solution)/shard_map/ppermute | solution.py:45
  126.6 0.9 copy-start.3
  127.5 4.6 %collective-permute-start.14 = (bf16[192,2048]{1,0:T(8,128)(2,1)}, bf16[192,2048]{1,0:T(8,128)(2,1)}, u32[]{:S(2)}, u32[]{:S(2)}) collective-permute-start(bf16[192,2048]{1,0:T(8,128)(2,1)} %broadcast_select_fusion.refs_9_), channel_id=1, source_target_pairs={{0,1},{1,0},{2,3},{3,2},{4,5},{5,4},{6,7},{7,6},{8,9},{9,8},{10,11... | collective-permute-start | bytes 2359304 | tf_op jit(solution)/shard_map/ppermute | solution.py:45
  132.1 1.1 copy-start.2
  133.3 1.1 copy-start.4
  150.2 1.7 copy-start
  151.9 15.5 %copy-start.6 = (s32[64,8]{0,1:T(8,128)S(1)}, s32[64,8]{0,1:T(8,128)}, u32[]{:S(2)}) copy-start(s32[64,8]{0,1:T(8,128)} %param.7) | copy-start | bytes 6148
  151.9 15.6 %copy-start.7 = (f32[64,8]{0,1:T(8,128)S(1)}, f32[64,8]{0,1:T(8,128)}, u32[]{:S(2)}) copy-start(f32[64,8]{0,1:T(8,128)} %param.8) | copy-start | bytes 6148
  151.9 116.1 %all-to-all-start.1 = ((bf16[128,96,128]{2,1,0:T(8,128)(2,1)}), bf16[128,96,128]{2,1,0:T(8,128)(2,1)}, u32[]{:S(2)}, u32[]{:S(2)}) async-start(bf16[128,96,128]{2,1,0:T(8,128)(2,1)} %bitcast.25), calls=%async_computation.1 | async-start | bytes 6291456 | tf_op jit(solution)/shard_map/all_to_all | solution.py:185

commit v3 on v1

v3 whole, which is shorter than its diff:
```python
import jax
import jax.numpy as jnp
from jax import lax
from jax.experimental import pallas as pl
from jax.experimental.pallas import tpu as pltpu
from jax.sharding import Mesh, PartitionSpec as P

SIZES = (4, 2, 2, 2, 8, 2)
NAMES = ("x", "h", "p", "b", "z", "c")
MOST = 6
CHUNKS = 4
PLANE = 32
EXTRA = 128
SPLIT = 4


def flips(axes):
    return [(i, i ^ (2 ** len(axes) - 1)) for i in range(2 ** len(axes))]


def place(p, b, c):
    return p * 4 + b * 2 + c


FIRST = [
    (place(1, 0, 0), place(0, 1, 1)),
    (place(1, 1, 0), place(0, 0, 1)),
    (place(0, 1, 1), place(1, 0, 0)),
    (place(0, 0, 1), place(1, 1, 0)),
    (place(0, 0, 0), place(0, 1, 0)),
    (place(0, 1, 0), place(0, 0, 0)),
    (place(1, 0, 1), place(1, 1, 1)),
    (place(1, 1, 1), place(1, 0, 1)),
]
SECOND = [
    (place(0, 0, 1), place(0, 1, 1)),
    (place(0, 1, 1), place(0, 0, 1)),
    (place(1, 0, 0), place(1, 1, 0)),
    (place(1, 1, 0), place(1, 0, 0)),
]
PARTNERS = (("p",), ("h", "p", "b"), ("h", "b"))


def swap(value, axes):
    return lax.ppermute(value, axes, flips(axes))


def expert_kernel(rows_ref, *refs):
    pieces, out_ref = refs[:4], refs[4]
    panels, sems = refs[5:8], refs[8]
    first = pl.program_id(0) == 0
    hid = pieces[0].shape[0] // 3
    copies = [
        pltpu.make_async_copy(
            piece.at[pl.ds(k * hid, hid)], panel.at[pl.ds(q * hid, hid)], sems.at[k * SPLIT + q]
        )
        for k, panel in enumerate(panels)
        for q, piece in enumerate(pieces)
    ]

    @pl.when(first)
    def _():
        for copy in copies:
            copy.start()
        for copy in copies[: 2 * SPLIT]:
            copy.wait()

    gate, up, down = panels
    dims = (((1,), (1,)), ((), ()))
    rows = rows_ref[...]
    g = lax.dot_general(rows, gate[...], dims, preferred_element_type=jnp.float32)
    u = lax.dot_general(rows, up[...], dims, preferred_element_type=jnp.float32)
    hidden = (g / (1.0 + jnp.exp(-g)) * u).astype(jnp.bfloat16)

    @pl.when(first)
    def _():
        for copy in copies[2 * SPLIT :]:
            copy.wait()

    out_ref[...] = jnp.dot(hidden, down[...], preferred_element_type=jnp.float32).astype(
        jnp.bfloat16
    )


def run_expert(rows, pieces):
    count, width = rows.shape
    hid = pieces[0].shape[0] // 3
    tile = 256
    block = pl.BlockSpec((tile, width), lambda i: (i, 0))
    return pl.pallas_call(
        expert_kernel,
        grid=(count // tile,),
        out_shape=jax.ShapeDtypeStruct((count, width), jnp.bfloat16),
        in_specs=[block] + [pl.BlockSpec(memory_space=pltpu.HBM)] * SPLIT,
        out_specs=block,
        scratch_shapes=[pltpu.VMEM((SPLIT * hid, width), jnp.bfloat16)] * 3
        + [pltpu.SemaphoreType.DMA((3 * SPLIT,))],
        compiler_params=pltpu.CompilerParams(vmem_limit_bytes=60 * 1024 * 1024),
        cost_estimate=pl.CostEstimate(
            flops=2 * count * width * hid * 12,
            bytes_accessed=4 * count * width + 24 * hid * width,
            transcendentals=count * hid * 4,
        ),
    )(rows, *pieces)


def pick_kernel(hit_ref, *refs):
    sources, out_ref = refs[:-1], refs[-1]
    count = sources[0].shape[0]
    total = None
    for k, source in enumerate(sources):
        part = jnp.dot(
            hit_ref[:, k * count : (k + 1) * count], source[...], preferred_element_type=jnp.float32
        )
        total = part if total is None else total + part
    out_ref[...] = total.astype(jnp.bfloat16)


def pick_rows(hit, sources, width):
    count, tokens = hit.shape
    tile = 256
    whole = pl.BlockSpec((tokens // len(sources), width), lambda i: (0, 0))
    return pl.pallas_call(
        pick_kernel,
        grid=(count // tile,),
        out_shape=jax.ShapeDtypeStruct((count, width), jnp.bfloat16),
        in_specs=[pl.BlockSpec((tile, tokens), lambda i: (i, 0))] + [whole] * len(sources),
        out_specs=pl.BlockSpec((tile, width), lambda i: (i, 0)),
        compiler_params=pltpu.CompilerParams(vmem_limit_bytes=16 * 1024 * 1024),
        cost_estimate=pl.CostEstimate(
            flops=2 * count * tokens * width,
            bytes_accessed=2 * (count + tokens) * (width + tokens),
            transcendentals=0,
        ),
    )(hit, *sources)


def matches(named, experts):
    return named[:, :, None] == experts[None, None, :]


def ranks(chosen, count):
    order = jnp.arange(chosen.shape[0], dtype=jnp.int32)
    before = (order[:, None] // count == order[None, :] // count) & (order[None, :] < order[:, None])
    return jnp.dot(
        before.astype(jnp.bfloat16), chosen.astype(jnp.bfloat16), preferred_element_type=jnp.float32
    ).astype(jnp.int32)


def shards(tokens, routes, route_weights, gate_weight, up_weight, down_weight):
    count, width = tokens.shape
    top = routes.shape[1]
    h, p, c = (lax.axis_index(n) for n in ("h", "p", "c"))
    zs = SIZES[4]

    high = route_weights.astype(jnp.bfloat16)
    low = (route_weights - high.astype(jnp.float32)).astype(jnp.bfloat16)
    fields = (routes.astype(jnp.bfloat16), high, low)
    meta = sum(
        jnp.pad(f, ((0, 0), (top * k, EXTRA - top * (k + 1)))) for k, f in enumerate(fields)
    )
    record = jnp.concatenate([tokens, meta], axis=1)
    received = [swap(record, axes) for axes in PARTNERS]

    own = jnp.concatenate([gate_weight[0, 0], up_weight[0, 0], down_weight[0, 0]], axis=0)
    own, received = lax.optimization_barrier((own, received))
    axes = ("p", "b", "c")
    first = lax.ppermute(own, axes, FIRST)
    second = jnp.where(c == p, own, lax.ppermute(first, axes, SECOND))
    pieces = [first, second, swap(first, ("c",)), swap(second, ("c",))]

    records = [record] + received
    meta = jnp.concatenate([r[:, width:] for r in records], axis=0).astype(jnp.float32)
    named = meta[:, :top].astype(jnp.int32)
    weight = meta[:, top : 2 * top] + meta[:, 2 * top : 3 * top]
    target = jnp.arange(PLANE, dtype=jnp.int32)
    match = matches(named, (2 * (target % zs) + p) * 8 + 2 * (target // zs) + h)
    chosen = jnp.any(match, axis=1)
    weight = jnp.sum(jnp.where(match, weight[:, :, None], 0.0), axis=1)
    chunk = jnp.arange(CHUNKS * count, dtype=jnp.int32) // count
    slot = jnp.where(chosen, ranks(chosen, count) + (chunk * MOST)[:, None], -1).T
    slots = jnp.arange(CHUNKS * MOST, dtype=jnp.int32)
    hit = (slot[:, None, :] == slots[None, :, None]).reshape(PLANE * CHUNKS * MOST, CHUNKS * count)
    spread = jnp.broadcast_to(
        weight.T[:, None, :], (PLANE, CHUNKS * MOST, CHUNKS * count)
    ).reshape(hit.shape)
    spread = jnp.where(hit, spread, 0.0)
    upper = spread.astype(jnp.bfloat16)
    lower = (spread - upper.astype(jnp.float32)).astype(jnp.bfloat16)

    def exchange(rows):
        share = (PLANE, CHUNKS * MOST, width)
        return lax.all_to_all(rows.reshape(share), ("x", "z"), 0, 0, tiled=True).reshape(-1, width)

    sent = pick_rows(hit.astype(jnp.bfloat16), records, width)
    returned = exchange(run_expert(exchange(sent), pieces))

    dims = (((0,), (0,)), ((), ()))
    partial = lax.dot_general(
        upper, returned, dims, preferred_element_type=jnp.float32
    ) + lax.dot_general(lower, returned, dims, preferred_element_type=jnp.float32)
    mixed = partial[:count]
    for k, names in enumerate(PARTNERS, 1):
        part = partial[k * count : (k + 1) * count].astype(jnp.bfloat16)
        mixed = mixed + swap(part, names).astype(jnp.float32)
    return mixed.astype(jnp.bfloat16)


def solution(mesh):
    fine = Mesh(mesh.devices.reshape(SIZES), NAMES)
    rows = P(NAMES, None)
    weights = P(("x", "h", "p", "b"), ("z", "c"), None, None)
    return jax.shard_map(
        shards,
        mesh=fine,
        in_specs=(rows, rows, rows, weights, weights, weights),
        out_specs=rows,
        check_vma=False,
    )
```

time: 281 us -> 270 us (0.961)
  the two profiles are of different devices: /device:TPU:4 before, /device:TPU:1 now
where the time goes in v3:
time: 270 us; the launch traced here: 269 us
  waiting for transfers between devices  173 us (64%)
  starting transfers between devices  60 us (22%)
  Pallas kernels  18.7 us (7%)
  other arithmetic  9.64 us (4%)
  matrix products  4.71 us (2%)
  local copies, waits for them, and re-layouts  3.61 us (1%)
    all_to_all x2, waiting for transfers between devices, exchange(): lax.all_to_all(rows.reshape(share), ('x', 'z'), 0, 0, tiled=True)  78.5 us
    ppermute x8, waiting for transfers between devices, swap(): return lax.ppermute(value, axes, flips(axes))  39.2 us
    ppermute x8, starting transfers between devices, swap(): return lax.ppermute(value, axes, flips(axes))  30.2 us
    ppermute x1, waiting for transfers between devices, shards(): first = lax.ppermute(own, axes, FIRST)  29.9 us
    ppermute x1, waiting for transfers between devices, shards(): second = jnp.where(c == p, own, lax.ppermute(first, axes, SECOND))  24.9 us
    all_to_all x2, starting transfers between devices, exchange(): lax.all_to_all(rows.reshape(share), ('x', 'z'), 0, 0, tiled=True)  22.9 us
    pallas_call x1, Pallas kernels, run_expert(): pl.pallas_call(expert_kernel, grid=(count // tile,), out_shape=jax.ShapeD...  13.7 us
  transfers between devices with their start and end apart: 12, of which 10 were waited for; matrix products, arithmetic and copies ran while one was open for 3% of the time, Pallas kernels for 2%

profile of v3, /device:TPU:1, one launch (start us, length us, event | category | flops | bytes accessed | tf_op | source)
XLA Modules:
  0.0 269.5 jit_solution(3194191535622835529)
XLA Ops:
  0.0 0.7 convert_element_type.62
  0.7 0.1 copy.32
  0.8 0.1 copy.34
  0.9 0.8 copy.33
  1.7 0.7 convert_element_type.61
  2.3 0.1 copy.31
  2.5 0.1 pad_add_fusion
  2.5 1.0 pad_maximum_fusion.1.refs_0_
  3.5 7.5 %collective-permute-start.2 = (bf16[64,2176]{1,0:T(8,128)(2,1)S(1)}, bf16[64,2176]{1,0:T(8,128)(2,1)S(1)}, u32[]{:S(2)}, u32[]{:S(2)}) collective-permute-start(bf16[64,2176]{1,0:T(8,128)(2,1)S(1)} %pad_maximum_fusion.1.refs_0_), channel_id=1, source_target_pairs={{0,80},{16,64},{64,16},{80,0},{1,81},{17,65},{65,17},{81,1},{2,82}... | collective-permute-start | bytes 835592 | tf_op jit(solution)/shard_map/ppermute | solution.py:45
  11.0 1.9 collective-permute-start.1
  13.0 3.1 %collective-permute-start = (bf16[64,2176]{1,0:T(8,128)(2,1)S(1)}, bf16[64,2176]{1,0:T(8,128)(2,1)S(1)}, u32[]{:S(2)}, u32[]{:S(2)}) collective-permute-start(bf16[64,2176]{1,0:T(8,128)(2,1)S(1)} %pad_maximum_fusion.1.refs_0_), channel_id=1, source_target_pairs={{0,32},{32,0},{1,33},{33,1},{2,34},{34,2},{3,35},{35,3},{4,36},{36... | collective-permute-start | bytes 835592 | tf_op jit(solution)/shard_map/ppermute | solution.py:45
  16.1 1.8 pad_maximum_fusion
  17.8 10.2 %collective-permute-done.2.refs_3_ = bf16[64,2176]{1,0:T(8,128)(2,1)S(1)} collective-permute-done((bf16[64,2176]{1,0:T(8,128)(2,1)S(1)}, bf16[64,2176]{1,0:T(8,128)(2,1)S(1)}, u32[]{:S(2)}, u32[]{:S(2)}) %collective-permute-start.2) | collective-permute-done | bytes 278560 | tf_op jit(solution)/shard_map/ppermute | solution.py:45
  28.0 7.8 %collective-permute-done.1.refs_2_ = bf16[64,2176]{1,0:T(8,128)(2,1)S(1)} collective-permute-done((bf16[64,2176]{1,0:T(8,128)(2,1)S(1)}, bf16[64,2176]{1,0:T(8,128)(2,1)S(1)}, u32[]{:S(2)}, u32[]{:S(2)}) %collective-permute-start.1) | collective-permute-done | bytes 278560 | tf_op jit(solution)/shard_map/ppermute | solution.py:45
  35.9 0.4 collective-permute-done.refs_1_
  36.3 5.1 %collective-permute-start.3 = (bf16[576,2048]{1,0:T(8,128)(2,1)S(1)}, bf16[576,2048]{1,0:T(8,128)(2,1)}, u32[]{:S(2)}, u32[]{:S(2)}) collective-permute-start(bf16[576,2048]{1,0:T(8,128)(2,1)S(1)} %pad_maximum_fusion), channel_id=1, source_target_pairs={{32,17},{48,1},{17,32},{1,48},{0,16},{16,0},{33,49},{49,33},{34,19... | collective-permute-start | bytes 7077896 | tf_op jit(solution)/shard_map/ppermute | solution.py:168
  41.4 0.1 eq.68
  41.5 0.8 slice_add_fusion.1
  42.3 1.0 copy.35
  43.3 0.1 compare_reduce_fusion
  43.4 0.2 fusion.14
  43.7 0.2 fusion.16.hit_ref
  43.9 5.0 %shard_map.64 = bf16[768,2048]{1,0:T(8,128)(2,1)} custom-call(bf16[768,256]{1,0:T(8,128)(2,1)S(1)} %fusion.16.hit_ref, bf16[64,2176]{1,0:T(8,128)(2,1)S(1)} %pad_maximum_fusion.1.refs_0_, bf16[64,2176]{1,0:T(8,128)(2,1)S(1)} %collective-permute-done.refs_1_, bf16[64,2176]{1,0:T(8,128)(2,1)S(1)} %collective-permute-done.1.refs_2_, ...), custom_call_target="tpu_custom_call" | custom-call | flops 805306368 | bytes 4718592 | tf_op jit(solution)/shard_map/pallas_call | solution.py:123
  48.9 13.0 %all-to-all-start = ((bf16[32,24,2048]{2,1,0:T(8,128)(2,1)}), bf16[32,24,2048]{2,1,0:T(8,128)(2,1)}, u32[]{:S(2)}, u32[]{:S(2)}) async-start(bf16[32,24,2048]{2,1,0:T(8,128)(2,1)} %bitcast.6), calls=%async_computation | async-start | bytes 6291456 | tf_op jit(solution)/shard_map/all_to_all | solution.py:193
  61.9 29.9 %collective-permute-done.3.refs_0_ = bf16[576,2048]{1,0:T(8,128)(2,1)} collective-permute-done((bf16[576,2048]{1,0:T(8,128)(2,1)S(1)}, bf16[576,2048]{1,0:T(8,128)(2,1)}, u32[]{:S(2)}, u32[]{:S(2)}) %collective-permute-start.3) | collective-permute-done | bytes 2359328 | tf_op jit(solution)/shard_map/ppermute | solution.py:168
  91.8 1.9 collective-permute-start.4
  93.8 3.4 %collective-permute-start.5 = (bf16[576,2048]{1,0:T(8,128)(2,1)}, bf16[576,2048]{1,0:T(8,128)(2,1)}, u32[]{:S(2)}, u32[]{:S(2)}) collective-permute-start(bf16[576,2048]{1,0:T(8,128)(2,1)} %collective-permute-done.3.refs_0_), channel_id=1, source_target_pairs={{0,1},{1,0},{2,3},{3,2},{4,5},{5,4},{6,7},{7,6},{8,9},{9,8},{10,11... | collective-permute-start | bytes 7077896 | tf_op jit(solution)/shard_map/ppermute | solution.py:45
  97.1 24.9 %collective-permute-done.4 = bf16[576,2048]{1,0:T(8,128)(2,1)} collective-permute-done((bf16[576,2048]{1,0:T(8,128)(2,1)}, bf16[576,2048]{1,0:T(8,128)(2,1)}, u32[]{:S(2)}, u32[]{:S(2)}) %collective-permute-start.4) | collective-permute-done | bytes 2359328 | tf_op jit(solution)/shard_map/ppermute | solution.py:169
  122.0 3.4 %broadcast_select_fusion.refs_1_ = bf16[576,2048]{1,0:T(8,128)(2,1)} fusion(bf16[576,2048]{1,0:T(8,128)(2,1)S(1)} %pad_maximum_fusion, bf16[576,2048]{1,0:T(8,128)(2,1)} %collective-permute-done.4, pred[]{:T(512)S(6)} %eq.71), kind=kLoop, calls=%fused_computation.8 | loop fusion | flops 1179648 | bytes 7077889 | tf_op jit(solution)/shard_map/jit(_where)/select_n | solution.py:169
  125.4 1.9 collective-permute-start.6
  127.3 7.8 %all-to-all-done = bf16[32,24,2048]{2,1,0:T(8,128)(2,1)} async-done(((bf16[32,24,2048]{2,1,0:T(8,128)(2,1)}), bf16[32,24,2048]{2,1,0:T(8,128)(2,1)}, u32[]{:S(2)}, u32[]{:S(2)}) %all-to-all-start) | async-done | bytes 3145760 | tf_op jit(solution)/shard_map/all_to_all | solution.py:193
  135.2 1.4 copy-done.1
  136.5 13.7 %shard_map.65 = bf16[768,2048]{1,0:T(8,128)(2,1)} custom-call(bf16[768,2048]{1,0:T(8,128)(2,1)} %bitcast.7.rows_ref, bf16[576,2048]{1,0:T(8,128)(2,1)} %collective-permute-done.3.refs_0_, bf16[576,2048]{1,0:T(8,128)(2,1)} %broadcast_select_fusion.refs_1_, bf16[576,2048]{1,0:T(8,128)(2,1)} %collective-permute-done.5.refs_2_, bf16[576,2048]{1,0:T(8,128)(2,1)} %copy-done.1), custom_call_target="tpu_custom_call" | custom-call | flops 7247757312 | bytes 15728640 | tf_op jit(solution)/shard_map/pallas_call | solution.py:90
  150.3 0.0 copy-start
  150.3 9.9 %all-to-all-start.1 = ((bf16[32,24,2048]{2,1,0:T(8,128)(2,1)}), bf16[32,24,2048]{2,1,0:T(8,128)(2,1)S(1)}, u32[]{:S(2)}, u32[]{:S(2)}) async-start(bf16[32,24,2048]{2,1,0:T(8,128)(2,1)} %bitcast.20), calls=%async_computation.1 | async-start | bytes 6291456 | tf_op jit(solution)/shard_map/all_to_all | solution.py:193
  160.2 0.1 copy.36
  160.2 0.1 fusion.27
  160.4 70.6 %all-to-all-done.1 = bf16[32,24,2048]{2,1,0:T(8,128)(2,1)S(1)} async-done(((bf16[32,24,2048]{2,1,0:T(8,128)(2,1)}), bf16[32,24,2048]{2,1,0:T(8,128)(2,1)S(1)}, u32[]{:S(2)}, u32[]{:S(2)}) %all-to-all-start.1) | async-done | bytes 3145760 | tf_op jit(solution)/shard_map/all_to_all | solution.py:193
  231.0 2.2 fusion.7
  233.2 2.3 fusion.42
  235.5 0.1 fusion.41
  235.5 4.9 %collective-permute-start.7 = (bf16[64,2048]{1,0:T(8,128)(2,1)S(1)}, bf16[64,2048]{1,0:T(8,128)(2,1)S(1)}, u32[]{:S(2)}, u32[]{:S(2)}) collective-permute-start(bf16[64,2048]{1,0:T(8,128)(2,1)S(1)} %get-tuple-element.13), channel_id=1, source_target_pairs={{0,32},{32,0},{1,33},{33,1},{2,34},{34,2},{3,35},{35,3},{4,36},{36... | collective-permute-start | bytes 786440 | tf_op jit(solution)/shard_map/ppermute | solution.py:45
  240.4 5.6 %collective-permute-start.9 = (bf16[64,2048]{1,0:T(8,128)(2,1)S(1)}, bf16[64,2048]{1,0:T(8,128)(2,1)S(1)}, u32[]{:S(2)}, u32[]{:S(2)}) collective-permute-start(bf16[64,2048]{1,0:T(8,128)(2,1)S(1)} %get-tuple-element.14), channel_id=1, source_target_pairs={{0,80},{16,64},{64,16},{80,0},{1,81},{17,65},{65,17},{81,1},{2,82}... | collective-permute-start | bytes 786440 | tf_op jit(solution)/shard_map/ppermute | solution.py:45
  246.0 1.9 collective-permute-start.8
  247.9 5.9 %collective-permute-done.7 = bf16[64,2048]{1,0:T(8,128)(2,1)S(1)} collective-permute-done((bf16[64,2048]{1,0:T(8,128)(2,1)S(1)}, bf16[64,2048]{1,0:T(8,128)(2,1)S(1)}, u32[]{:S(2)}, u32[]{:S(2)}) %collective-permute-start.7) | collective-permute-done | bytes 262176 | tf_op jit(solution)/shard_map/ppermute | solution.py:45
  253.8 11.8 %collective-permute-done.9 = bf16[64,2048]{1,0:T(8,128)(2,1)S(1)} collective-permute-done((bf16[64,2048]{1,0:T(8,128)(2,1)S(1)}, bf16[64,2048]{1,0:T(8,128)(2,1)S(1)}, u32[]{:S(2)}, u32[]{:S(2)}) %collective-permute-start.9) | collective-permute-done | bytes 262176 | tf_op jit(solution)/shard_map/ppermute | solution.py:45
  265.7 3.0 %collective-permute-done.8 = bf16[64,2048]{1,0:T(8,128)(2,1)S(1)} collective-permute-done((bf16[64,2048]{1,0:T(8,128)(2,1)S(1)}, bf16[64,2048]{1,0:T(8,128)(2,1)S(1)}, u32[]{:S(2)}, u32[]{:S(2)}) %collective-permute-start.8) | collective-permute-done | bytes 262176 | tf_op jit(solution)/shard_map/ppermute | solution.py:45
  268.7 0.8 fusion.19
  (12 shorter events, 0.1 us)
Async XLA Ops:
  3.5 24.5 %collective-permute-start.2 = (bf16[64,2176]{1,0:T(8,128)(2,1)S(1)}, bf16[64,2176]{1,0:T(8,128)(2,1)S(1)}, u32[]{:S(2)}, u32[]{:S(2)}) collective-permute-start(bf16[64,2176]{1,0:T(8,128)(2,1)S(1)} %pad_maximum_fusion.1.refs_0_), channel_id=1, source_target_pairs={{0,80},{16,64},{64,16},{80,0},{1,81},{17,65},{65,17},{81,1},{2,82}... | collective-permute-start | bytes 835592 | tf_op jit(solution)/shard_map/ppermute | solution.py:45
  11.0 24.9 %collective-permute-start.1 = (bf16[64,2176]{1,0:T(8,128)(2,1)S(1)}, bf16[64,2176]{1,0:T(8,128)(2,1)S(1)}, u32[]{:S(2)}, u32[]{:S(2)}) collective-permute-start(bf16[64,2176]{1,0:T(8,128)(2,1)S(1)} %pad_maximum_fusion.1.refs_0_), channel_id=1, source_target_pairs={{0,112},{16,96},{32,80},{48,64},{64,48},{80,32},{96,16},{112,0},{1... | collective-permute-start | bytes 835592 | tf_op jit(solution)/shard_map/ppermute | solution.py:45
  13.0 23.3 %collective-permute-start = (bf16[64,2176]{1,0:T(8,128)(2,1)S(1)}, bf16[64,2176]{1,0:T(8,128)(2,1)S(1)}, u32[]{:S(2)}, u32[]{:S(2)}) collective-permute-start(bf16[64,2176]{1,0:T(8,128)(2,1)S(1)} %pad_maximum_fusion.1.refs_0_), channel_id=1, source_target_pairs={{0,32},{32,0},{1,33},{33,1},{2,34},{34,2},{3,35},{35,3},{4,36},{36... | collective-permute-start | bytes 835592 | tf_op jit(solution)/shard_map/ppermute | solution.py:45
  36.3 55.5 %collective-permute-start.3 = (bf16[576,2048]{1,0:T(8,128)(2,1)S(1)}, bf16[576,2048]{1,0:T(8,128)(2,1)}, u32[]{:S(2)}, u32[]{:S(2)}) collective-permute-start(bf16[576,2048]{1,0:T(8,128)(2,1)S(1)} %pad_maximum_fusion), channel_id=1, source_target_pairs={{32,17},{48,1},{17,32},{1,48},{0,16},{16,0},{33,49},{49,33},{34,19... | collective-permute-start | bytes 7077896 | tf_op jit(solution)/shard_map/ppermute | solution.py:168
  48.9 86.3 %all-to-all-start = ((bf16[32,24,2048]{2,1,0:T(8,128)(2,1)}), bf16[32,24,2048]{2,1,0:T(8,128)(2,1)}, u32[]{:S(2)}, u32[]{:S(2)}) async-start(bf16[32,24,2048]{2,1,0:T(8,128)(2,1)} %bitcast.6), calls=%async_computation | async-start | bytes 6291456 | tf_op jit(solution)/shard_map/all_to_all | solution.py:193
  91.8 30.2 %collective-permute-start.4 = (bf16[576,2048]{1,0:T(8,128)(2,1)}, bf16[576,2048]{1,0:T(8,128)(2,1)}, u32[]{:S(2)}, u32[]{:S(2)}) collective-permute-start(bf16[576,2048]{1,0:T(8,128)(2,1)} %collective-permute-done.3.refs_0_), channel_id=1, source_target_pairs={{1,17},{17,1},{32,48},{48,32},{3,19},{19,3},{34,50},{50,34},{5,21}... | collective-permute-start | bytes 7077896 | tf_op jit(solution)/shard_map/ppermute | solution.py:169
  93.8 33.5 %collective-permute-start.5 = (bf16[576,2048]{1,0:T(8,128)(2,1)}, bf16[576,2048]{1,0:T(8,128)(2,1)}, u32[]{:S(2)}, u32[]{:S(2)}) collective-permute-start(bf16[576,2048]{1,0:T(8,128)(2,1)} %collective-permute-done.3.refs_0_), channel_id=1, source_target_pairs={{0,1},{1,0},{2,3},{3,2},{4,5},{5,4},{6,7},{7,6},{8,9},{9,8},{10,11... | collective-permute-start | bytes 7077896 | tf_op jit(solution)/shard_map/ppermute | solution.py:45
  125.4 9.8 %collective-permute-start.6 = (bf16[576,2048]{1,0:T(8,128)(2,1)}, bf16[576,2048]{1,0:T(8,128)(2,1)S(1)}, u32[]{:S(2)}, u32[]{:S(2)}) collective-permute-start(bf16[576,2048]{1,0:T(8,128)(2,1)} %broadcast_select_fusion.refs_1_), channel_id=1, source_target_pairs={{0,1},{1,0},{2,3},{3,2},{4,5},{5,4},{6,7},{7,6},{8,9},{9,8},{10,11... | collective-permute-start | bytes 7077896 | tf_op jit(solution)/shard_map/ppermute | solution.py:45
  135.2 1.4 copy-start.1
  150.3 9.9 %copy-start = (f32[256,8]{1,0:T(8,128)S(1)}, f32[256,8]{1,0:T(8,128)}, u32[]{:S(2)}) copy-start(f32[256,8]{1,0:T(8,128)} %get-tuple-element.16) | copy-start | bytes 24580
  150.3 80.7 %all-to-all-start.1 = ((bf16[32,24,2048]{2,1,0:T(8,128)(2,1)}), bf16[32,24,2048]{2,1,0:T(8,128)(2,1)S(1)}, u32[]{:S(2)}, u32[]{:S(2)}) async-start(bf16[32,24,2048]{2,1,0:T(8,128)(2,1)} %bitcast.20), calls=%async_computation.1 | async-start | bytes 6291456 | tf_op jit(solution)/shard_map/all_to_all | solution.py:193
  235.5 18.3 %collective-permute-start.7 = (bf16[64,2048]{1,0:T(8,128)(2,1)S(1)}, bf16[64,2048]{1,0:T(8,128)(2,1)S(1)}, u32[]{:S(2)}, u32[]{:S(2)}) collective-permute-start(bf16[64,2048]{1,0:T(8,128)(2,1)S(1)} %get-tuple-element.13), channel_id=1, source_target_pairs={{0,32},{32,0},{1,33},{33,1},{2,34},{34,2},{3,35},{35,3},{4,36},{36... | collective-permute-start | bytes 786440 | tf_op jit(solution)/shard_map/ppermute | solution.py:45
  240.4 25.3 %collective-permute-start.9 = (bf16[64,2048]{1,0:T(8,128)(2,1)S(1)}, bf16[64,2048]{1,0:T(8,128)(2,1)S(1)}, u32[]{:S(2)}, u32[]{:S(2)}) collective-permute-start(bf16[64,2048]{1,0:T(8,128)(2,1)S(1)} %get-tuple-element.14), channel_id=1, source_target_pairs={{0,80},{16,64},{64,16},{80,0},{1,81},{17,65},{65,17},{81,1},{2,82}... | collective-permute-start | bytes 786440 | tf_op jit(solution)/shard_map/ppermute | solution.py:45
  246.0 22.7 %collective-permute-start.8 = (bf16[64,2048]{1,0:T(8,128)(2,1)S(1)}, bf16[64,2048]{1,0:T(8,128)(2,1)S(1)}, u32[]{:S(2)}, u32[]{:S(2)}) collective-permute-start(bf16[64,2048]{1,0:T(8,128)(2,1)S(1)} %get-tuple-element.15), channel_id=1, source_target_pairs={{0,112},{16,96},{32,80},{48,64},{64,48},{80,32},{96,16},{112,0},{1... | collective-permute-start | bytes 786440 | tf_op jit(solution)/shard_map/ppermute | solution.py:45

commit v4 on v3

--- a/solution.py
+++ b/solution.py
@@ -11,6 +11,8 @@
 CHUNKS = 4
 PLANE = 32
 EXTRA = 128
+LANES = 128
+WIDE = 256
 SPLIT = 4
 
 
@@ -46,56 +48,94 @@
 
 
 def expert_kernel(rows_ref, *refs):
-    pieces, out_ref = refs[:4], refs[4]
-    panels, sems = refs[5:8], refs[8]
-    first = pl.program_id(0) == 0
+    pieces, (own_out, far_out) = refs[:SPLIT], refs[SPLIT : SPLIT + 2]
+    panels, (hidden, lined, staged, in_sems, out_sems) = refs[6:9], refs[9:]
     hid = pieces[0].shape[0] // 3
     copies = [
-        pltpu.make_async_copy(
-            piece.at[pl.ds(k * hid, hid)], panel.at[pl.ds(q * hid, hid)], sems.at[k * SPLIT + q]
-        )
+        [
+            pltpu.make_async_copy(
+                piece.at[pl.ds(k * hid, hid)],
+                panel.at[pl.ds(q * hid, hid)],
+                in_sems.at[k * SPLIT + q],
+            )
+            for q, piece in enumerate(pieces)
+        ]
         for k, panel in enumerate(panels)
-        for q, piece in enumerate(pieces)
     ]
-
-    @pl.when(first)
-    def _():
-        for copy in copies:
-            copy.start()
-        for copy in copies[: 2 * SPLIT]:
-            copy.wait()
+    gates, ups, downs = copies
+    for gate_copy, up_copy in zip(gates, ups):
+        gate_copy.start()
+        up_copy.start()
+    for copy in downs:
+        copy.start()
 
     gate, up, down = panels
     dims = (((1,), (1,)), ((), ()))
     rows = rows_ref[...]
-    g = lax.dot_general(rows, gate[...], dims, preferred_element_type=jnp.float32)
-    u = lax.dot_general(rows, up[...], dims, preferred_element_type=jnp.float32)
-    hidden = (g / (1.0 + jnp.exp(-g)) * u).astype(jnp.bfloat16)
-
-    @pl.when(first)
-    def _():
-        for copy in copies[2 * SPLIT :]:
-            copy.wait()
-
-    out_ref[...] = jnp.dot(hidden, down[...], preferred_element_type=jnp.float32).astype(
-        jnp.bfloat16
-    )
+    here = 0
+    for start in range(0, SPLIT * hid, WIDE):
+        while here * hid < start + WIDE:
+            gates[here].wait()
+            ups[here].wait()
+            here += 1
+        part = slice(start, start + WIDE)
+        g = lax.dot_general(rows, gate[part, :], dims, preferred_element_type=jnp.float32)
+        u = lax.dot_general(rows, up[part, :], dims, preferred_element_type=jnp.float32)
+        hidden[:, part] = (g / (1.0 + jnp.exp(-g)) * u).astype(jnp.bfloat16)
+    for copy in downs:
+        copy.wait()
+
+    lines = down.shape[1] // LANES
+    tile = lined.shape[0] // lines
+    share = CHUNKS * MOST
+    sources = tile // share
+    writes = []
+    for k in range(rows.shape[0] // tile):
+        result = jnp.dot(
+            hidden[k * tile : (k + 1) * tile, :], down[...], preferred_element_type=jnp.float32
+        )
+        for n in range(lines):
+            lined[pl.ds(n, tile, stride=lines), :] = result[:, n * LANES : (n + 1) * LANES]
+        span = slice(k * sources, (k + 1) * sources)
+        staged[span] = lined[...].astype(jnp.bfloat16).reshape(sources, share * lines, LANES)
+        span = pl.ds(k * sources, sources)
+        cut = MOST * lines
+        for n, (out, part) in enumerate(
+            ((own_out, pl.ds(0, cut)), (far_out, pl.ds(cut, share * lines - cut)))
+        ):
+            write = pltpu.make_async_copy(
+                staged.at[span, part], out.at[span], out_sems.at[2 * k + n]
+            )
+            write.start()
+            writes.append(write)
+    for write in writes:
+        write.wait()
 
 
 def run_expert(rows, pieces):
     count, width = rows.shape
     hid = pieces[0].shape[0] // 3
-    tile = 256
-    block = pl.BlockSpec((tile, width), lambda i: (i, 0))
+    lines = width // LANES
+    tile = count // 2
+    cut = MOST * lines
+    everything = (PLANE, CHUNKS * cut, LANES)
     return pl.pallas_call(
         expert_kernel,
-        grid=(count // tile,),
-        out_shape=jax.ShapeDtypeStruct((count, width), jnp.bfloat16),
-        in_specs=[block] + [pl.BlockSpec(memory_space=pltpu.HBM)] * SPLIT,
-        out_specs=block,
+        out_shape=[
+            jax.ShapeDtypeStruct((PLANE, n, LANES), jnp.bfloat16) for n in (cut, (CHUNKS - 1) * cut)
+        ],
+        in_specs=[pl.BlockSpec(memory_space=pltpu.VMEM)]
+        + [pl.BlockSpec(memory_space=pl.ANY)] * SPLIT,
+        out_specs=[pl.BlockSpec(memory_space=pltpu.HBM)] * 2,
         scratch_shapes=[pltpu.VMEM((SPLIT * hid, width), jnp.bfloat16)] * 3
-        + [pltpu.SemaphoreType.DMA((3 * SPLIT,))],
-        compiler_params=pltpu.CompilerParams(vmem_limit_bytes=60 * 1024 * 1024),
+        + [
+            pltpu.VMEM((count, SPLIT * hid), jnp.bfloat16),
+            pltpu.VMEM((tile * lines, LANES), jnp.float32),
+            pltpu.VMEM(everything, jnp.bfloat16),
+            pltpu.SemaphoreType.DMA((3 * SPLIT,)),
+            pltpu.SemaphoreType.DMA((2 * count // tile,)),
+        ],
+        compiler_params=pltpu.CompilerParams(vmem_limit_bytes=57 * 1024 * 1024),
         cost_estimate=pl.CostEstimate(
             flops=2 * count * width * hid * 12,
             bytes_accessed=4 * count * width + 24 * hid * width,
@@ -106,14 +146,10 @@
 
 def pick_kernel(hit_ref, *refs):
     sources, out_ref = refs[:-1], refs[-1]
-    count = sources[0].shape[0]
-    total = None
-    for k, source in enumerate(sources):
-        part = jnp.dot(
-            hit_ref[:, k * count : (k + 1) * count], source[...], preferred_element_type=jnp.float32
-        )
-        total = part if total is None else total + part
-    out_ref[...] = total.astype(jnp.bfloat16)
+    rows = jnp.concatenate([source[...] for source in sources], axis=0)
+    out_ref[...] = jnp.dot(hit_ref[...], rows, preferred_element_type=jnp.float32).astype(
+        jnp.bfloat16
+    )
 
 
 def pick_rows(hit, sources, width):
@@ -181,28 +217,45 @@
     slot = jnp.where(chosen, ranks(chosen, count) + (chunk * MOST)[:, None], -1).T
     slots = jnp.arange(CHUNKS * MOST, dtype=jnp.int32)
     hit = (slot[:, None, :] == slots[None, :, None]).reshape(PLANE * CHUNKS * MOST, CHUNKS * count)
-    spread = jnp.broadcast_to(
-        weight.T[:, None, :], (PLANE, CHUNKS * MOST, CHUNKS * count)
-    ).reshape(hit.shape)
-    spread = jnp.where(hit, spread, 0.0)
+    sent = pick_rows(hit.astype(jnp.bfloat16), records, width)
+
+    def exchange(rows):
+        return lax.all_to_all(rows, ("x", "z"), 0, 0, tiled=True)
+
+    arrived = exchange(sent.reshape(PLANE, CHUNKS * MOST, width)).reshape(-1, width)
+    own_out, far_out = run_expert(arrived, pieces)
+
+    spread = jnp.where(
+        slot[:, None, :] == slots[None, :, None], weight.T[:, None, :], 0.0
+    )
     upper = spread.astype(jnp.bfloat16)
     lower = (spread - upper.astype(jnp.float32)).astype(jnp.bfloat16)
-
-    def exchange(rows):
-        share = (PLANE, CHUNKS * MOST, width)
-        return lax.all_to_all(rows.reshape(share), ("x", "z"), 0, 0, tiled=True).reshape(-1, width)
-
-    sent = pick_rows(hit.astype(jnp.bfloat16), records, width)
-    returned = exchange(run_expert(exchange(sent), pieces))
-
-    dims = (((0,), (0,)), ((), ()))
-    partial = lax.dot_general(
-        upper, returned, dims, preferred_element_type=jnp.float32
-    ) + lax.dot_general(lower, returned, dims, preferred_element_type=jnp.float32)
-    mixed = partial[:count]
-    for k, names in enumerate(PARTNERS, 1):
-        part = partial[k * count : (k + 1) * count].astype(jnp.bfloat16)
-        mixed = mixed + swap(part, names).astype(jnp.float32)
+    halves = [
+        [
+            half[:, :MOST, :count].reshape(-1, count),
+            half[:, MOST:, count:].reshape(-1, (CHUNKS - 1) * count),
+        ]
+        for half in (upper, lower)
+    ]
+    halves, own_out = lax.optimization_barrier((halves, own_out))
+
+    def combine(returned, k):
+        returned = returned.reshape(-1, width)
+        dims = (((0,), (0,)), ((), ()))
+        return lax.dot_general(
+            halves[0][k], returned, dims, preferred_element_type=jnp.float32
+        ) + lax.dot_general(halves[1][k], returned, dims, preferred_element_type=jnp.float32)
+
+    far_back = exchange(far_out)
+    own_out, far_back = lax.optimization_barrier((own_out, far_back))
+    own_back = exchange(own_out)
+    far = combine(far_back, 1).astype(jnp.bfloat16)
+    gained = [
+        swap(far[k * count : (k + 1) * count], names) for k, names in enumerate(PARTNERS)
+    ]
+    mixed = combine(own_back, 0)
+    for part in gained:
+        mixed = mixed + part.astype(jnp.float32)
     return mixed.astype(jnp.bfloat16)
 
 

time: 270 us -> 266 us (0.985); the launches traced: 269 us -> 262 us
  waiting for transfers between devices: 173 us -> 149 us
  starting transfers between devices: 60 us -> 69.7 us
  local copies, waits for them, and re-layouts: 3.61 us -> 12.8 us
    all_to_all x2 -> x3, waiting for transfers between devices: 78.5 us -> 55.2 us  [exchange(): return lax.all_to_all(rows, ('x', 'z'), 0, 0, tiled=True)]
    all_to_all x2 -> x3, starting transfers between devices: 22.9 us -> 34.3 us  [exchange(): return lax.all_to_all(rows, ('x', 'z'), 0, 0, tiled=True)]
    reshape x0 -> x6, local copies, waits for them, and re-layouts: none -> 6.5 us  [the longest x2 3.98 us: combine(): returned = returned.reshape(-1, width)]
    ppermute x8, waiting for transfers between devices: 39.2 us -> 34.4 us  [swap(): return lax.ppermute(value, axes, flips(axes))]
    ppermute x1, waiting for transfers between devices: 29.9 us -> 33.8 us  [shards(): first = lax.ppermute(own, axes, FIRST)]
    ppermute x8, starting transfers between devices: 30.2 us -> 27.4 us  [swap(): return lax.ppermute(value, axes, flips(axes))]
  transfers between devices with their start and end apart: 12 -> 13, of which waited for: 10 -> 12; matrix products, arithmetic and copies ran while one was open for 3% -> 7% of each run, Pallas kernels for 2% -> 1%
where the time goes in v4:
time: 266 us; the launch traced here: 262 us
  waiting for transfers between devices  149 us (56%)
  starting transfers between devices  69.7 us (26%)
  Pallas kernels  17.6 us (7%)
  local copies, waits for them, and re-layouts  12.8 us (5%)
  other arithmetic  9.13 us (3%)
  matrix products  4.15 us (2%)
    all_to_all x3, waiting for transfers between devices, exchange(): return lax.all_to_all(rows, ('x', 'z'), 0, 0, tiled=True)  55.2 us
    ppermute x8, waiting for transfers between devices, swap(): return lax.ppermute(value, axes, flips(axes))  34.4 us
    all_to_all x3, starting transfers between devices, exchange(): return lax.all_to_all(rows, ('x', 'z'), 0, 0, tiled=True)  34.3 us
    ppermute x1, waiting for transfers between devices, shards(): first = lax.ppermute(own, axes, FIRST)  33.8 us
    ppermute x8, starting transfers between devices, swap(): return lax.ppermute(value, axes, flips(axes))  27.4 us
    ppermute x1, waiting for transfers between devices, shards(): second = jnp.where(c == p, own, lax.ppermute(first, axes, SECOND))  25.2 us
    pallas_call x1, Pallas kernels, run_expert(): pl.pallas_call(expert_kernel, out_shape=[jax.ShapeDtypeStruct((PLANE, n,...  14.6 us
  transfers between devices with their start and end apart: 13, of which 12 were waited for; matrix products, arithmetic and copies ran while one was open for 7% of the time, Pallas kernels for 1%

profile of v4, /device:TPU:1, one launch (start us, length us, event | category | flops | bytes accessed | tf_op | source)
XLA Modules:
  0.0 262.3 jit_solution(2321890216393241754)
XLA Ops:
  0.0 0.7 convert_element_type.58
  0.7 0.8 copy.20
  1.7 0.7 convert_element_type.57
  2.5 1.0 pad_maximum_fusion.1.refs_0_
  3.5 5.0 %collective-permute-start = (bf16[64,2176]{1,0:T(8,128)(2,1)S(1)}, bf16[64,2176]{1,0:T(8,128)(2,1)S(1)}, u32[]{:S(2)}, u32[]{:S(2)}) collective-permute-start(bf16[64,2176]{1,0:T(8,128)(2,1)S(1)} %pad_maximum_fusion.1.refs_0_), channel_id=1, source_target_pairs={{0,32},{32,0},{1,33},{33,1},{2,34},{34,2},{3,35},{35,3},{4,36},{36... | collective-permute-start | bytes 835592 | tf_op jit(solution)/shard_map/ppermute | solution.py:47
  8.6 4.6 %collective-permute-start.1 = (bf16[64,2176]{1,0:T(8,128)(2,1)S(1)}, bf16[64,2176]{1,0:T(8,128)(2,1)S(1)}, u32[]{:S(2)}, u32[]{:S(2)}) collective-permute-start(bf16[64,2176]{1,0:T(8,128)(2,1)S(1)} %pad_maximum_fusion.1.refs_0_), channel_id=1, source_target_pairs={{0,112},{16,96},{32,80},{48,64},{64,48},{80,32},{96,16},{112,0},{1... | collective-permute-start | bytes 835592 | tf_op jit(solution)/shard_map/ppermute | solution.py:47
  13.2 2.5 collective-permute-start.2
  15.7 1.8 pad_maximum_fusion
  17.5 2.8 %collective-permute-done.refs_1_ = bf16[64,2176]{1,0:T(8,128)(2,1)S(1)} collective-permute-done((bf16[64,2176]{1,0:T(8,128)(2,1)S(1)}, bf16[64,2176]{1,0:T(8,128)(2,1)S(1)}, u32[]{:S(2)}, u32[]{:S(2)}) %collective-permute-start) | collective-permute-done | bytes 278560 | tf_op jit(solution)/shard_map/ppermute | solution.py:47
  20.3 1.0 collective-permute-done.1.refs_2_
  21.3 14.8 %collective-permute-done.2.refs_3_ = bf16[64,2176]{1,0:T(8,128)(2,1)S(1)} collective-permute-done((bf16[64,2176]{1,0:T(8,128)(2,1)S(1)}, bf16[64,2176]{1,0:T(8,128)(2,1)S(1)}, u32[]{:S(2)}, u32[]{:S(2)}) %collective-permute-start.2) | collective-permute-done | bytes 278560 | tf_op jit(solution)/shard_map/ppermute | solution.py:47
  36.1 4.9 %collective-permute-start.3 = (bf16[576,2048]{1,0:T(8,128)(2,1)S(1)}, bf16[576,2048]{1,0:T(8,128)(2,1)}, u32[]{:S(2)}, u32[]{:S(2)}) collective-permute-start(bf16[576,2048]{1,0:T(8,128)(2,1)S(1)} %pad_maximum_fusion), channel_id=1, source_target_pairs={{32,17},{48,1},{17,32},{1,48},{0,16},{16,0},{33,49},{49,33},{34,19... | collective-permute-start | bytes 7077896 | tf_op jit(solution)/shard_map/ppermute | solution.py:204
  41.2 0.8 slice_convert_fusion
  42.0 1.0 copy.22
  43.6 3.0 %shard_map.64 = bf16[768,2048]{1,0:T(8,128)(2,1)} custom-call(bf16[768,256]{1,0:T(8,128)(2,1)S(1)} %fusion.4.hit_ref, bf16[64,2176]{1,0:T(8,128)(2,1)S(1)} %pad_maximum_fusion.1.refs_0_, bf16[64,2176]{1,0:T(8,128)(2,1)S(1)} %collective-permute-done.refs_1_, bf16[64,2176]{1,0:T(8,128)(2,1)S(1)} %collective-permute-done.1.refs_2_, ...), custom_call_target="tpu_custom_call" | custom-call | flops 805306368 | bytes 4718592 | tf_op jit(solution)/shard_map/pallas_call | solution.py:159
  46.6 13.0 %all-to-all-start = ((bf16[32,24,2048]{2,1,0:T(8,128)(2,1)}), bf16[32,24,2048]{2,1,0:T(8,128)(2,1)}, u32[]{:S(2)}, u32[]{:S(2)}) async-start(bf16[32,24,2048]{2,1,0:T(8,128)(2,1)} %bitcast.6), calls=%async_computation | async-start | bytes 6291456 | tf_op jit(solution)/shard_map/all_to_all | solution.py:223
  59.6 33.8 %collective-permute-done.3.refs_0_ = bf16[576,2048]{1,0:T(8,128)(2,1)} collective-permute-done((bf16[576,2048]{1,0:T(8,128)(2,1)S(1)}, bf16[576,2048]{1,0:T(8,128)(2,1)}, u32[]{:S(2)}, u32[]{:S(2)}) %collective-permute-start.3) | collective-permute-done | bytes 2359328 | tf_op jit(solution)/shard_map/ppermute | solution.py:204
  93.4 3.0 %collective-permute-start.4 = (bf16[576,2048]{1,0:T(8,128)(2,1)}, bf16[576,2048]{1,0:T(8,128)(2,1)}, u32[]{:S(2)}, u32[]{:S(2)}) collective-permute-start(bf16[576,2048]{1,0:T(8,128)(2,1)} %collective-permute-done.3.refs_0_), channel_id=1, source_target_pairs={{1,17},{17,1},{32,48},{48,32},{3,19},{19,3},{34,50},{50,34},{5,21}... | collective-permute-start | bytes 7077896 | tf_op jit(solution)/shard_map/ppermute | solution.py:205
  96.4 1.9 collective-permute-start.5
  98.3 25.2 %collective-permute-done.4 = bf16[576,2048]{1,0:T(8,128)(2,1)} collective-permute-done((bf16[576,2048]{1,0:T(8,128)(2,1)}, bf16[576,2048]{1,0:T(8,128)(2,1)}, u32[]{:S(2)}, u32[]{:S(2)}) %collective-permute-start.4) | collective-permute-done | bytes 2359328 | tf_op jit(solution)/shard_map/ppermute | solution.py:205
  123.6 3.4 %broadcast_select_fusion.refs_1_ = bf16[576,2048]{1,0:T(8,128)(2,1)} fusion(bf16[576,2048]{1,0:T(8,128)(2,1)S(1)} %pad_maximum_fusion, bf16[576,2048]{1,0:T(8,128)(2,1)} %collective-permute-done.4, pred[]{:T(512)S(6)} %eq.76), kind=kLoop, calls=%fused_computation.3 | loop fusion | flops 1179648 | bytes 7077889 | tf_op jit(solution)/shard_map/jit(_where)/select_n | solution.py:205
  126.9 1.9 collective-permute-start.6
  128.9 4.0 %all-to-all-done = bf16[32,24,2048]{2,1,0:T(8,128)(2,1)} async-done(((bf16[32,24,2048]{2,1,0:T(8,128)(2,1)}), bf16[32,24,2048]{2,1,0:T(8,128)(2,1)}, u32[]{:S(2)}, u32[]{:S(2)}) %all-to-all-start) | async-done | bytes 3145760 | tf_op jit(solution)/shard_map/all_to_all | solution.py:223
  132.9 0.7 collective-permute-done.6.refs_3_
  133.6 1.4 copy-done.3
  135.0 14.6 %shard_map.65 = (bf16[32,96,128]{2,1,0:T(8,128)(2,1)}, bf16[32,288,128]{2,1,0:T(8,128)(2,1)}) custom-call(bf16[768,2048]{1,0:T(8,128)(2,1)} %bitcast.7.rows_ref, bf16[576,2048]{1,0:T(8,128)(2,1)} %collective-permute-done.3.refs_0_, bf16[576,2048]{1,0:T(8,128)(2,1)} %broadcast_select_fusion.refs_1_, bf16[576,2048]{1,0:T(8,128)(2,1)} %collective-permute-done.5.refs_2_, ...), custom_call_target="tpu_custom_call" | custom-call | flops 7247757312 | bytes 15728640 | tf_op jit(solution)/shard_map/pallas_call | solution.py:122
  149.5 13.3 %all-to-all-start.1 = ((bf16[32,288,128]{2,1,0:T(8,128)(2,1)}), bf16[32,288,128]{2,1,0:T(8,128)(2,1)S(1)}, u32[]{:S(2)}, u32[]{:S(2)}) async-start(bf16[32,288,128]{2,1,0:T(8,128)(2,1)} %get-tuple-element.25), calls=%async_computation.1 | async-start | bytes 4718592 | tf_op jit(solution)/shard_map/all_to_all | solution.py:223
  163.5 0.6 slice.57
  164.3 0.3 slice.56
  164.7 0.9 reshape.136
  165.6 0.9 reshape.135
  166.4 0.7 reshape.134
  167.1 50.0 %all-to-all-done.1 = bf16[32,288,128]{2,1,0:T(8,128)(2,1)S(1)} async-done(((bf16[32,288,128]{2,1,0:T(8,128)(2,1)}), bf16[32,288,128]{2,1,0:T(8,128)(2,1)S(1)}, u32[]{:S(2)}, u32[]{:S(2)}) %all-to-all-start.1) | async-done | bytes 2359328 | tf_op jit(solution)/shard_map/all_to_all | solution.py:223
  217.0 1.4 copy-done
  218.5 8.0 %all-to-all-start.2 = ((bf16[32,96,128]{2,1,0:T(8,128)(2,1)}), bf16[32,96,128]{2,1,0:T(8,128)(2,1)S(1)}, u32[]{:S(2)}, u32[]{:S(2)}) async-start(bf16[32,96,128]{2,1,0:T(8,128)(2,1)} %get-tuple-element.26), calls=%async_computation.2 | async-start | bytes 1572864 | tf_op jit(solution)/shard_map/all_to_all | solution.py:223
  226.5 3.7 %reshape.141 = bf16[576,2048]{1,0:T(8,128)(2,1)S(1)} reshape(bf16[32,288,128]{2,1,0:T(8,128)(2,1)} %copy-done) | data formatting | bytes 4718592 | tf_op jit(solution)/shard_map/reshape | solution.py:243
  230.2 1.8 fusion.19
  232.0 0.8 fusion
  232.8 4.2 %collective-permute-start.7 = (bf16[64,2048]{1,0:T(8,128)(2,1)S(1)}, bf16[64,2048]{1,0:T(8,128)(2,1)S(1)}, u32[]{:S(2)}, u32[]{:S(2)}) collective-permute-start(bf16[64,2048]{1,0:T(8,128)(2,1)S(1)} %get-tuple-element.31), channel_id=1, source_target_pairs={{0,32},{32,0},{1,33},{33,1},{2,34},{34,2},{3,35},{35,3},{4,36},{36... | collective-permute-start | bytes 786440 | tf_op jit(solution)/shard_map/ppermute | solution.py:47
  237.1 1.9 collective-permute-start.8
  239.0 5.3 %collective-permute-start.9 = (bf16[64,2048]{1,0:T(8,128)(2,1)S(1)}, bf16[64,2048]{1,0:T(8,128)(2,1)S(1)}, u32[]{:S(2)}, u32[]{:S(2)}) collective-permute-start(bf16[64,2048]{1,0:T(8,128)(2,1)S(1)} %get-tuple-element.32), channel_id=1, source_target_pairs={{0,80},{16,64},{64,16},{80,0},{1,81},{17,65},{65,17},{81,1},{2,82}... | collective-permute-start | bytes 786440 | tf_op jit(solution)/shard_map/ppermute | solution.py:47
  244.2 1.2 all-to-all-done.2
  245.5 0.3 reshape.140
  245.8 0.3 fusion.18
  246.1 2.7 %collective-permute-done.7 = bf16[64,2048]{1,0:T(8,128)(2,1)S(1)} collective-permute-done((bf16[64,2048]{1,0:T(8,128)(2,1)S(1)}, bf16[64,2048]{1,0:T(8,128)(2,1)S(1)}, u32[]{:S(2)}, u32[]{:S(2)}) %collective-permute-start.7) | collective-permute-done | bytes 262176 | tf_op jit(solution)/shard_map/ppermute | solution.py:47
  248.8 10.3 %collective-permute-done.8 = bf16[64,2048]{1,0:T(8,128)(2,1)S(1)} collective-permute-done((bf16[64,2048]{1,0:T(8,128)(2,1)S(1)}, bf16[64,2048]{1,0:T(8,128)(2,1)S(1)}, u32[]{:S(2)}, u32[]{:S(2)}) %collective-permute-start.8) | collective-permute-done | bytes 262176 | tf_op jit(solution)/shard_map/ppermute | solution.py:47
  259.1 2.1 collective-permute-done.9
  261.2 1.0 add_convert_fusion
  (31 shorter events, 2.0 us)
Async XLA Ops:
  3.5 16.8 %collective-permute-start = (bf16[64,2176]{1,0:T(8,128)(2,1)S(1)}, bf16[64,2176]{1,0:T(8,128)(2,1)S(1)}, u32[]{:S(2)}, u32[]{:S(2)}) collective-permute-start(bf16[64,2176]{1,0:T(8,128)(2,1)S(1)} %pad_maximum_fusion.1.refs_0_), channel_id=1, source_target_pairs={{0,32},{32,0},{1,33},{33,1},{2,34},{34,2},{3,35},{35,3},{4,36},{36... | collective-permute-start | bytes 835592 | tf_op jit(solution)/shard_map/ppermute | solution.py:47
  8.6 12.7 %collective-permute-start.1 = (bf16[64,2176]{1,0:T(8,128)(2,1)S(1)}, bf16[64,2176]{1,0:T(8,128)(2,1)S(1)}, u32[]{:S(2)}, u32[]{:S(2)}) collective-permute-start(bf16[64,2176]{1,0:T(8,128)(2,1)S(1)} %pad_maximum_fusion.1.refs_0_), channel_id=1, source_target_pairs={{0,112},{16,96},{32,80},{48,64},{64,48},{80,32},{96,16},{112,0},{1... | collective-permute-start | bytes 835592 | tf_op jit(solution)/shard_map/ppermute | solution.py:47
  13.2 22.9 %collective-permute-start.2 = (bf16[64,2176]{1,0:T(8,128)(2,1)S(1)}, bf16[64,2176]{1,0:T(8,128)(2,1)S(1)}, u32[]{:S(2)}, u32[]{:S(2)}) collective-permute-start(bf16[64,2176]{1,0:T(8,128)(2,1)S(1)} %pad_maximum_fusion.1.refs_0_), channel_id=1, source_target_pairs={{0,80},{16,64},{64,16},{80,0},{1,81},{17,65},{65,17},{81,1},{2,82}... | collective-permute-start | bytes 835592 | tf_op jit(solution)/shard_map/ppermute | solution.py:47
  36.1 57.3 %collective-permute-start.3 = (bf16[576,2048]{1,0:T(8,128)(2,1)S(1)}, bf16[576,2048]{1,0:T(8,128)(2,1)}, u32[]{:S(2)}, u32[]{:S(2)}) collective-permute-start(bf16[576,2048]{1,0:T(8,128)(2,1)S(1)} %pad_maximum_fusion), channel_id=1, source_target_pairs={{32,17},{48,1},{17,32},{1,48},{0,16},{16,0},{33,49},{49,33},{34,19... | collective-permute-start | bytes 7077896 | tf_op jit(solution)/shard_map/ppermute | solution.py:204
  46.6 86.3 %all-to-all-start = ((bf16[32,24,2048]{2,1,0:T(8,128)(2,1)}), bf16[32,24,2048]{2,1,0:T(8,128)(2,1)}, u32[]{:S(2)}, u32[]{:S(2)}) async-start(bf16[32,24,2048]{2,1,0:T(8,128)(2,1)} %bitcast.6), calls=%async_computation | async-start | bytes 6291456 | tf_op jit(solution)/shard_map/all_to_all | solution.py:223
  93.4 30.2 %collective-permute-start.4 = (bf16[576,2048]{1,0:T(8,128)(2,1)}, bf16[576,2048]{1,0:T(8,128)(2,1)}, u32[]{:S(2)}, u32[]{:S(2)}) collective-permute-start(bf16[576,2048]{1,0:T(8,128)(2,1)} %collective-permute-done.3.refs_0_), channel_id=1, source_target_pairs={{1,17},{17,1},{32,48},{48,32},{3,19},{19,3},{34,50},{50,34},{5,21}... | collective-permute-start | bytes 7077896 | tf_op jit(solution)/shard_map/ppermute | solution.py:205
  96.4 32.4 %collective-permute-start.5 = (bf16[576,2048]{1,0:T(8,128)(2,1)}, bf16[576,2048]{1,0:T(8,128)(2,1)}, u32[]{:S(2)}, u32[]{:S(2)}) collective-permute-start(bf16[576,2048]{1,0:T(8,128)(2,1)} %collective-permute-done.3.refs_0_), channel_id=1, source_target_pairs={{0,1},{1,0},{2,3},{3,2},{4,5},{5,4},{6,7},{7,6},{8,9},{9,8},{10,11... | collective-permute-start | bytes 7077896 | tf_op jit(solution)/shard_map/ppermute | solution.py:47
  126.9 6.6 %collective-permute-start.6 = (bf16[576,2048]{1,0:T(8,128)(2,1)}, bf16[576,2048]{1,0:T(8,128)(2,1)S(1)}, u32[]{:S(2)}, u32[]{:S(2)}) collective-permute-start(bf16[576,2048]{1,0:T(8,128)(2,1)} %broadcast_select_fusion.refs_1_), channel_id=1, source_target_pairs={{0,1},{1,0},{2,3},{3,2},{4,5},{5,4},{6,7},{7,6},{8,9},{9,8},{10,11... | collective-permute-start | bytes 7077896 | tf_op jit(solution)/shard_map/ppermute | solution.py:47
  133.6 1.4 copy-start.3
  149.5 13.3 %copy-start.1 = (f32[256,8]{1,0:T(8,128)S(1)}, f32[256,8]{1,0:T(8,128)}, u32[]{:S(2)}) copy-start(f32[256,8]{1,0:T(8,128)} %get-tuple-element.35) | copy-start | bytes 24580
  149.5 67.5 %all-to-all-start.1 = ((bf16[32,288,128]{2,1,0:T(8,128)(2,1)}), bf16[32,288,128]{2,1,0:T(8,128)(2,1)S(1)}, u32[]{:S(2)}, u32[]{:S(2)}) async-start(bf16[32,288,128]{2,1,0:T(8,128)(2,1)} %get-tuple-element.25), calls=%async_computation.1 | async-start | bytes 4718592 | tf_op jit(solution)/shard_map/all_to_all | solution.py:223
  217.0 1.4 copy-start
  218.5 27.0 %all-to-all-start.2 = ((bf16[32,96,128]{2,1,0:T(8,128)(2,1)}), bf16[32,96,128]{2,1,0:T(8,128)(2,1)S(1)}, u32[]{:S(2)}, u32[]{:S(2)}) async-start(bf16[32,96,128]{2,1,0:T(8,128)(2,1)} %get-tuple-element.26), calls=%async_computation.2 | async-start | bytes 1572864 | tf_op jit(solution)/shard_map/all_to_all | solution.py:223
  232.8 13.1 %copy-start.2 = (bf16[192,64]{1,0:T(8,128)(2,1)S(1)}, bf16[192,64]{1,0:T(8,128)(2,1)}, u32[]{:S(2)}) copy-start(bf16[192,64]{1,0:T(8,128)(2,1)} %reshape.134) | copy-start | bytes 73732
  232.8 16.0 %collective-permute-start.7 = (bf16[64,2048]{1,0:T(8,128)(2,1)S(1)}, bf16[64,2048]{1,0:T(8,128)(2,1)S(1)}, u32[]{:S(2)}, u32[]{:S(2)}) collective-permute-start(bf16[64,2048]{1,0:T(8,128)(2,1)S(1)} %get-tuple-element.31), channel_id=1, source_target_pairs={{0,32},{32,0},{1,33},{33,1},{2,34},{34,2},{3,35},{35,3},{4,36},{36... | collective-permute-start | bytes 786440 | tf_op jit(solution)/shard_map/ppermute | solution.py:47
  237.1 22.1 %collective-permute-start.8 = (bf16[64,2048]{1,0:T(8,128)(2,1)S(1)}, bf16[64,2048]{1,0:T(8,128)(2,1)S(1)}, u32[]{:S(2)}, u32[]{:S(2)}) collective-permute-start(bf16[64,2048]{1,0:T(8,128)(2,1)S(1)} %get-tuple-element.33), channel_id=1, source_target_pairs={{0,112},{16,96},{32,80},{48,64},{64,48},{80,32},{96,16},{112,0},{1... | collective-permute-start | bytes 786440 | tf_op jit(solution)/shard_map/ppermute | solution.py:47
  239.0 22.2 %collective-permute-start.9 = (bf16[64,2048]{1,0:T(8,128)(2,1)S(1)}, bf16[64,2048]{1,0:T(8,128)(2,1)S(1)}, u32[]{:S(2)}, u32[]{:S(2)}) collective-permute-start(bf16[64,2048]{1,0:T(8,128)(2,1)S(1)} %get-tuple-element.32), channel_id=1, source_target_pairs={{0,80},{16,64},{64,16},{80,0},{1,81},{17,65},{65,17},{81,1},{2,82}... | collective-permute-start | bytes 786440 | tf_op jit(solution)/shard_map/ppermute | solution.py:47

commit v5 on v4

--- a/solution.py
+++ b/solution.py
@@ -13,6 +13,7 @@
 EXTRA = 128
 LANES = 128
 WIDE = 256
+TOP = 8
 SPLIT = 4
 
 
@@ -144,31 +145,92 @@
     )(rows, *pieces)
 
 
-def pick_kernel(hit_ref, *refs):
+def pick_kernel(where_ref, *refs):
     sources, out_ref = refs[:-1], refs[-1]
-    rows = jnp.concatenate([source[...] for source in sources], axis=0)
-    out_ref[...] = jnp.dot(hit_ref[...], rows, preferred_element_type=jnp.float32).astype(
-        jnp.bfloat16
-    )
-
-
-def pick_rows(hit, sources, width):
-    count, tokens = hit.shape
-    tile = 256
-    whole = pl.BlockSpec((tokens // len(sources), width), lambda i: (0, 0))
+    width = out_ref.shape[1]
+    records = jnp.concatenate([source[...] for source in sources], axis=0)
+    named = records[:, width:].astype(jnp.float32).T
+    tokens = records.shape[0]
+    count = tokens // len(sources)
+    share = CHUNKS * MOST
+    experts = out_ref.shape[0] // share
+    target = pl.program_id(0) * experts + lax.broadcasted_iota(jnp.int32, (experts, tokens), 0)
+    zs = SIZES[4]
+    expert = (2 * (target % zs) + where_ref[0]) * 8 + 2 * (target // zs) + where_ref[1]
+    expert = expert.astype(jnp.float32)
+    chosen = jnp.zeros((experts, tokens), jnp.float32)
+    for k in range(TOP):
+        chosen = jnp.where(named[k : k + 1, :] == expert, 1.0, chosen)
+    row = lax.broadcasted_iota(jnp.int32, (tokens, tokens), 0)
+    column = lax.broadcasted_iota(jnp.int32, (tokens, tokens), 1)
+    before = jnp.where((row // count == column // count) & (row < column), 1.0, 0.0)
+    rank = jnp.dot(
+        chosen.astype(jnp.bfloat16), before.astype(jnp.bfloat16), preferred_element_type=jnp.float32
+    )
+    chunk = lax.broadcasted_iota(jnp.int32, (experts, tokens), 1) // count
+    slot = jnp.where(chosen > 0.0, rank.astype(jnp.int32) + chunk * MOST, -1)
+    slots = lax.broadcasted_iota(jnp.int32, (experts, share, tokens), 1)
+    hit = jnp.where(slot[:, None, :] == slots, 1.0, 0.0).reshape(experts * share, tokens)
+    out_ref[...] = jnp.dot(
+        hit.astype(jnp.bfloat16), records[:, :width], preferred_element_type=jnp.float32
+    ).astype(jnp.bfloat16)
+
+
+def pick_rows(where, sources, width):
+    tokens = len(sources) * sources[0].shape[0]
+    count = PLANE * CHUNKS * MOST
+    steps = SIZES[0]
+    whole = pl.BlockSpec(sources[0].shape, lambda i: (0, 0))
     return pl.pallas_call(
         pick_kernel,
-        grid=(count // tile,),
+        grid=(steps,),
         out_shape=jax.ShapeDtypeStruct((count, width), jnp.bfloat16),
-        in_specs=[pl.BlockSpec((tile, tokens), lambda i: (i, 0))] + [whole] * len(sources),
-        out_specs=pl.BlockSpec((tile, width), lambda i: (i, 0)),
-        compiler_params=pltpu.CompilerParams(vmem_limit_bytes=16 * 1024 * 1024),
+        in_specs=[pl.BlockSpec(memory_space=pltpu.SMEM)] + [whole] * len(sources),
+        out_specs=pl.BlockSpec((count // steps, width), lambda i: (i, 0)),
+        compiler_params=pltpu.CompilerParams(vmem_limit_bytes=20 * 1024 * 1024),
         cost_estimate=pl.CostEstimate(
             flops=2 * count * tokens * width,
             bytes_accessed=2 * (count + tokens) * (width + tokens),
             transcendentals=0,
         ),
-    )(hit, *sources)
+    )(where, *sources)
+
+
+def sum_kernel(returned_ref, spread_ref, *refs):
+    outs, (lined, rows) = refs[:-2], refs[-2:]
+    count, width = rows.shape
+    lines = width // LANES
+    lined[...] = returned_ref[...].astype(jnp.float32)
+    for n in range(lines):
+        part = slice(n * LANES, (n + 1) * LANES)
+        rows[:, part] = lined[pl.ds(n, count, stride=lines), :].astype(jnp.bfloat16)
+    total = lax.dot_general(
+        spread_ref[...], rows[...], (((0,), (0,)), ((), ())), preferred_element_type=jnp.float32
+    )
+    half = total.shape[0] // 2
+    total = total[:half] + total[half:]
+    tokens = outs[0].shape[0]
+    for k, out in enumerate(outs):
+        out[...] = total[k * tokens : (k + 1) * tokens].astype(jnp.bfloat16)
+
+
+def sum_rows(returned, spread, planes, width):
+    count = spread.shape[0]
+    tokens = spread.shape[1] // 2 // planes
+    return pl.pallas_call(
+        sum_kernel,
+        out_shape=[jax.ShapeDtypeStruct((tokens, width), jnp.bfloat16)] * planes,
+        scratch_shapes=[
+            pltpu.VMEM((count * width // LANES, LANES), jnp.float32),
+            pltpu.VMEM((count, width), jnp.bfloat16),
+        ],
+        compiler_params=pltpu.CompilerParams(vmem_limit_bytes=24 * 1024 * 1024),
+        cost_estimate=pl.CostEstimate(
+            flops=2 * count * spread.shape[1] * width,
+            bytes_accessed=2 * count * width,
+            transcendentals=0,
+        ),
+    )(returned, spread)
 
 
 def matches(named, experts):
@@ -199,7 +261,7 @@
     received = [swap(record, axes) for axes in PARTNERS]
 
     own = jnp.concatenate([gate_weight[0, 0], up_weight[0, 0], down_weight[0, 0]], axis=0)
-    own, received = lax.optimization_barrier((own, received))
+    own, received[0], received[2] = lax.optimization_barrier((own, received[0], received[2]))
     axes = ("p", "b", "c")
     first = lax.ppermute(own, axes, FIRST)
     second = jnp.where(c == p, own, lax.ppermute(first, axes, SECOND))
@@ -216,8 +278,8 @@
     chunk = jnp.arange(CHUNKS * count, dtype=jnp.int32) // count
     slot = jnp.where(chosen, ranks(chosen, count) + (chunk * MOST)[:, None], -1).T
     slots = jnp.arange(CHUNKS * MOST, dtype=jnp.int32)
-    hit = (slot[:, None, :] == slots[None, :, None]).reshape(PLANE * CHUNKS * MOST, CHUNKS * count)
-    sent = pick_rows(hit.astype(jnp.bfloat16), records, width)
+    where = jnp.stack([p, h]).astype(jnp.int32)
+    sent = pick_rows(where, records, width)
 
     def exchange(rows):
         return lax.all_to_all(rows, ("x", "z"), 0, 0, tiled=True)
@@ -230,30 +292,21 @@
     )
     upper = spread.astype(jnp.bfloat16)
     lower = (spread - upper.astype(jnp.float32)).astype(jnp.bfloat16)
-    halves = [
-        [
-            half[:, :MOST, :count].reshape(-1, count),
-            half[:, MOST:, count:].reshape(-1, (CHUNKS - 1) * count),
-        ]
-        for half in (upper, lower)
-    ]
-    halves, own_out = lax.optimization_barrier((halves, own_out))
-
-    def combine(returned, k):
-        returned = returned.reshape(-1, width)
-        dims = (((0,), (0,)), ((), ()))
-        return lax.dot_general(
-            halves[0][k], returned, dims, preferred_element_type=jnp.float32
-        ) + lax.dot_general(halves[1][k], returned, dims, preferred_element_type=jnp.float32)
+    own_spread = [half[:, :MOST, :count].reshape(-1, count) for half in (upper, lower)]
+    far_spread = jnp.concatenate([half[:, MOST:, count:] for half in (upper, lower)], axis=2)
+    far_spread = far_spread.reshape(-1, 2 * (CHUNKS - 1) * count)
+    own_spread, far_spread, own_out = lax.optimization_barrier((own_spread, far_spread, own_out))
 
     far_back = exchange(far_out)
     own_out, far_back = lax.optimization_barrier((own_out, far_back))
-    own_back = exchange(own_out)
-    far = combine(far_back, 1).astype(jnp.bfloat16)
-    gained = [
-        swap(far[k * count : (k + 1) * count], names) for k, names in enumerate(PARTNERS)
-    ]
-    mixed = combine(own_back, 0)
+    own_back = exchange(own_out).reshape(-1, width)
+    far = sum_rows(far_back.reshape(-1, LANES), far_spread, CHUNKS - 1, width)
+    gained = [swap(part, names) for part, names in zip(far, PARTNERS)]
+    dims = (((0,), (0,)), ((), ()))
+    mixed = sum(
+        lax.dot_general(half, own_back, dims, preferred_element_type=jnp.float32)
+        for half in own_spread
+    )
     for part in gained:
         mixed = mixed + part.astype(jnp.float32)
     return mixed.astype(jnp.bfloat16)

time: 266 us -> 305 us (1.15)
  starting transfers between devices: 69.7 us -> 112 us
  local copies, waits for them, and re-layouts: 12.8 us -> 4.15 us
  Pallas kernels: 17.6 us -> 22 us
    ppermute x8, starting transfers between devices: 27.4 us -> 57.6 us  [swap(): return lax.ppermute(value, axes, flips(axes))]
    ppermute x1, starting transfers between devices: 3.02 us -> 19.5 us  [shards(): second = jnp.where(c == p, own, lax.ppermute(first, axes, SECOND))]
    ppermute x8, waiting for transfers between devices: 34.4 us -> 46.9 us  [swap(): return lax.ppermute(value, axes, flips(axes))]
    ppermute x1, waiting for transfers between devices: 33.8 us -> 27.1 us  [shards(): first = lax.ppermute(own, axes, FIRST)]
    all_to_all x3, waiting for transfers between devices: 55.2 us -> 50.3 us  [exchange(): return lax.all_to_all(rows, ('x', 'z'), 0, 0, tiled=True)]
    pallas_call x1 -> x2, Pallas kernels: 3 us -> 7.42 us  [the longest x1 4.07 us: pick_rows(): pl.pallas_call(pick_kernel, grid=(steps,), out_shape=jax.ShapeDtypeStruct...]
    all_to_all x3, starting transfers between devices: 34.3 us -> 30.2 us  [exchange(): return lax.all_to_all(rows, ('x', 'z'), 0, 0, tiled=True)]
    reshape x4 -> x2, local copies, waits for them, and re-layouts: 4.98 us -> 1.57 us  [the longest x1 1.43 us: shards(): own_back = exchange(own_out).reshape(-1, width)]
  transfers between devices with their start and end apart: 13 -> 13, of which waited for: 12 -> 9; matrix products, arithmetic and copies ran while one was open for 7% -> 4% of each run, Pallas kernels for 1% -> 2%
where the time goes in v5:
time: 305 us; the launch traced here: 299 us
  waiting for transfers between devices  149 us (49%)
  starting transfers between devices  112 us (37%)
  Pallas kernels  22 us (7%)
  other arithmetic  9.75 us (3%)
  local copies, waits for them, and re-layouts  4.15 us (1%)
    ppermute x8, starting transfers between devices, swap(): return lax.ppermute(value, axes, flips(axes))  57.6 us
    all_to_all x3, waiting for transfers between devices, exchange(): return lax.all_to_all(rows, ('x', 'z'), 0, 0, tiled=True)  50.3 us
    ppermute x8, waiting for transfers between devices, swap(): return lax.ppermute(value, axes, flips(axes))  46.9 us
    all_to_all x3, starting transfers between devices, exchange(): return lax.all_to_all(rows, ('x', 'z'), 0, 0, tiled=True)  30.2 us
    ppermute x1, waiting for transfers between devices, shards(): first = lax.ppermute(own, axes, FIRST)  27.1 us
    ppermute x1, waiting for transfers between devices, shards(): second = jnp.where(c == p, own, lax.ppermute(first, axes, SECOND))  24.9 us
    ppermute x1, starting transfers between devices, shards(): second = jnp.where(c == p, own, lax.ppermute(first, axes, SECOND))  19.5 us
    pallas_call x1, Pallas kernels, run_expert(): pl.pallas_call(expert_kernel, out_shape=[jax.ShapeDtypeStruct((PLANE, n,...  14.5 us
  transfers between devices with their start and end apart: 13, of which 9 were waited for; matrix products, arithmetic and copies ran while one was open for 4% of the time, Pallas kernels for 2%

profile of v5, /device:TPU:1, one launch (start us, length us, event | category | flops | bytes accessed | tf_op | source)
XLA Modules:
  0.0 299.3 jit_solution(16556115249681452951)
XLA Ops:
  0.0 0.7 convert_element_type.52
  0.7 0.1 copy.19
  0.8 0.1 copy.21
  0.9 0.8 copy.20
  1.7 0.7 convert_element_type.51
  2.3 0.1 copy.18
  2.5 0.1 pad_add_fusion
  2.5 1.0 pad_maximum_fusion.2.refs_0_
  3.5 7.5 %collective-permute-start.1 = (bf16[64,2176]{1,0:T(8,128)(2,1)S(1)}, bf16[64,2176]{1,0:T(8,128)(2,1)S(1)}, u32[]{:S(2)}, u32[]{:S(2)}) collective-permute-start(bf16[64,2176]{1,0:T(8,128)(2,1)S(1)} %pad_maximum_fusion.2.refs_0_), channel_id=1, source_target_pairs={{0,80},{16,64},{64,16},{80,0},{1,81},{17,65},{65,17},{81,1},{2,82}... | collective-permute-start | bytes 835592 | tf_op jit(solution)/shard_map/ppermute | solution.py:48
  11.0 2.4 collective-permute-start
  13.5 3.4 %pad_maximum_fusion = bf16[576,2048]{1,0:T(8,128)(2,1)} fusion(bf16[192,2048]{1,0:T(8,128)(2,1)} %bitcast.17, bf16[192,2048]{1,0:T(8,128)(2,1)} %bitcast.18, bf16[192,2048]{1,0:T(8,128)(2,1)} %bitcast.19), kind=kLoop, calls=%fused_computation | loop fusion | flops 7077888 | bytes 4718592 | tf_op jit(solution)/shard_map/concatenate | solution.py:263
  16.9 2.1 collective-permute-done.1.refs_3_
  19.0 17.3 %collective-permute-done.refs_1_ = bf16[64,2176]{1,0:T(8,128)(2,1)S(1)} collective-permute-done((bf16[64,2176]{1,0:T(8,128)(2,1)S(1)}, bf16[64,2176]{1,0:T(8,128)(2,1)S(1)}, u32[]{:S(2)}, u32[]{:S(2)}) %collective-permute-start) | collective-permute-done | bytes 278560 | tf_op jit(solution)/shard_map/ppermute | solution.py:48
  36.2 5.1 %collective-permute-start.3 = (bf16[576,2048]{1,0:T(8,128)(2,1)}, bf16[576,2048]{1,0:T(8,128)(2,1)}, u32[]{:S(2)}, u32[]{:S(2)}) collective-permute-start(bf16[576,2048]{1,0:T(8,128)(2,1)} %pad_maximum_fusion), channel_id=1, source_target_pairs={{32,17},{48,1},{17,32},{1,48},{0,16},{16,0},{33,49},{49,33},{34,19... | collective-permute-start | bytes 7077896 | tf_op jit(solution)/shard_map/ppermute | solution.py:266
  41.3 1.9 collective-permute-start.2
  43.3 9.0 %collective-permute-done.2.refs_2_ = bf16[64,2176]{1,0:T(8,128)(2,1)S(1)} collective-permute-done((bf16[64,2176]{1,0:T(8,128)(2,1)S(1)}, bf16[64,2176]{1,0:T(8,128)(2,1)S(1)}, u32[]{:S(2)}, u32[]{:S(2)}) %collective-permute-start.2) | collective-permute-done | bytes 278560 | tf_op jit(solution)/shard_map/ppermute | solution.py:48
  52.3 4.1 %shard_map.64 = bf16[768,2048]{1,0:T(8,128)(2,1)} custom-call(s32[2]{0:T(128)S(1)} %pad_add_fusion.1.where_ref, bf16[64,2176]{1,0:T(8,128)(2,1)S(1)} %pad_maximum_fusion.2.refs_0_, bf16[64,2176]{1,0:T(8,128)(2,1)S(1)} %collective-permute-done.refs_1_, bf16[64,2176]{1,0:T(8,128)(2,1)S(1)} %collective-permute-done.2.refs_2_, ...), custom_call_target="tpu_custom_call" | custom-call | flops 805306368 | bytes 4718592 | tf_op jit(solution)/shard_map/pallas_call | solution.py:184
  56.3 13.0 %all-to-all-start = ((bf16[32,24,2048]{2,1,0:T(8,128)(2,1)}), bf16[32,24,2048]{2,1,0:T(8,128)(2,1)}, u32[]{:S(2)}, u32[]{:S(2)}) async-start(bf16[32,24,2048]{2,1,0:T(8,128)(2,1)} %bitcast.7), calls=%async_computation | async-start | bytes 6291456 | tf_op jit(solution)/shard_map/all_to_all | solution.py:285
  69.3 27.1 %collective-permute-done.3.refs_0_ = bf16[576,2048]{1,0:T(8,128)(2,1)} collective-permute-done((bf16[576,2048]{1,0:T(8,128)(2,1)}, bf16[576,2048]{1,0:T(8,128)(2,1)}, u32[]{:S(2)}, u32[]{:S(2)}) %collective-permute-start.3) | collective-permute-done | bytes 2359328 | tf_op jit(solution)/shard_map/ppermute | solution.py:266
  96.5 19.5 %collective-permute-start.4 = (bf16[576,2048]{1,0:T(8,128)(2,1)}, bf16[576,2048]{1,0:T(8,128)(2,1)}, u32[]{:S(2)}, u32[]{:S(2)}) collective-permute-start(bf16[576,2048]{1,0:T(8,128)(2,1)} %collective-permute-done.3.refs_0_), channel_id=1, source_target_pairs={{1,17},{17,1},{32,48},{48,32},{3,19},{19,3},{34,50},{50,34},{5,21}... | collective-permute-start | bytes 7077896 | tf_op jit(solution)/shard_map/ppermute | solution.py:267
  115.9 1.9 collective-permute-start.5
  117.9 24.9 %collective-permute-done.4 = bf16[576,2048]{1,0:T(8,128)(2,1)} collective-permute-done((bf16[576,2048]{1,0:T(8,128)(2,1)}, bf16[576,2048]{1,0:T(8,128)(2,1)}, u32[]{:S(2)}, u32[]{:S(2)}) %collective-permute-start.4) | collective-permute-done | bytes 2359328 | tf_op jit(solution)/shard_map/ppermute | solution.py:267
  142.8 1.9 broadcast_select_fusion.refs_1_
  144.7 1.9 collective-permute-start.6
  146.6 4.6 %collective-permute-done.6.refs_3_ = bf16[576,2048]{1,0:T(8,128)(2,1)} collective-permute-done((bf16[576,2048]{1,0:T(8,128)(2,1)S(1)}, bf16[576,2048]{1,0:T(8,128)(2,1)}, u32[]{:S(2)}, u32[]{:S(2)}) %collective-permute-start.6) | collective-permute-done | bytes 2359328 | tf_op jit(solution)/shard_map/ppermute | solution.py:48
  151.3 14.5 %shard_map.65 = (bf16[32,96,128]{2,1,0:T(8,128)(2,1)}, bf16[32,288,128]{2,1,0:T(8,128)(2,1)}) custom-call(bf16[768,2048]{1,0:T(8,128)(2,1)} %bitcast.8.rows_ref, bf16[576,2048]{1,0:T(8,128)(2,1)} %collective-permute-done.3.refs_0_, bf16[576,2048]{1,0:T(8,128)(2,1)} %copy-done, bf16[576,2048]{1,0:T(8,128)(2,1)} %collective-permute-done.5.refs_2_, ...), custom_call_target="tpu_custom_call" | custom-call | flops 7247757312 | bytes 15728640 | tf_op jit(solution)/shard_map/pallas_call | solution.py:123
  165.8 9.1 %all-to-all-start.1 = ((bf16[32,288,128]{2,1,0:T(8,128)(2,1)}), bf16[32,288,128]{2,1,0:T(8,128)(2,1)S(1)}, u32[]{:S(2)}, u32[]{:S(2)}) async-start(bf16[32,288,128]{2,1,0:T(8,128)(2,1)} %get-tuple-element.25), calls=%async_computation.1 | async-start | bytes 4718592 | tf_op jit(solution)/shard_map/all_to_all | solution.py:285
  174.9 0.1 slice_convert_fusion
  175.2 0.1 compare_reduce_fusion
  175.3 0.1 fusion.3
  175.4 0.2 fusion.1
  175.7 0.2 fusion.2
  175.9 0.3 slice.47
  176.2 0.2 select_convert_fusion
  176.3 1.0 slice.46
  177.4 1.2 pad_maximum_fusion.1
  178.6 0.1 reshape.130.spread_ref
  178.8 50.3 %all-to-all-done.1 = bf16[32,288,128]{2,1,0:T(8,128)(2,1)S(1)} async-done(((bf16[32,288,128]{2,1,0:T(8,128)(2,1)}), bf16[32,288,128]{2,1,0:T(8,128)(2,1)S(1)}, u32[]{:S(2)}, u32[]{:S(2)}) %all-to-all-start.1) | async-done | bytes 2359328 | tf_op jit(solution)/shard_map/all_to_all | solution.py:285
  229.1 8.1 %all-to-all-start.2 = ((bf16[32,96,128]{2,1,0:T(8,128)(2,1)}), bf16[32,96,128]{2,1,0:T(8,128)(2,1)}, u32[]{:S(2)}, u32[]{:S(2)}) async-start(bf16[32,96,128]{2,1,0:T(8,128)(2,1)} %get-tuple-element.26), calls=%async_computation.2 | async-start | bytes 1572864 | tf_op jit(solution)/shard_map/all_to_all | solution.py:285
  237.2 3.3 %shard_map.66 = (bf16[64,2048]{1,0:T(8,128)(2,1)}, bf16[64,2048]{1,0:T(8,128)(2,1)S(1)}, bf16[64,2048]{1,0:T(8,128)(2,1)S(1)}) custom-call(bf16[9216,128]{1,0:T(8,128)(2,1)S(1)} %bitcast.16, bf16[576,384]{1,0:T(8,128)(2,1)S(1)} %reshape.130.spread_ref), custom_call_target="tpu_custom_call" | custom-call | flops 905969664 | bytes 2359296 | tf_op jit(solution)/shard_map/pallas_call | solution.py:220
  240.6 22.2 %collective-permute-start.7 = (bf16[64,2048]{1,0:T(8,128)(2,1)}, bf16[64,2048]{1,0:T(8,128)(2,1)S(1)}, u32[]{:S(2)}, u32[]{:S(2)}) collective-permute-start(bf16[64,2048]{1,0:T(8,128)(2,1)} %get-tuple-element.30), channel_id=1, source_target_pairs={{0,32},{32,0},{1,33},{33,1},{2,34},{34,2},{3,35},{35,3},{4,36},{36... | collective-permute-start | bytes 786440 | tf_op jit(solution)/shard_map/ppermute | solution.py:48
  262.8 17.8 %collective-permute-start.8 = (bf16[64,2048]{1,0:T(8,128)(2,1)S(1)}, bf16[64,2048]{1,0:T(8,128)(2,1)S(1)}, u32[]{:S(2)}, u32[]{:S(2)}) collective-permute-start(bf16[64,2048]{1,0:T(8,128)(2,1)S(1)} %get-tuple-element.31), channel_id=1, source_target_pairs={{0,112},{16,96},{32,80},{48,64},{64,48},{80,32},{96,16},{112,0},{1... | collective-permute-start | bytes 786440 | tf_op jit(solution)/shard_map/ppermute | solution.py:48
  280.6 1.9 collective-permute-start.9
  282.6 1.4 reshape.133
  284.0 0.3 fusion.15
  284.3 12.7 %collective-permute-done.8 = bf16[64,2048]{1,0:T(8,128)(2,1)S(1)} collective-permute-done((bf16[64,2048]{1,0:T(8,128)(2,1)S(1)}, bf16[64,2048]{1,0:T(8,128)(2,1)S(1)}, u32[]{:S(2)}, u32[]{:S(2)}) %collective-permute-start.8) | collective-permute-done | bytes 262176 | tf_op jit(solution)/shard_map/ppermute | solution.py:48
  297.0 1.3 collective-permute-done.9
  298.3 1.0 add_convert_fusion
  (20 shorter events, 0.3 us)
Async XLA Ops:
  3.5 15.4 %collective-permute-start.1 = (bf16[64,2176]{1,0:T(8,128)(2,1)S(1)}, bf16[64,2176]{1,0:T(8,128)(2,1)S(1)}, u32[]{:S(2)}, u32[]{:S(2)}) collective-permute-start(bf16[64,2176]{1,0:T(8,128)(2,1)S(1)} %pad_maximum_fusion.2.refs_0_), channel_id=1, source_target_pairs={{0,80},{16,64},{64,16},{80,0},{1,81},{17,65},{65,17},{81,1},{2,82}... | collective-permute-start | bytes 835592 | tf_op jit(solution)/shard_map/ppermute | solution.py:48
  11.0 25.2 %collective-permute-start = (bf16[64,2176]{1,0:T(8,128)(2,1)S(1)}, bf16[64,2176]{1,0:T(8,128)(2,1)S(1)}, u32[]{:S(2)}, u32[]{:S(2)}) collective-permute-start(bf16[64,2176]{1,0:T(8,128)(2,1)S(1)} %pad_maximum_fusion.2.refs_0_), channel_id=1, source_target_pairs={{0,32},{32,0},{1,33},{33,1},{2,34},{34,2},{3,35},{35,3},{4,36},{36... | collective-permute-start | bytes 835592 | tf_op jit(solution)/shard_map/ppermute | solution.py:48
  36.2 60.2 %collective-permute-start.3 = (bf16[576,2048]{1,0:T(8,128)(2,1)}, bf16[576,2048]{1,0:T(8,128)(2,1)}, u32[]{:S(2)}, u32[]{:S(2)}) collective-permute-start(bf16[576,2048]{1,0:T(8,128)(2,1)} %pad_maximum_fusion), channel_id=1, source_target_pairs={{32,17},{48,1},{17,32},{1,48},{0,16},{16,0},{33,49},{49,33},{34,19... | collective-permute-start | bytes 7077896 | tf_op jit(solution)/shard_map/ppermute | solution.py:266
  41.3 11.0 %collective-permute-start.2 = (bf16[64,2176]{1,0:T(8,128)(2,1)S(1)}, bf16[64,2176]{1,0:T(8,128)(2,1)S(1)}, u32[]{:S(2)}, u32[]{:S(2)}) collective-permute-start(bf16[64,2176]{1,0:T(8,128)(2,1)S(1)} %pad_maximum_fusion.2.refs_0_), channel_id=1, source_target_pairs={{0,112},{16,96},{32,80},{48,64},{64,48},{80,32},{96,16},{112,0},{1... | collective-permute-start | bytes 835592 | tf_op jit(solution)/shard_map/ppermute | solution.py:48
  56.3 90.3 %all-to-all-start = ((bf16[32,24,2048]{2,1,0:T(8,128)(2,1)}), bf16[32,24,2048]{2,1,0:T(8,128)(2,1)}, u32[]{:S(2)}, u32[]{:S(2)}) async-start(bf16[32,24,2048]{2,1,0:T(8,128)(2,1)} %bitcast.7), calls=%async_computation | async-start | bytes 6291456 | tf_op jit(solution)/shard_map/all_to_all | solution.py:285
  96.5 46.3 %collective-permute-start.4 = (bf16[576,2048]{1,0:T(8,128)(2,1)}, bf16[576,2048]{1,0:T(8,128)(2,1)}, u32[]{:S(2)}, u32[]{:S(2)}) collective-permute-start(bf16[576,2048]{1,0:T(8,128)(2,1)} %collective-permute-done.3.refs_0_), channel_id=1, source_target_pairs={{1,17},{17,1},{32,48},{48,32},{3,19},{19,3},{34,50},{50,34},{5,21}... | collective-permute-start | bytes 7077896 | tf_op jit(solution)/shard_map/ppermute | solution.py:267
  115.9 30.7 %collective-permute-start.5 = (bf16[576,2048]{1,0:T(8,128)(2,1)}, bf16[576,2048]{1,0:T(8,128)(2,1)}, u32[]{:S(2)}, u32[]{:S(2)}) collective-permute-start(bf16[576,2048]{1,0:T(8,128)(2,1)} %collective-permute-done.3.refs_0_), channel_id=1, source_target_pairs={{0,1},{1,0},{2,3},{3,2},{4,5},{5,4},{6,7},{7,6},{8,9},{9,8},{10,11... | collective-permute-start | bytes 7077896 | tf_op jit(solution)/shard_map/ppermute | solution.py:48
  144.7 6.6 %copy-start = (bf16[576,2048]{1,0:T(8,128)(2,1)}, bf16[576,2048]{1,0:T(8,128)(2,1)S(1)}, u32[]{:S(2)}) copy-start(bf16[576,2048]{1,0:T(8,128)(2,1)S(1)} %broadcast_select_fusion.refs_1_) | copy-start | bytes 7077892
  144.7 6.6 %collective-permute-start.6 = (bf16[576,2048]{1,0:T(8,128)(2,1)S(1)}, bf16[576,2048]{1,0:T(8,128)(2,1)}, u32[]{:S(2)}, u32[]{:S(2)}) collective-permute-start(bf16[576,2048]{1,0:T(8,128)(2,1)S(1)} %broadcast_select_fusion.refs_1_), channel_id=1, source_target_pairs={{0,1},{1,0},{2,3},{3,2},{4,5},{5,4},{6,7},{7,6},{8,9},{9,8},{10,11... | collective-permute-start | bytes 7077896 | tf_op jit(solution)/shard_map/ppermute | solution.py:48
  165.8 63.3 %all-to-all-start.1 = ((bf16[32,288,128]{2,1,0:T(8,128)(2,1)}), bf16[32,288,128]{2,1,0:T(8,128)(2,1)S(1)}, u32[]{:S(2)}, u32[]{:S(2)}) async-start(bf16[32,288,128]{2,1,0:T(8,128)(2,1)} %get-tuple-element.25), calls=%async_computation.1 | async-start | bytes 4718592 | tf_op jit(solution)/shard_map/all_to_all | solution.py:285
  229.1 53.5 %all-to-all-start.2 = ((bf16[32,96,128]{2,1,0:T(8,128)(2,1)}), bf16[32,96,128]{2,1,0:T(8,128)(2,1)}, u32[]{:S(2)}, u32[]{:S(2)}) async-start(bf16[32,96,128]{2,1,0:T(8,128)(2,1)} %get-tuple-element.26), calls=%async_computation.2 | async-start | bytes 1572864 | tf_op jit(solution)/shard_map/all_to_all | solution.py:285
  240.6 43.7 %collective-permute-start.7 = (bf16[64,2048]{1,0:T(8,128)(2,1)}, bf16[64,2048]{1,0:T(8,128)(2,1)S(1)}, u32[]{:S(2)}, u32[]{:S(2)}) collective-permute-start(bf16[64,2048]{1,0:T(8,128)(2,1)} %get-tuple-element.30), channel_id=1, source_target_pairs={{0,32},{32,0},{1,33},{33,1},{2,34},{34,2},{3,35},{35,3},{4,36},{36... | collective-permute-start | bytes 786440 | tf_op jit(solution)/shard_map/ppermute | solution.py:48
  262.8 34.2 %collective-permute-start.8 = (bf16[64,2048]{1,0:T(8,128)(2,1)S(1)}, bf16[64,2048]{1,0:T(8,128)(2,1)S(1)}, u32[]{:S(2)}, u32[]{:S(2)}) collective-permute-start(bf16[64,2048]{1,0:T(8,128)(2,1)S(1)} %get-tuple-element.31), channel_id=1, source_target_pairs={{0,112},{16,96},{32,80},{48,64},{64,48},{80,32},{96,16},{112,0},{1... | collective-permute-start | bytes 786440 | tf_op jit(solution)/shard_map/ppermute | solution.py:48
  280.6 17.6 %collective-permute-start.9 = (bf16[64,2048]{1,0:T(8,128)(2,1)S(1)}, bf16[64,2048]{1,0:T(8,128)(2,1)S(1)}, u32[]{:S(2)}, u32[]{:S(2)}) collective-permute-start(bf16[64,2048]{1,0:T(8,128)(2,1)S(1)} %get-tuple-element.32), channel_id=1, source_target_pairs={{0,80},{16,64},{64,16},{80,0},{1,81},{17,65},{65,17},{81,1},{2,82}... | collective-permute-start | bytes 786440 | tf_op jit(solution)/shard_map/ppermute | solution.py:48

commit v6 on v5

--- a/solution.py
+++ b/solution.py
@@ -261,7 +261,7 @@
     received = [swap(record, axes) for axes in PARTNERS]
 
     own = jnp.concatenate([gate_weight[0, 0], up_weight[0, 0], down_weight[0, 0]], axis=0)
-    own, received[0], received[2] = lax.optimization_barrier((own, received[0], received[2]))
+    own, received = lax.optimization_barrier((own, received))
     axes = ("p", "b", "c")
     first = lax.ppermute(own, axes, FIRST)
     second = jnp.where(c == p, own, lax.ppermute(first, axes, SECOND))

time: 305 us -> 257 us (0.84)
  starting transfers between devices: 112 us -> 69.3 us
    ppermute x8, starting transfers between devices: 57.6 us -> 29.2 us  [swap(): return lax.ppermute(value, axes, flips(axes))]
    ppermute x8, waiting for transfers between devices: 46.9 us -> 28 us  [swap(): return lax.ppermute(value, axes, flips(axes))]
    ppermute x1, starting transfers between devices: 19.5 us -> 1.91 us  [shards(): second = jnp.where(c == p, own, lax.ppermute(first, axes, SECOND))]
    all_to_all x3, waiting for transfers between devices: 50.3 us -> 60.2 us  [exchange(): return lax.all_to_all(rows, ('x', 'z'), 0, 0, tiled=True)]
    ppermute x1, waiting for transfers between devices: 27.1 us -> 33.5 us  [shards(): first = lax.ppermute(own, axes, FIRST)]
  transfers between devices with their start and end apart: 13 -> 13, of which waited for: 9 -> 9; matrix products, arithmetic and copies ran while one was open for 4% -> 4% of each run, Pallas kernels for 2% -> 3%
where the time goes in v6:
time: 257 us; the launch traced here: 254 us
  waiting for transfers between devices  147 us (57%)
  starting transfers between devices  69.3 us (27%)
  Pallas kernels  22 us (9%)
  other arithmetic  9.75 us (4%)
  local copies, waits for them, and re-layouts  4.15 us (2%)
    all_to_all x3, waiting for transfers between devices, exchange(): return lax.all_to_all(rows, ('x', 'z'), 0, 0, tiled=True)  60.2 us
    ppermute x1, waiting for transfers between devices, shards(): first = lax.ppermute(own, axes, FIRST)  33.5 us
    all_to_all x3, starting transfers between devices, exchange(): return lax.all_to_all(rows, ('x', 'z'), 0, 0, tiled=True)  33.1 us
    ppermute x8, starting transfers between devices, swap(): return lax.ppermute(value, axes, flips(axes))  29.2 us
    ppermute x8, waiting for transfers between devices, swap(): return lax.ppermute(value, axes, flips(axes))  28 us
    ppermute x1, waiting for transfers between devices, shards(): second = jnp.where(c == p, own, lax.ppermute(first, axes, SECOND))  24.9 us
    pallas_call x1, Pallas kernels, run_expert(): pl.pallas_call(expert_kernel, out_shape=[jax.ShapeDtypeStruct((PLANE, n,...  14.5 us
  transfers between devices with their start and end apart: 13, of which 9 were waited for; matrix products, arithmetic and copies ran while one was open for 4% of the time, Pallas kernels for 3%

profile of v6, /device:TPU:1, one launch (start us, length us, event | category | flops | bytes accessed | tf_op | source)
XLA Modules:
  0.0 253.6 jit_solution(8848523716214480192)
XLA Ops:
  0.0 0.7 convert_element_type.52
  0.7 0.1 copy.19
  0.8 0.1 copy.21
  0.9 0.8 copy.20
  1.7 0.7 convert_element_type.51
  2.3 0.1 copy.18
  2.5 0.1 pad_add_fusion
  2.5 1.0 pad_maximum_fusion.2.refs_0_
  3.5 7.5 %collective-permute-start.2 = (bf16[64,2176]{1,0:T(8,128)(2,1)S(1)}, bf16[64,2176]{1,0:T(8,128)(2,1)S(1)}, u32[]{:S(2)}, u32[]{:S(2)}) collective-permute-start(bf16[64,2176]{1,0:T(8,128)(2,1)S(1)} %pad_maximum_fusion.2.refs_0_), channel_id=1, source_target_pairs={{0,80},{16,64},{64,16},{80,0},{1,81},{17,65},{65,17},{81,1},{2,82}... | collective-permute-start | bytes 835592 | tf_op jit(solution)/shard_map/ppermute | solution.py:48
  11.0 1.9 collective-permute-start.1
  13.0 3.1 %collective-permute-start = (bf16[64,2176]{1,0:T(8,128)(2,1)S(1)}, bf16[64,2176]{1,0:T(8,128)(2,1)S(1)}, u32[]{:S(2)}, u32[]{:S(2)}) collective-permute-start(bf16[64,2176]{1,0:T(8,128)(2,1)S(1)} %pad_maximum_fusion.2.refs_0_), channel_id=1, source_target_pairs={{0,32},{32,0},{1,33},{33,1},{2,34},{34,2},{3,35},{35,3},{4,36},{36... | collective-permute-start | bytes 835592 | tf_op jit(solution)/shard_map/ppermute | solution.py:48
  16.1 3.4 %pad_maximum_fusion = bf16[576,2048]{1,0:T(8,128)(2,1)} fusion(bf16[192,2048]{1,0:T(8,128)(2,1)} %bitcast.17, bf16[192,2048]{1,0:T(8,128)(2,1)} %bitcast.18, bf16[192,2048]{1,0:T(8,128)(2,1)} %bitcast.19), kind=kLoop, calls=%fused_computation | loop fusion | flops 7077888 | bytes 4718592 | tf_op jit(solution)/shard_map/concatenate | solution.py:263
  19.5 8.6 %collective-permute-done.2.refs_3_ = bf16[64,2176]{1,0:T(8,128)(2,1)S(1)} collective-permute-done((bf16[64,2176]{1,0:T(8,128)(2,1)S(1)}, bf16[64,2176]{1,0:T(8,128)(2,1)S(1)}, u32[]{:S(2)}, u32[]{:S(2)}) %collective-permute-start.2) | collective-permute-done | bytes 278560 | tf_op jit(solution)/shard_map/ppermute | solution.py:48
  28.0 7.8 %collective-permute-done.1.refs_2_ = bf16[64,2176]{1,0:T(8,128)(2,1)S(1)} collective-permute-done((bf16[64,2176]{1,0:T(8,128)(2,1)S(1)}, bf16[64,2176]{1,0:T(8,128)(2,1)S(1)}, u32[]{:S(2)}, u32[]{:S(2)}) %collective-permute-start.1) | collective-permute-done | bytes 278560 | tf_op jit(solution)/shard_map/ppermute | solution.py:48
  35.9 0.4 collective-permute-done.refs_1_
  36.3 5.1 %collective-permute-start.3 = (bf16[576,2048]{1,0:T(8,128)(2,1)}, bf16[576,2048]{1,0:T(8,128)(2,1)}, u32[]{:S(2)}, u32[]{:S(2)}) collective-permute-start(bf16[576,2048]{1,0:T(8,128)(2,1)} %pad_maximum_fusion), channel_id=1, source_target_pairs={{32,17},{48,1},{17,32},{1,48},{0,16},{16,0},{33,49},{49,33},{34,19... | collective-permute-start | bytes 7077896 | tf_op jit(solution)/shard_map/ppermute | solution.py:266
  41.4 4.1 %shard_map.64 = bf16[768,2048]{1,0:T(8,128)(2,1)} custom-call(s32[2]{0:T(128)S(1)} %pad_add_fusion.1.where_ref, bf16[64,2176]{1,0:T(8,128)(2,1)S(1)} %pad_maximum_fusion.2.refs_0_, bf16[64,2176]{1,0:T(8,128)(2,1)S(1)} %collective-permute-done.refs_1_, bf16[64,2176]{1,0:T(8,128)(2,1)S(1)} %collective-permute-done.1.refs_2_, ...), custom_call_target="tpu_custom_call" | custom-call | flops 805306368 | bytes 4718592 | tf_op jit(solution)/shard_map/pallas_call | solution.py:184
  45.5 13.0 %all-to-all-start = ((bf16[32,24,2048]{2,1,0:T(8,128)(2,1)}), bf16[32,24,2048]{2,1,0:T(8,128)(2,1)}, u32[]{:S(2)}, u32[]{:S(2)}) async-start(bf16[32,24,2048]{2,1,0:T(8,128)(2,1)} %bitcast.7), calls=%async_computation | async-start | bytes 6291456 | tf_op jit(solution)/shard_map/all_to_all | solution.py:285
  58.5 33.5 %collective-permute-done.3.refs_0_ = bf16[576,2048]{1,0:T(8,128)(2,1)} collective-permute-done((bf16[576,2048]{1,0:T(8,128)(2,1)}, bf16[576,2048]{1,0:T(8,128)(2,1)}, u32[]{:S(2)}, u32[]{:S(2)}) %collective-permute-start.3) | collective-permute-done | bytes 2359328 | tf_op jit(solution)/shard_map/ppermute | solution.py:266
  92.0 1.9 collective-permute-start.4
  94.0 3.4 %collective-permute-start.5 = (bf16[576,2048]{1,0:T(8,128)(2,1)}, bf16[576,2048]{1,0:T(8,128)(2,1)}, u32[]{:S(2)}, u32[]{:S(2)}) collective-permute-start(bf16[576,2048]{1,0:T(8,128)(2,1)} %collective-permute-done.3.refs_0_), channel_id=1, source_target_pairs={{0,1},{1,0},{2,3},{3,2},{4,5},{5,4},{6,7},{7,6},{8,9},{9,8},{10,11... | collective-permute-start | bytes 7077896 | tf_op jit(solution)/shard_map/ppermute | solution.py:48
  97.4 24.9 %collective-permute-done.4 = bf16[576,2048]{1,0:T(8,128)(2,1)} collective-permute-done((bf16[576,2048]{1,0:T(8,128)(2,1)}, bf16[576,2048]{1,0:T(8,128)(2,1)}, u32[]{:S(2)}, u32[]{:S(2)}) %collective-permute-start.4) | collective-permute-done | bytes 2359328 | tf_op jit(solution)/shard_map/ppermute | solution.py:267
  122.2 1.9 broadcast_select_fusion.refs_1_
  124.2 1.9 collective-permute-start.6
  126.1 5.7 %all-to-all-done = bf16[32,24,2048]{2,1,0:T(8,128)(2,1)} async-done(((bf16[32,24,2048]{2,1,0:T(8,128)(2,1)}), bf16[32,24,2048]{2,1,0:T(8,128)(2,1)}, u32[]{:S(2)}, u32[]{:S(2)}) %all-to-all-start) | async-done | bytes 3145760 | tf_op jit(solution)/shard_map/all_to_all | solution.py:285
  131.8 14.5 %shard_map.65 = (bf16[32,96,128]{2,1,0:T(8,128)(2,1)}, bf16[32,288,128]{2,1,0:T(8,128)(2,1)}) custom-call(bf16[768,2048]{1,0:T(8,128)(2,1)} %bitcast.8.rows_ref, bf16[576,2048]{1,0:T(8,128)(2,1)} %collective-permute-done.3.refs_0_, bf16[576,2048]{1,0:T(8,128)(2,1)} %copy-done, bf16[576,2048]{1,0:T(8,128)(2,1)} %collective-permute-done.5.refs_2_, ...), custom_call_target="tpu_custom_call" | custom-call | flops 7247757312 | bytes 15728640 | tf_op jit(solution)/shard_map/pallas_call | solution.py:123
  146.4 12.0 %all-to-all-start.1 = ((bf16[32,288,128]{2,1,0:T(8,128)(2,1)}), bf16[32,288,128]{2,1,0:T(8,128)(2,1)S(1)}, u32[]{:S(2)}, u32[]{:S(2)}) async-start(bf16[32,288,128]{2,1,0:T(8,128)(2,1)} %get-tuple-element.27), calls=%async_computation.1 | async-start | bytes 4718592 | tf_op jit(solution)/shard_map/all_to_all | solution.py:285
  158.4 0.1 slice_convert_fusion
  158.7 0.1 compare_reduce_fusion
  158.8 0.1 fusion.3
  158.9 0.2 fusion.1
  159.2 0.2 fusion.2
  159.4 0.3 slice.46
  159.6 0.2 select_convert_fusion
  159.8 1.0 slice.45
  160.9 1.2 pad_maximum_fusion.1
  162.1 0.1 reshape.130.spread_ref
  162.3 50.3 %all-to-all-done.1 = bf16[32,288,128]{2,1,0:T(8,128)(2,1)S(1)} async-done(((bf16[32,288,128]{2,1,0:T(8,128)(2,1)}), bf16[32,288,128]{2,1,0:T(8,128)(2,1)S(1)}, u32[]{:S(2)}, u32[]{:S(2)}) %all-to-all-start.1) | async-done | bytes 2359328 | tf_op jit(solution)/shard_map/all_to_all | solution.py:285
  212.6 8.1 %all-to-all-start.2 = ((bf16[32,96,128]{2,1,0:T(8,128)(2,1)}), bf16[32,96,128]{2,1,0:T(8,128)(2,1)}, u32[]{:S(2)}, u32[]{:S(2)}) async-start(bf16[32,96,128]{2,1,0:T(8,128)(2,1)} %get-tuple-element.28), calls=%async_computation.2 | async-start | bytes 1572864 | tf_op jit(solution)/shard_map/all_to_all | solution.py:285
  220.7 3.4 %shard_map.66 = (bf16[64,2048]{1,0:T(8,128)(2,1)}, bf16[64,2048]{1,0:T(8,128)(2,1)S(1)}, bf16[64,2048]{1,0:T(8,128)(2,1)S(1)}) custom-call(bf16[9216,128]{1,0:T(8,128)(2,1)S(1)} %bitcast.16, bf16[576,384]{1,0:T(8,128)(2,1)S(1)} %reshape.130.spread_ref), custom_call_target="tpu_custom_call" | custom-call | flops 905969664 | bytes 2359296 | tf_op jit(solution)/shard_map/pallas_call | solution.py:220
  224.1 3.4 %collective-permute-start.7 = (bf16[64,2048]{1,0:T(8,128)(2,1)}, bf16[64,2048]{1,0:T(8,128)(2,1)S(1)}, u32[]{:S(2)}, u32[]{:S(2)}) collective-permute-start(bf16[64,2048]{1,0:T(8,128)(2,1)} %get-tuple-element.32), channel_id=1, source_target_pairs={{0,32},{32,0},{1,33},{33,1},{2,34},{34,2},{3,35},{35,3},{4,36},{36... | collective-permute-start | bytes 786440 | tf_op jit(solution)/shard_map/ppermute | solution.py:48
  227.4 3.5 %collective-permute-start.8 = (bf16[64,2048]{1,0:T(8,128)(2,1)S(1)}, bf16[64,2048]{1,0:T(8,128)(2,1)S(1)}, u32[]{:S(2)}, u32[]{:S(2)}) collective-permute-start(bf16[64,2048]{1,0:T(8,128)(2,1)S(1)} %get-tuple-element.33), channel_id=1, source_target_pairs={{0,112},{16,96},{32,80},{48,64},{64,48},{80,32},{96,16},{112,0},{1... | collective-permute-start | bytes 786440 | tf_op jit(solution)/shard_map/ppermute | solution.py:48
  230.9 4.5 %collective-permute-start.9 = (bf16[64,2048]{1,0:T(8,128)(2,1)S(1)}, bf16[64,2048]{1,0:T(8,128)(2,1)S(1)}, u32[]{:S(2)}, u32[]{:S(2)}) collective-permute-start(bf16[64,2048]{1,0:T(8,128)(2,1)S(1)} %get-tuple-element.34), channel_id=1, source_target_pairs={{0,80},{16,64},{64,16},{80,0},{1,81},{17,65},{65,17},{81,1},{2,82}... | collective-permute-start | bytes 786440 | tf_op jit(solution)/shard_map/ppermute | solution.py:48
  235.4 4.2 %all-to-all-done.2 = bf16[32,96,128]{2,1,0:T(8,128)(2,1)} async-done(((bf16[32,96,128]{2,1,0:T(8,128)(2,1)}), bf16[32,96,128]{2,1,0:T(8,128)(2,1)}, u32[]{:S(2)}, u32[]{:S(2)}) %all-to-all-start.2) | async-done | bytes 786464 | tf_op jit(solution)/shard_map/all_to_all | solution.py:285
  239.7 1.4 reshape.133
  241.1 0.3 fusion.15
  241.4 11.2 %collective-permute-done.9 = bf16[64,2048]{1,0:T(8,128)(2,1)S(1)} collective-permute-done((bf16[64,2048]{1,0:T(8,128)(2,1)S(1)}, bf16[64,2048]{1,0:T(8,128)(2,1)S(1)}, u32[]{:S(2)}, u32[]{:S(2)}) %collective-permute-start.9) | collective-permute-done | bytes 262176 | tf_op jit(solution)/shard_map/ppermute | solution.py:48
  252.6 1.0 add_convert_fusion
  (20 shorter events, 0.3 us)
Async XLA Ops:
  3.5 24.5 %collective-permute-start.2 = (bf16[64,2176]{1,0:T(8,128)(2,1)S(1)}, bf16[64,2176]{1,0:T(8,128)(2,1)S(1)}, u32[]{:S(2)}, u32[]{:S(2)}) collective-permute-start(bf16[64,2176]{1,0:T(8,128)(2,1)S(1)} %pad_maximum_fusion.2.refs_0_), channel_id=1, source_target_pairs={{0,80},{16,64},{64,16},{80,0},{1,81},{17,65},{65,17},{81,1},{2,82}... | collective-permute-start | bytes 835592 | tf_op jit(solution)/shard_map/ppermute | solution.py:48
  11.0 24.9 %collective-permute-start.1 = (bf16[64,2176]{1,0:T(8,128)(2,1)S(1)}, bf16[64,2176]{1,0:T(8,128)(2,1)S(1)}, u32[]{:S(2)}, u32[]{:S(2)}) collective-permute-start(bf16[64,2176]{1,0:T(8,128)(2,1)S(1)} %pad_maximum_fusion.2.refs_0_), channel_id=1, source_target_pairs={{0,112},{16,96},{32,80},{48,64},{64,48},{80,32},{96,16},{112,0},{1... | collective-permute-start | bytes 835592 | tf_op jit(solution)/shard_map/ppermute | solution.py:48
  13.0 23.3 %collective-permute-start = (bf16[64,2176]{1,0:T(8,128)(2,1)S(1)}, bf16[64,2176]{1,0:T(8,128)(2,1)S(1)}, u32[]{:S(2)}, u32[]{:S(2)}) collective-permute-start(bf16[64,2176]{1,0:T(8,128)(2,1)S(1)} %pad_maximum_fusion.2.refs_0_), channel_id=1, source_target_pairs={{0,32},{32,0},{1,33},{33,1},{2,34},{34,2},{3,35},{35,3},{4,36},{36... | collective-permute-start | bytes 835592 | tf_op jit(solution)/shard_map/ppermute | solution.py:48
  36.3 55.7 %collective-permute-start.3 = (bf16[576,2048]{1,0:T(8,128)(2,1)}, bf16[576,2048]{1,0:T(8,128)(2,1)}, u32[]{:S(2)}, u32[]{:S(2)}) collective-permute-start(bf16[576,2048]{1,0:T(8,128)(2,1)} %pad_maximum_fusion), channel_id=1, source_target_pairs={{32,17},{48,1},{17,32},{1,48},{0,16},{16,0},{33,49},{49,33},{34,19... | collective-permute-start | bytes 7077896 | tf_op jit(solution)/shard_map/ppermute | solution.py:266
  45.5 86.3 %all-to-all-start = ((bf16[32,24,2048]{2,1,0:T(8,128)(2,1)}), bf16[32,24,2048]{2,1,0:T(8,128)(2,1)}, u32[]{:S(2)}, u32[]{:S(2)}) async-start(bf16[32,24,2048]{2,1,0:T(8,128)(2,1)} %bitcast.7), calls=%async_computation | async-start | bytes 6291456 | tf_op jit(solution)/shard_map/all_to_all | solution.py:285
  92.0 30.2 %collective-permute-start.4 = (bf16[576,2048]{1,0:T(8,128)(2,1)}, bf16[576,2048]{1,0:T(8,128)(2,1)}, u32[]{:S(2)}, u32[]{:S(2)}) collective-permute-start(bf16[576,2048]{1,0:T(8,128)(2,1)} %collective-permute-done.3.refs_0_), channel_id=1, source_target_pairs={{1,17},{17,1},{32,48},{48,32},{3,19},{19,3},{34,50},{50,34},{5,21}... | collective-permute-start | bytes 7077896 | tf_op jit(solution)/shard_map/ppermute | solution.py:267
  94.0 32.1 %collective-permute-start.5 = (bf16[576,2048]{1,0:T(8,128)(2,1)}, bf16[576,2048]{1,0:T(8,128)(2,1)}, u32[]{:S(2)}, u32[]{:S(2)}) collective-permute-start(bf16[576,2048]{1,0:T(8,128)(2,1)} %collective-permute-done.3.refs_0_), channel_id=1, source_target_pairs={{0,1},{1,0},{2,3},{3,2},{4,5},{5,4},{6,7},{7,6},{8,9},{9,8},{10,11... | collective-permute-start | bytes 7077896 | tf_op jit(solution)/shard_map/ppermute | solution.py:48
  124.1 7.7 %copy-start = (bf16[576,2048]{1,0:T(8,128)(2,1)}, bf16[576,2048]{1,0:T(8,128)(2,1)S(1)}, u32[]{:S(2)}) copy-start(bf16[576,2048]{1,0:T(8,128)(2,1)S(1)} %broadcast_select_fusion.refs_1_) | copy-start | bytes 7077892
  124.2 7.6 %collective-permute-start.6 = (bf16[576,2048]{1,0:T(8,128)(2,1)S(1)}, bf16[576,2048]{1,0:T(8,128)(2,1)}, u32[]{:S(2)}, u32[]{:S(2)}) collective-permute-start(bf16[576,2048]{1,0:T(8,128)(2,1)S(1)} %broadcast_select_fusion.refs_1_), channel_id=1, source_target_pairs={{0,1},{1,0},{2,3},{3,2},{4,5},{5,4},{6,7},{7,6},{8,9},{9,8},{10,11... | collective-permute-start | bytes 7077896 | tf_op jit(solution)/shard_map/ppermute | solution.py:48
  146.4 66.2 %all-to-all-start.1 = ((bf16[32,288,128]{2,1,0:T(8,128)(2,1)}), bf16[32,288,128]{2,1,0:T(8,128)(2,1)S(1)}, u32[]{:S(2)}, u32[]{:S(2)}) async-start(bf16[32,288,128]{2,1,0:T(8,128)(2,1)} %get-tuple-element.27), calls=%async_computation.1 | async-start | bytes 4718592 | tf_op jit(solution)/shard_map/all_to_all | solution.py:285
  212.6 27.1 %all-to-all-start.2 = ((bf16[32,96,128]{2,1,0:T(8,128)(2,1)}), bf16[32,96,128]{2,1,0:T(8,128)(2,1)}, u32[]{:S(2)}, u32[]{:S(2)}) async-start(bf16[32,96,128]{2,1,0:T(8,128)(2,1)} %get-tuple-element.28), calls=%async_computation.2 | async-start | bytes 1572864 | tf_op jit(solution)/shard_map/all_to_all | solution.py:285
  224.1 17.3 %collective-permute-start.7 = (bf16[64,2048]{1,0:T(8,128)(2,1)}, bf16[64,2048]{1,0:T(8,128)(2,1)S(1)}, u32[]{:S(2)}, u32[]{:S(2)}) collective-permute-start(bf16[64,2048]{1,0:T(8,128)(2,1)} %get-tuple-element.32), channel_id=1, source_target_pairs={{0,32},{32,0},{1,33},{33,1},{2,34},{34,2},{3,35},{35,3},{4,36},{36... | collective-permute-start | bytes 786440 | tf_op jit(solution)/shard_map/ppermute | solution.py:48
  227.4 14.0 %collective-permute-start.8 = (bf16[64,2048]{1,0:T(8,128)(2,1)S(1)}, bf16[64,2048]{1,0:T(8,128)(2,1)S(1)}, u32[]{:S(2)}, u32[]{:S(2)}) collective-permute-start(bf16[64,2048]{1,0:T(8,128)(2,1)S(1)} %get-tuple-element.33), channel_id=1, source_target_pairs={{0,112},{16,96},{32,80},{48,64},{64,48},{80,32},{96,16},{112,0},{1... | collective-permute-start | bytes 786440 | tf_op jit(solution)/shard_map/ppermute | solution.py:48
  230.9 21.6 %collective-permute-start.9 = (bf16[64,2048]{1,0:T(8,128)(2,1)S(1)}, bf16[64,2048]{1,0:T(8,128)(2,1)S(1)}, u32[]{:S(2)}, u32[]{:S(2)}) collective-permute-start(bf16[64,2048]{1,0:T(8,128)(2,1)S(1)} %get-tuple-element.34), channel_id=1, source_target_pairs={{0,80},{16,64},{64,16},{80,0},{1,81},{17,65},{65,17},{81,1},{2,82}... | collective-permute-start | bytes 786440 | tf_op jit(solution)/shard_map/ppermute | solution.py:48

commit v7 on v6

--- a/solution.py
+++ b/solution.py
@@ -48,27 +48,39 @@
     return lax.ppermute(value, axes, flips(axes))
 
 
-def expert_kernel(rows_ref, *refs):
-    pieces, (own_out, far_out) = refs[:SPLIT], refs[SPLIT : SPLIT + 2]
-    panels, (hidden, lined, staged, in_sems, out_sems) = refs[6:9], refs[9:]
-    hid = pieces[0].shape[0] // 3
-    copies = [
-        [
-            pltpu.make_async_copy(
-                piece.at[pl.ds(k * hid, hid)],
-                panel.at[pl.ds(q * hid, hid)],
-                in_sems.at[k * SPLIT + q],
-            )
-            for q, piece in enumerate(pieces)
-        ]
-        for k, panel in enumerate(panels)
-    ]
-    gates, ups, downs = copies
-    for gate_copy, up_copy in zip(gates, ups):
-        gate_copy.start()
-        up_copy.start()
-    for copy in downs:
-        copy.start()
+def expert_kernel(home_ref, rows_ref, *refs):
+    first, third, own, late, got, early = refs[:6]
+    own_out, far_out = refs[6:8]
+    panels, (hidden, lined, staged, in_sems, out_sems) = refs[8:11], refs[11:]
+    hid = first.shape[0] // 3
+    home = home_ref[0] == 1
+
+    def load(piece, k, q):
+        return pltpu.make_async_copy(
+            piece.at[pl.ds(k * hid, hid)],
+            panels[k].at[pl.ds(q * hid, hid)],
+            in_sems.at[k * SPLIT + q],
+        )
+
+    def start(kinds, quarters, pieces):
+        for q, piece in zip(quarters, pieces):
+            for k in kinds:
+                load(piece, k, q).start()
+
+    start((0, 1), (0, 1), (first, third))
+
+    @pl.when(home)
+    def _():
+        start((0, 1), (2, 3), (own, late))
+        start((2,), (2, 3), (own, late))
+
+    @pl.when(jnp.logical_not(home))
+    def _():
+        start((0, 1), (2, 3), (got, early))
+        start((2,), (2, 3), (got, early))
+
+    start((2,), (0, 1), (first, third))
+    gates, ups, downs = [[load(first, k, q) for q in range(SPLIT)] for k in range(3)]
 
     gate, up, down = panels
     dims = (((1,), (1,)), ((), ()))
@@ -113,7 +125,7 @@
         write.wait()
 
 
-def run_expert(rows, pieces):
+def run_expert(home, rows, pieces):
     count, width = rows.shape
     hid = pieces[0].shape[0] // 3
     lines = width // LANES
@@ -125,8 +137,11 @@
         out_shape=[
             jax.ShapeDtypeStruct((PLANE, n, LANES), jnp.bfloat16) for n in (cut, (CHUNKS - 1) * cut)
         ],
-        in_specs=[pl.BlockSpec(memory_space=pltpu.VMEM)]
-        + [pl.BlockSpec(memory_space=pl.ANY)] * SPLIT,
+        in_specs=[
+            pl.BlockSpec(memory_space=pltpu.SMEM),
+            pl.BlockSpec(memory_space=pltpu.VMEM),
+        ]
+        + [pl.BlockSpec(memory_space=pl.ANY)] * len(pieces),
         out_specs=[pl.BlockSpec(memory_space=pltpu.HBM)] * 2,
         scratch_shapes=[pltpu.VMEM((SPLIT * hid, width), jnp.bfloat16)] * 3
         + [
@@ -142,7 +157,7 @@
             bytes_accessed=4 * count * width + 24 * hid * width,
             transcendentals=count * hid * 4,
         ),
-    )(rows, *pieces)
+    )(home, rows, *pieces)
 
 
 def pick_kernel(where_ref, *refs):
@@ -264,8 +279,12 @@
     own, received = lax.optimization_barrier((own, received))
     axes = ("p", "b", "c")
     first = lax.ppermute(own, axes, FIRST)
-    second = jnp.where(c == p, own, lax.ppermute(first, axes, SECOND))
-    pieces = [first, second, swap(first, ("c",)), swap(second, ("c",))]
+    third = swap(first, ("c",))
+    got = lax.ppermute(first, axes, SECOND)
+    early = lax.ppermute(own, ("p", "c"), ((0, 1), (3, 2)))
+    late = lax.ppermute(got, ("p", "c"), ((1, 0), (2, 3)))
+    pieces = [first, third, own, late, got, early]
+    home = (c == p).astype(jnp.int32).reshape(1)
 
     records = [record] + received
     meta = jnp.concatenate([r[:, width:] for r in records], axis=0).astype(jnp.float32)
@@ -285,7 +304,7 @@
         return lax.all_to_all(rows, ("x", "z"), 0, 0, tiled=True)
 
     arrived = exchange(sent.reshape(PLANE, CHUNKS * MOST, width)).reshape(-1, width)
-    own_out, far_out = run_expert(arrived, pieces)
+    own_out, far_out = run_expert(home, arrived, pieces)
 
     spread = jnp.where(
         slot[:, None, :] == slots[None, :, None], weight.T[:, None, :], 0.0

time: 257 us -> 254 us (0.988)
    ppermute x1 -> x3, starting transfers between devices: 1.91 us -> 5.87 us  [the longest x1 2.67 us: shards(): late = lax.ppermute(got, ('p', 'c'), ((1, 0), (2, 3)))]
    all_to_all x3, starting transfers between devices: 33.1 us -> 29.8 us  [exchange(): return lax.all_to_all(rows, ('x', 'z'), 0, 0, tiled=True)]
    ppermute x1 -> x3, waiting for transfers between devices: 24.9 us -> 22.5 us  [the longest x1 22.5 us: shards(): got = lax.ppermute(first, axes, SECOND)]
    ppermute x8 -> x7, waiting for transfers between devices: 28 us -> 29.7 us  [swap(): return lax.ppermute(value, axes, flips(axes))]
    ppermute x8 -> x7, starting transfers between devices: 29.2 us -> 28.8 us  [swap(): return lax.ppermute(value, axes, flips(axes))]
  transfers between devices with their start and end apart: 13 -> 14, of which waited for: 9 -> 10; matrix products, arithmetic and copies ran while one was open for 4% -> 4% of each run, Pallas kernels for 3% -> 3%
where the time goes in v7:
time: 254 us; the launch traced here: 252 us
  waiting for transfers between devices  147 us (58%)
  starting transfers between devices  69.5 us (27%)
  Pallas kernels  22 us (9%)
  other arithmetic  7.8 us (3%)
  local copies, waits for them, and re-layouts  4.16 us (2%)
    all_to_all x3, waiting for transfers between devices, exchange(): return lax.all_to_all(rows, ('x', 'z'), 0, 0, tiled=True)  61.1 us
    ppermute x1, waiting for transfers between devices, shards(): first = lax.ppermute(own, axes, FIRST)  33.5 us
    all_to_all x3, starting transfers between devices, exchange(): return lax.all_to_all(rows, ('x', 'z'), 0, 0, tiled=True)  29.8 us
    ppermute x7, waiting for transfers between devices, swap(): return lax.ppermute(value, axes, flips(axes))  29.7 us
    ppermute x7, starting transfers between devices, swap(): return lax.ppermute(value, axes, flips(axes))  28.8 us
    ppermute x1, waiting for transfers between devices, shards(): got = lax.ppermute(first, axes, SECOND)  22.5 us
    pallas_call x1, Pallas kernels, run_expert(): pl.pallas_call(expert_kernel, out_shape=[jax.ShapeDtypeStruct((PLANE, n,...  14.5 us
  transfers between devices with their start and end apart: 14, of which 10 were waited for; matrix products, arithmetic and copies ran while one was open for 4% of the time, Pallas kernels for 3%

profile of v7, /device:TPU:1, one launch (start us, length us, event | category | flops | bytes accessed | tf_op | source)
XLA Modules:
  0.0 252.1 jit_solution(10385723244551152804)
XLA Ops:
  0.0 0.7 convert_element_type.53
  0.7 0.1 copy.19
  0.8 0.1 copy.21
  0.9 0.8 copy.20
  1.7 0.7 convert_element_type.52
  2.3 0.1 copy.18
  2.5 1.0 pad_maximum_fusion.2.refs_0_
  3.5 7.5 %collective-permute-start.2 = (bf16[64,2176]{1,0:T(8,128)(2,1)S(1)}, bf16[64,2176]{1,0:T(8,128)(2,1)S(1)}, u32[]{:S(2)}, u32[]{:S(2)}) collective-permute-start(bf16[64,2176]{1,0:T(8,128)(2,1)S(1)} %pad_maximum_fusion.2.refs_0_), channel_id=1, source_target_pairs={{0,80},{16,64},{64,16},{80,0},{1,81},{17,65},{65,17},{81,1},{2,82}... | collective-permute-start | bytes 835592 | tf_op jit(solution)/shard_map/ppermute | solution.py:48
  11.0 1.9 collective-permute-start.1
  13.0 3.1 %collective-permute-start = (bf16[64,2176]{1,0:T(8,128)(2,1)S(1)}, bf16[64,2176]{1,0:T(8,128)(2,1)S(1)}, u32[]{:S(2)}, u32[]{:S(2)}) collective-permute-start(bf16[64,2176]{1,0:T(8,128)(2,1)S(1)} %pad_maximum_fusion.2.refs_0_), channel_id=1, source_target_pairs={{0,32},{32,0},{1,33},{33,1},{2,34},{34,2},{3,35},{35,3},{4,36},{36... | collective-permute-start | bytes 835592 | tf_op jit(solution)/shard_map/ppermute | solution.py:48
  16.1 3.4 %pad_maximum_fusion.refs_2_ = bf16[576,2048]{1,0:T(8,128)(2,1)} fusion(bf16[192,2048]{1,0:T(8,128)(2,1)} %bitcast.18, bf16[192,2048]{1,0:T(8,128)(2,1)} %bitcast.19, bf16[192,2048]{1,0:T(8,128)(2,1)} %bitcast.20), kind=kLoop, calls=%fused_computation | loop fusion | flops 7077888 | bytes 4718592 | tf_op jit(solution)/shard_map/concatenate | solution.py:278
  19.4 8.6 %collective-permute-done.2.refs_3_ = bf16[64,2176]{1,0:T(8,128)(2,1)S(1)} collective-permute-done((bf16[64,2176]{1,0:T(8,128)(2,1)S(1)}, bf16[64,2176]{1,0:T(8,128)(2,1)S(1)}, u32[]{:S(2)}, u32[]{:S(2)}) %collective-permute-start.2) | collective-permute-done | bytes 278560 | tf_op jit(solution)/shard_map/ppermute | solution.py:48
  28.0 7.8 %collective-permute-done.1.refs_2_ = bf16[64,2176]{1,0:T(8,128)(2,1)S(1)} collective-permute-done((bf16[64,2176]{1,0:T(8,128)(2,1)S(1)}, bf16[64,2176]{1,0:T(8,128)(2,1)S(1)}, u32[]{:S(2)}, u32[]{:S(2)}) %collective-permute-start.1) | collective-permute-done | bytes 278560 | tf_op jit(solution)/shard_map/ppermute | solution.py:48
  35.9 0.4 collective-permute-done.refs_1_
  36.3 5.1 %collective-permute-start.3 = (bf16[576,2048]{1,0:T(8,128)(2,1)}, bf16[576,2048]{1,0:T(8,128)(2,1)}, u32[]{:S(2)}, u32[]{:S(2)}) collective-permute-start(bf16[576,2048]{1,0:T(8,128)(2,1)} %pad_maximum_fusion.refs_2_), channel_id=1, source_target_pairs={{32,17},{48,1},{17,32},{1,48},{0,16},{16,0},{33,49},{49,33},{34,19... | collective-permute-start | bytes 7077896 | tf_op jit(solution)/shard_map/ppermute | solution.py:281
  41.4 4.1 %shard_map.64 = bf16[768,2048]{1,0:T(8,128)(2,1)} custom-call(s32[2]{0:T(128)S(1)} %pad_add_fusion.1.where_ref, bf16[64,2176]{1,0:T(8,128)(2,1)S(1)} %pad_maximum_fusion.2.refs_0_, bf16[64,2176]{1,0:T(8,128)(2,1)S(1)} %collective-permute-done.refs_1_, bf16[64,2176]{1,0:T(8,128)(2,1)S(1)} %collective-permute-done.1.refs_2_, ...), custom_call_target="tpu_custom_call" | custom-call | flops 805306368 | bytes 4718592 | tf_op jit(solution)/shard_map/pallas_call | solution.py:199
  45.5 13.0 %all-to-all-start = ((bf16[32,24,2048]{2,1,0:T(8,128)(2,1)}), bf16[32,24,2048]{2,1,0:T(8,128)(2,1)}, u32[]{:S(2)}, u32[]{:S(2)}) async-start(bf16[32,24,2048]{2,1,0:T(8,128)(2,1)} %bitcast.8), calls=%async_computation | async-start | bytes 6291456 | tf_op jit(solution)/shard_map/all_to_all | solution.py:304
  58.5 33.5 %collective-permute-done.3.refs_0_ = bf16[576,2048]{1,0:T(8,128)(2,1)} collective-permute-done((bf16[576,2048]{1,0:T(8,128)(2,1)}, bf16[576,2048]{1,0:T(8,128)(2,1)}, u32[]{:S(2)}, u32[]{:S(2)}) %collective-permute-start.3) | collective-permute-done | bytes 2359328 | tf_op jit(solution)/shard_map/ppermute | solution.py:281
  92.0 1.9 collective-permute-start.5
  94.0 1.3 collective-permute-start.7
  95.3 4.4 %collective-permute-start.4 = (bf16[576,2048]{1,0:T(8,128)(2,1)}, bf16[576,2048]{1,0:T(8,128)(2,1)}, u32[]{:S(2)}, u32[]{:S(2)}) collective-permute-start(bf16[576,2048]{1,0:T(8,128)(2,1)} %collective-permute-done.3.refs_0_), channel_id=1, source_target_pairs={{0,1},{1,0},{2,3},{3,2},{4,5},{5,4},{6,7},{7,6},{8,9},{9,8},{10,11... | collective-permute-start | bytes 7077896 | tf_op jit(solution)/shard_map/ppermute | solution.py:48
  99.7 22.5 %collective-permute-done.5.refs_4_ = bf16[576,2048]{1,0:T(8,128)(2,1)S(1)} collective-permute-done((bf16[576,2048]{1,0:T(8,128)(2,1)}, bf16[576,2048]{1,0:T(8,128)(2,1)S(1)}, u32[]{:S(2)}, u32[]{:S(2)}) %collective-permute-start.5) | collective-permute-done | bytes 2359328 | tf_op jit(solution)/shard_map/ppermute | solution.py:283
  122.2 2.7 %collective-permute-start.6 = (bf16[576,2048]{1,0:T(8,128)(2,1)S(1)}, bf16[576,2048]{1,0:T(8,128)(2,1)}, u32[]{:S(2)}, u32[]{:S(2)}) collective-permute-start(bf16[576,2048]{1,0:T(8,128)(2,1)S(1)} %collective-permute-done.5.refs_4_), channel_id=1, source_target_pairs={{1,0},{32,33},{3,2},{34,35},{5,4},{36,37},{7,6},{38,39},{9,8},{40,... | collective-permute-start | bytes 7077896 | tf_op jit(solution)/shard_map/ppermute | solution.py:285
  124.9 6.9 %all-to-all-done = bf16[32,24,2048]{2,1,0:T(8,128)(2,1)} async-done(((bf16[32,24,2048]{2,1,0:T(8,128)(2,1)}), bf16[32,24,2048]{2,1,0:T(8,128)(2,1)}, u32[]{:S(2)}, u32[]{:S(2)}) %all-to-all-start) | async-done | bytes 3145760 | tf_op jit(solution)/shard_map/all_to_all | solution.py:304
  131.8 14.5 %shard_map.65 = (bf16[32,96,128]{2,1,0:T(8,128)(2,1)}, bf16[32,288,128]{2,1,0:T(8,128)(2,1)}) custom-call(s32[1]{0:T(128)} %bitcast.5.home_ref, bf16[768,2048]{1,0:T(8,128)(2,1)} %bitcast.9.rows_ref, bf16[576,2048]{1,0:T(8,128)(2,1)} %collective-permute-done.3.refs_0_, bf16[576,2048]{1,0:T(8,128)(2,1)} %collective-permute-done.4.refs_1_, ...), custom_call_target="tpu_custom_call" | custom-call | flops 7247757312 | bytes 15728640 | tf_op jit(solution)/shard_map/pallas_call | solution.py:135
  146.4 9.0 %all-to-all-start.1 = ((bf16[32,288,128]{2,1,0:T(8,128)(2,1)}), bf16[32,288,128]{2,1,0:T(8,128)(2,1)S(1)}, u32[]{:S(2)}, u32[]{:S(2)}) async-start(bf16[32,288,128]{2,1,0:T(8,128)(2,1)} %get-tuple-element.27), calls=%async_computation.1 | async-start | bytes 4718592 | tf_op jit(solution)/shard_map/all_to_all | solution.py:304
  155.5 0.1 slice_convert_fusion
  155.8 0.1 compare_reduce_fusion
  155.9 0.1 fusion.3
  156.0 0.2 fusion.1
  156.2 0.2 fusion.2
  156.4 0.3 slice.46
  156.7 0.2 select_convert_fusion
  156.9 1.0 slice.45
  158.0 1.2 pad_maximum_fusion.1
  159.2 0.1 reshape.135.spread_ref
  159.3 50.3 %all-to-all-done.1 = bf16[32,288,128]{2,1,0:T(8,128)(2,1)S(1)} async-done(((bf16[32,288,128]{2,1,0:T(8,128)(2,1)}), bf16[32,288,128]{2,1,0:T(8,128)(2,1)S(1)}, u32[]{:S(2)}, u32[]{:S(2)}) %all-to-all-start.1) | async-done | bytes 2359328 | tf_op jit(solution)/shard_map/all_to_all | solution.py:304
  209.6 7.7 %all-to-all-start.2 = ((bf16[32,96,128]{2,1,0:T(8,128)(2,1)}), bf16[32,96,128]{2,1,0:T(8,128)(2,1)}, u32[]{:S(2)}, u32[]{:S(2)}) async-start(bf16[32,96,128]{2,1,0:T(8,128)(2,1)} %get-tuple-element.28), calls=%async_computation.2 | async-start | bytes 1572864 | tf_op jit(solution)/shard_map/all_to_all | solution.py:304
  217.4 3.4 %shard_map.66 = (bf16[64,2048]{1,0:T(8,128)(2,1)}, bf16[64,2048]{1,0:T(8,128)(2,1)S(1)}, bf16[64,2048]{1,0:T(8,128)(2,1)S(1)}) custom-call(bf16[9216,128]{1,0:T(8,128)(2,1)S(1)} %bitcast.17, bf16[576,384]{1,0:T(8,128)(2,1)S(1)} %reshape.135.spread_ref), custom_call_target="tpu_custom_call" | custom-call | flops 905969664 | bytes 2359296 | tf_op jit(solution)/shard_map/pallas_call | solution.py:235
  220.7 4.4 %collective-permute-start.8 = (bf16[64,2048]{1,0:T(8,128)(2,1)}, bf16[64,2048]{1,0:T(8,128)(2,1)S(1)}, u32[]{:S(2)}, u32[]{:S(2)}) collective-permute-start(bf16[64,2048]{1,0:T(8,128)(2,1)} %get-tuple-element.32), channel_id=1, source_target_pairs={{0,32},{32,0},{1,33},{33,1},{2,34},{34,2},{3,35},{35,3},{4,36},{36... | collective-permute-start | bytes 786440 | tf_op jit(solution)/shard_map/ppermute | solution.py:48
  225.1 3.5 %collective-permute-start.9 = (bf16[64,2048]{1,0:T(8,128)(2,1)S(1)}, bf16[64,2048]{1,0:T(8,128)(2,1)S(1)}, u32[]{:S(2)}, u32[]{:S(2)}) collective-permute-start(bf16[64,2048]{1,0:T(8,128)(2,1)S(1)} %get-tuple-element.33), channel_id=1, source_target_pairs={{0,112},{16,96},{32,80},{48,64},{64,48},{80,32},{96,16},{112,0},{1... | collective-permute-start | bytes 786440 | tf_op jit(solution)/shard_map/ppermute | solution.py:48
  228.6 4.0 %collective-permute-start.10 = (bf16[64,2048]{1,0:T(8,128)(2,1)S(1)}, bf16[64,2048]{1,0:T(8,128)(2,1)S(1)}, u32[]{:S(2)}, u32[]{:S(2)}) collective-permute-start(bf16[64,2048]{1,0:T(8,128)(2,1)S(1)} %get-tuple-element.34), channel_id=1, source_target_pairs={{0,80},{16,64},{64,16},{80,0},{1,81},{17,65},{65,17},{81,1},{2,82}... | collective-permute-start | bytes 786440 | tf_op jit(solution)/shard_map/ppermute | solution.py:48
  232.6 3.9 %all-to-all-done.2 = bf16[32,96,128]{2,1,0:T(8,128)(2,1)} async-done(((bf16[32,96,128]{2,1,0:T(8,128)(2,1)}), bf16[32,96,128]{2,1,0:T(8,128)(2,1)}, u32[]{:S(2)}, u32[]{:S(2)}) %all-to-all-start.2) | async-done | bytes 786464 | tf_op jit(solution)/shard_map/all_to_all | solution.py:304
  236.6 1.4 reshape.140
  238.0 0.3 fusion.15
  238.3 7.0 %collective-permute-done.9 = bf16[64,2048]{1,0:T(8,128)(2,1)S(1)} collective-permute-done((bf16[64,2048]{1,0:T(8,128)(2,1)S(1)}, bf16[64,2048]{1,0:T(8,128)(2,1)S(1)}, u32[]{:S(2)}, u32[]{:S(2)}) %collective-permute-start.9) | collective-permute-done | bytes 262176 | tf_op jit(solution)/shard_map/ppermute | solution.py:48
  245.3 5.8 %collective-permute-done.10 = bf16[64,2048]{1,0:T(8,128)(2,1)S(1)} collective-permute-done((bf16[64,2048]{1,0:T(8,128)(2,1)S(1)}, bf16[64,2048]{1,0:T(8,128)(2,1)S(1)}, u32[]{:S(2)}, u32[]{:S(2)}) %collective-permute-start.10) | collective-permute-done | bytes 262176 | tf_op jit(solution)/shard_map/ppermute | solution.py:48
  251.1 1.0 add_convert_fusion
  (21 shorter events, 0.4 us)
Async XLA Ops:
  3.5 24.5 %collective-permute-start.2 = (bf16[64,2176]{1,0:T(8,128)(2,1)S(1)}, bf16[64,2176]{1,0:T(8,128)(2,1)S(1)}, u32[]{:S(2)}, u32[]{:S(2)}) collective-permute-start(bf16[64,2176]{1,0:T(8,128)(2,1)S(1)} %pad_maximum_fusion.2.refs_0_), channel_id=1, source_target_pairs={{0,80},{16,64},{64,16},{80,0},{1,81},{17,65},{65,17},{81,1},{2,82}... | collective-permute-start | bytes 835592 | tf_op jit(solution)/shard_map/ppermute | solution.py:48
  11.0 24.9 %collective-permute-start.1 = (bf16[64,2176]{1,0:T(8,128)(2,1)S(1)}, bf16[64,2176]{1,0:T(8,128)(2,1)S(1)}, u32[]{:S(2)}, u32[]{:S(2)}) collective-permute-start(bf16[64,2176]{1,0:T(8,128)(2,1)S(1)} %pad_maximum_fusion.2.refs_0_), channel_id=1, source_target_pairs={{0,112},{16,96},{32,80},{48,64},{64,48},{80,32},{96,16},{112,0},{1... | collective-permute-start | bytes 835592 | tf_op jit(solution)/shard_map/ppermute | solution.py:48
  13.0 23.3 %collective-permute-start = (bf16[64,2176]{1,0:T(8,128)(2,1)S(1)}, bf16[64,2176]{1,0:T(8,128)(2,1)S(1)}, u32[]{:S(2)}, u32[]{:S(2)}) collective-permute-start(bf16[64,2176]{1,0:T(8,128)(2,1)S(1)} %pad_maximum_fusion.2.refs_0_), channel_id=1, source_target_pairs={{0,32},{32,0},{1,33},{33,1},{2,34},{34,2},{3,35},{35,3},{4,36},{36... | collective-permute-start | bytes 835592 | tf_op jit(solution)/shard_map/ppermute | solution.py:48
  36.3 55.7 %collective-permute-start.3 = (bf16[576,2048]{1,0:T(8,128)(2,1)}, bf16[576,2048]{1,0:T(8,128)(2,1)}, u32[]{:S(2)}, u32[]{:S(2)}) collective-permute-start(bf16[576,2048]{1,0:T(8,128)(2,1)} %pad_maximum_fusion.refs_2_), channel_id=1, source_target_pairs={{32,17},{48,1},{17,32},{1,48},{0,16},{16,0},{33,49},{49,33},{34,19... | collective-permute-start | bytes 7077896 | tf_op jit(solution)/shard_map/ppermute | solution.py:281
  45.5 86.3 %all-to-all-start = ((bf16[32,24,2048]{2,1,0:T(8,128)(2,1)}), bf16[32,24,2048]{2,1,0:T(8,128)(2,1)}, u32[]{:S(2)}, u32[]{:S(2)}) async-start(bf16[32,24,2048]{2,1,0:T(8,128)(2,1)} %bitcast.8), calls=%async_computation | async-start | bytes 6291456 | tf_op jit(solution)/shard_map/all_to_all | solution.py:304
  92.0 30.2 %collective-permute-start.5 = (bf16[576,2048]{1,0:T(8,128)(2,1)}, bf16[576,2048]{1,0:T(8,128)(2,1)S(1)}, u32[]{:S(2)}, u32[]{:S(2)}) collective-permute-start(bf16[576,2048]{1,0:T(8,128)(2,1)} %collective-permute-done.3.refs_0_), channel_id=1, source_target_pairs={{1,17},{17,1},{32,48},{48,32},{3,19},{19,3},{34,50},{50,34},{5,21}... | collective-permute-start | bytes 7077896 | tf_op jit(solution)/shard_map/ppermute | solution.py:283
  94.0 30.9 %collective-permute-start.7 = (bf16[576,2048]{1,0:T(8,128)(2,1)}, bf16[576,2048]{1,0:T(8,128)(2,1)}, u32[]{:S(2)}, u32[]{:S(2)}) collective-permute-start(bf16[576,2048]{1,0:T(8,128)(2,1)} %pad_maximum_fusion.refs_2_), channel_id=1, source_target_pairs={{0,1},{33,32},{2,3},{35,34},{4,5},{37,36},{6,7},{39,38},{8,9},{41,... | collective-permute-start | bytes 7077896 | tf_op jit(solution)/shard_map/ppermute | solution.py:284
  95.3 29.6 %collective-permute-start.4 = (bf16[576,2048]{1,0:T(8,128)(2,1)}, bf16[576,2048]{1,0:T(8,128)(2,1)}, u32[]{:S(2)}, u32[]{:S(2)}) collective-permute-start(bf16[576,2048]{1,0:T(8,128)(2,1)} %collective-permute-done.3.refs_0_), channel_id=1, source_target_pairs={{0,1},{1,0},{2,3},{3,2},{4,5},{5,4},{6,7},{7,6},{8,9},{9,8},{10,11... | collective-permute-start | bytes 7077896 | tf_op jit(solution)/shard_map/ppermute | solution.py:48
  122.2 9.6 %copy-start = (bf16[576,2048]{1,0:T(8,128)(2,1)}, bf16[576,2048]{1,0:T(8,128)(2,1)S(1)}, u32[]{:S(2)}) copy-start(bf16[576,2048]{1,0:T(8,128)(2,1)S(1)} %collective-permute-done.5.refs_4_) | copy-start | bytes 7077892
  122.2 9.6 %collective-permute-start.6 = (bf16[576,2048]{1,0:T(8,128)(2,1)S(1)}, bf16[576,2048]{1,0:T(8,128)(2,1)}, u32[]{:S(2)}, u32[]{:S(2)}) collective-permute-start(bf16[576,2048]{1,0:T(8,128)(2,1)S(1)} %collective-permute-done.5.refs_4_), channel_id=1, source_target_pairs={{1,0},{32,33},{3,2},{34,35},{5,4},{36,37},{7,6},{38,39},{9,8},{40,... | collective-permute-start | bytes 7077896 | tf_op jit(solution)/shard_map/ppermute | solution.py:285
  146.4 63.3 %all-to-all-start.1 = ((bf16[32,288,128]{2,1,0:T(8,128)(2,1)}), bf16[32,288,128]{2,1,0:T(8,128)(2,1)S(1)}, u32[]{:S(2)}, u32[]{:S(2)}) async-start(bf16[32,288,128]{2,1,0:T(8,128)(2,1)} %get-tuple-element.27), calls=%async_computation.1 | async-start | bytes 4718592 | tf_op jit(solution)/shard_map/all_to_all | solution.py:304
  209.6 26.9 %all-to-all-start.2 = ((bf16[32,96,128]{2,1,0:T(8,128)(2,1)}), bf16[32,96,128]{2,1,0:T(8,128)(2,1)}, u32[]{:S(2)}, u32[]{:S(2)}) async-start(bf16[32,96,128]{2,1,0:T(8,128)(2,1)} %get-tuple-element.28), calls=%async_computation.2 | async-start | bytes 1572864 | tf_op jit(solution)/shard_map/all_to_all | solution.py:304
  220.7 17.6 %collective-permute-start.8 = (bf16[64,2048]{1,0:T(8,128)(2,1)}, bf16[64,2048]{1,0:T(8,128)(2,1)S(1)}, u32[]{:S(2)}, u32[]{:S(2)}) collective-permute-start(bf16[64,2048]{1,0:T(8,128)(2,1)} %get-tuple-element.32), channel_id=1, source_target_pairs={{0,32},{32,0},{1,33},{33,1},{2,34},{34,2},{3,35},{35,3},{4,36},{36... | collective-permute-start | bytes 786440 | tf_op jit(solution)/shard_map/ppermute | solution.py:48
  225.1 20.2 %collective-permute-start.9 = (bf16[64,2048]{1,0:T(8,128)(2,1)S(1)}, bf16[64,2048]{1,0:T(8,128)(2,1)S(1)}, u32[]{:S(2)}, u32[]{:S(2)}) collective-permute-start(bf16[64,2048]{1,0:T(8,128)(2,1)S(1)} %get-tuple-element.33), channel_id=1, source_target_pairs={{0,112},{16,96},{32,80},{48,64},{64,48},{80,32},{96,16},{112,0},{1... | collective-permute-start | bytes 786440 | tf_op jit(solution)/shard_map/ppermute | solution.py:48
  228.6 22.5 %collective-permute-start.10 = (bf16[64,2048]{1,0:T(8,128)(2,1)S(1)}, bf16[64,2048]{1,0:T(8,128)(2,1)S(1)}, u32[]{:S(2)}, u32[]{:S(2)}) collective-permute-start(bf16[64,2048]{1,0:T(8,128)(2,1)S(1)} %get-tuple-element.34), channel_id=1, source_target_pairs={{0,80},{16,64},{64,16},{80,0},{1,81},{17,65},{65,17},{81,1},{2,82}... | collective-permute-start | bytes 786440 | tf_op jit(solution)/shard_map/ppermute | solution.py:48

commit v8 on v7

--- a/solution.py
+++ b/solution.py
@@ -161,10 +161,9 @@
 
 
 def pick_kernel(where_ref, *refs):
-    sources, out_ref = refs[:-1], refs[-1]
-    width = out_ref.shape[1]
+    sources, metas, out_ref = refs[:CHUNKS], refs[CHUNKS:-1], refs[-1]
     records = jnp.concatenate([source[...] for source in sources], axis=0)
-    named = records[:, width:].astype(jnp.float32).T
+    named = jnp.concatenate([meta[...] for meta in metas], axis=0).astype(jnp.float32).T
     tokens = records.shape[0]
     count = tokens // len(sources)
     share = CHUNKS * MOST
@@ -187,20 +186,20 @@
     slots = lax.broadcasted_iota(jnp.int32, (experts, share, tokens), 1)
     hit = jnp.where(slot[:, None, :] == slots, 1.0, 0.0).reshape(experts * share, tokens)
     out_ref[...] = jnp.dot(
-        hit.astype(jnp.bfloat16), records[:, :width], preferred_element_type=jnp.float32
+        hit.astype(jnp.bfloat16), records, preferred_element_type=jnp.float32
     ).astype(jnp.bfloat16)
 
 
-def pick_rows(where, sources, width):
+def pick_rows(where, sources, metas, width):
     tokens = len(sources) * sources[0].shape[0]
     count = PLANE * CHUNKS * MOST
     steps = SIZES[0]
-    whole = pl.BlockSpec(sources[0].shape, lambda i: (0, 0))
+    whole = [pl.BlockSpec(source.shape, lambda i: (0, 0)) for source in sources + metas]
     return pl.pallas_call(
         pick_kernel,
         grid=(steps,),
         out_shape=jax.ShapeDtypeStruct((count, width), jnp.bfloat16),
-        in_specs=[pl.BlockSpec(memory_space=pltpu.SMEM)] + [whole] * len(sources),
+        in_specs=[pl.BlockSpec(memory_space=pltpu.SMEM)] + whole,
         out_specs=pl.BlockSpec((count // steps, width), lambda i: (i, 0)),
         compiler_params=pltpu.CompilerParams(vmem_limit_bytes=20 * 1024 * 1024),
         cost_estimate=pl.CostEstimate(
@@ -208,7 +207,7 @@
             bytes_accessed=2 * (count + tokens) * (width + tokens),
             transcendentals=0,
         ),
-    )(where, *sources)
+    )(where, *sources, *metas)
 
 
 def sum_kernel(returned_ref, spread_ref, *refs):
@@ -272,11 +271,12 @@
     meta = sum(
         jnp.pad(f, ((0, 0), (top * k, EXTRA - top * (k + 1)))) for k, f in enumerate(fields)
     )
-    record = jnp.concatenate([tokens, meta], axis=1)
-    received = [swap(record, axes) for axes in PARTNERS]
+    received = [swap(tokens, axes) for axes in PARTNERS]
+    meta, received[0] = lax.optimization_barrier((meta, received[0]))
+    metas = [meta] + [swap(meta, axes) for axes in PARTNERS]
 
     own = jnp.concatenate([gate_weight[0, 0], up_weight[0, 0], down_weight[0, 0]], axis=0)
-    own, received = lax.optimization_barrier((own, received))
+    own, received, metas = lax.optimization_barrier((own, received, metas))
     axes = ("p", "b", "c")
     first = lax.ppermute(own, axes, FIRST)
     third = swap(first, ("c",))
@@ -286,8 +286,7 @@
     pieces = [first, third, own, late, got, early]
     home = (c == p).astype(jnp.int32).reshape(1)
 
-    records = [record] + received
-    meta = jnp.concatenate([r[:, width:] for r in records], axis=0).astype(jnp.float32)
+    meta = jnp.concatenate(metas, axis=0).astype(jnp.float32)
     named = meta[:, :top].astype(jnp.int32)
     weight = meta[:, top : 2 * top] + meta[:, 2 * top : 3 * top]
     target = jnp.arange(PLANE, dtype=jnp.int32)
@@ -298,7 +297,7 @@
     slot = jnp.where(chosen, ranks(chosen, count) + (chunk * MOST)[:, None], -1).T
     slots = jnp.arange(CHUNKS * MOST, dtype=jnp.int32)
     where = jnp.stack([p, h]).astype(jnp.int32)
-    sent = pick_rows(where, records, width)
+    sent = pick_rows(where, [tokens] + received, metas, width)
 
     def exchange(rows):
         return lax.all_to_all(rows, ("x", "z"), 0, 0, tiled=True)

time: 254 us -> 256 us (level)
  starting transfers between devices: 69.5 us -> 90.2 us
  waiting for transfers between devices: 147 us -> 128 us
    ppermute x7 -> x10, waiting for transfers between devices: 29.7 us -> 16.7 us  [swap(): return lax.ppermute(value, axes, flips(axes))]
    ppermute x7 -> x10, starting transfers between devices: 28.8 us -> 41.4 us  [swap(): return lax.ppermute(value, axes, flips(axes))]
    all_to_all x3, starting transfers between devices: 29.8 us -> 33.7 us  [exchange(): return lax.all_to_all(rows, ('x', 'z'), 0, 0, tiled=True)]
    all_to_all x3, waiting for transfers between devices: 61.1 us -> 57.7 us  [exchange(): return lax.all_to_all(rows, ('x', 'z'), 0, 0, tiled=True)]
  transfers between devices with their start and end apart: 14 -> 17, of which waited for: 10 -> 12; matrix products, arithmetic and copies ran while one was open for 4% -> 5% of each run, Pallas kernels for 3% -> 3%
where the time goes in v8:
time: 256 us; the launch traced here: 253 us
  waiting for transfers between devices  128 us (50%)
  starting transfers between devices  90.2 us (35%)
  Pallas kernels  22 us (9%)
  other arithmetic  6.72 us (3%)
  local copies, waits for them, and re-layouts  4.45 us (2%)
    all_to_all x3, waiting for transfers between devices, exchange(): return lax.all_to_all(rows, ('x', 'z'), 0, 0, tiled=True)  57.7 us
    ppermute x10, starting transfers between devices, swap(): return lax.ppermute(value, axes, flips(axes))  41.4 us
    all_to_all x3, starting transfers between devices, exchange(): return lax.all_to_all(rows, ('x', 'z'), 0, 0, tiled=True)  33.7 us
    ppermute x1, waiting for transfers between devices, shards(): first = lax.ppermute(own, axes, FIRST)  32.8 us
    ppermute x1, waiting for transfers between devices, shards(): got = lax.ppermute(first, axes, SECOND)  20.9 us
    ppermute x10, waiting for transfers between devices, swap(): return lax.ppermute(value, axes, flips(axes))  16.7 us
    pallas_call x1, Pallas kernels, run_expert(): pl.pallas_call(expert_kernel, out_shape=[jax.ShapeDtypeStruct((PLANE, n,...  14.6 us
    ppermute x1, starting transfers between devices, shards(): first = lax.ppermute(own, axes, FIRST)  6.92 us
  transfers between devices with their start and end apart: 17, of which 12 were waited for; matrix products, arithmetic and copies ran while one was open for 5% of the time, Pallas kernels for 3%

profile of v8, /device:TPU:1, one launch (start us, length us, event | category | flops | bytes accessed | tf_op | source)
XLA Modules:
  0.0 253.3 jit_solution(11401296866257256358)
XLA Ops:
  0.0 5.0 %collective-permute-start = (bf16[64,2048]{1,0:T(8,128)(2,1)}, bf16[64,2048]{1,0:T(8,128)(2,1)S(1)}, u32[]{:S(2)}, u32[]{:S(2)}) collective-permute-start(bf16[64,2048]{1,0:T(8,128)(2,1)} %refs_0_.1), channel_id=1, source_target_pairs={{0,32},{32,0},{1,33},{33,1},{2,34},{34,2},{3,35},{35,3},{4,36},{36... | collective-permute-start | bytes 786440 | tf_op jit(solution)/shard_map/ppermute | solution.py:48
  5.0 4.6 %collective-permute-start.1 = (bf16[64,2048]{1,0:T(8,128)(2,1)}, bf16[64,2048]{1,0:T(8,128)(2,1)S(1)}, u32[]{:S(2)}, u32[]{:S(2)}) collective-permute-start(bf16[64,2048]{1,0:T(8,128)(2,1)} %refs_0_.1), channel_id=1, source_target_pairs={{0,112},{16,96},{32,80},{48,64},{64,48},{80,32},{96,16},{112,0},{1... | collective-permute-start | bytes 786440 | tf_op jit(solution)/shard_map/ppermute | solution.py:48
  9.7 2.5 collective-permute-start.2
  12.2 0.7 convert_element_type.53
  12.9 0.8 copy.20
  13.8 0.7 convert_element_type.52
  14.7 1.5 collective-permute-done.refs_1_
  16.3 1.9 collective-permute-start.3
  18.2 5.7 %collective-permute-start.4 = (bf16[64,128]{1,0:T(8,128)(2,1)S(1)}, bf16[64,128]{1,0:T(8,128)(2,1)S(1)}, u32[]{:S(2)}, u32[]{:S(2)}) collective-permute-start(bf16[64,128]{1,0:T(8,128)(2,1)S(1)} %pad_add_fusion.refs_4_), channel_id=1, source_target_pairs={{0,112},{16,96},{32,80},{48,64},{64,48},{80,32},{96,16},{112,0},{1... | collective-permute-start | bytes 49160 | tf_op jit(solution)/shard_map/ppermute | solution.py:48
  23.9 4.0 %collective-permute-start.5 = (bf16[64,128]{1,0:T(8,128)(2,1)S(1)}, bf16[64,128]{1,0:T(8,128)(2,1)S(1)}, u32[]{:S(2)}, u32[]{:S(2)}) collective-permute-start(bf16[64,128]{1,0:T(8,128)(2,1)S(1)} %pad_add_fusion.refs_4_), channel_id=1, source_target_pairs={{0,80},{16,64},{64,16},{80,0},{1,81},{17,65},{65,17},{81,1},{2,82}... | collective-permute-start | bytes 49160 | tf_op jit(solution)/shard_map/ppermute | solution.py:48
  27.9 3.4 %pad_maximum_fusion.refs_2_ = bf16[576,2048]{1,0:T(8,128)(2,1)} fusion(bf16[192,2048]{1,0:T(8,128)(2,1)} %bitcast.18, bf16[192,2048]{1,0:T(8,128)(2,1)} %bitcast.19, bf16[192,2048]{1,0:T(8,128)(2,1)} %bitcast.20), kind=kLoop, calls=%fused_computation | loop fusion | flops 7077888 | bytes 4718592 | tf_op jit(solution)/shard_map/concatenate | solution.py:278
  31.4 0.5 collective-permute-done.2.refs_3_
  31.9 0.3 collective-permute-done.4.refs_6_
  32.2 0.4 collective-permute-done.5.refs_7_
  32.6 6.9 %collective-permute-start.6 = (bf16[576,2048]{1,0:T(8,128)(2,1)}, bf16[576,2048]{1,0:T(8,128)(2,1)S(1)}, u32[]{:S(2)}, u32[]{:S(2)}) collective-permute-start(bf16[576,2048]{1,0:T(8,128)(2,1)} %pad_maximum_fusion.refs_2_), channel_id=1, source_target_pairs={{32,17},{48,1},{17,32},{1,48},{0,16},{16,0},{33,49},{49,33},{34,19... | collective-permute-start | bytes 7077896 | tf_op jit(solution)/shard_map/ppermute | solution.py:281
  39.6 4.1 %shard_map.64 = bf16[768,2048]{1,0:T(8,128)(2,1)} custom-call(s32[2]{0:T(128)S(1)} %pad_add_fusion.1.where_ref, bf16[64,2048]{1,0:T(8,128)(2,1)S(1)} %copy-done, bf16[64,2048]{1,0:T(8,128)(2,1)S(1)} %collective-permute-done.refs_1_, bf16[64,2048]{1,0:T(8,128)(2,1)S(1)} %collective-permute-done.1.refs_2_, ...), custom_call_target="tpu_custom_call" | custom-call | flops 805306368 | bytes 4718592 | tf_op jit(solution)/shard_map/pallas_call | solution.py:198
  43.7 13.9 %all-to-all-start = ((bf16[32,24,2048]{2,1,0:T(8,128)(2,1)}), bf16[32,24,2048]{2,1,0:T(8,128)(2,1)}, u32[]{:S(2)}, u32[]{:S(2)}) async-start(bf16[32,24,2048]{2,1,0:T(8,128)(2,1)} %bitcast.8), calls=%async_computation | async-start | bytes 6291456 | tf_op jit(solution)/shard_map/all_to_all | solution.py:303
  57.6 32.8 %collective-permute-done.6.refs_0_ = bf16[576,2048]{1,0:T(8,128)(2,1)S(1)} collective-permute-done((bf16[576,2048]{1,0:T(8,128)(2,1)}, bf16[576,2048]{1,0:T(8,128)(2,1)S(1)}, u32[]{:S(2)}, u32[]{:S(2)}) %collective-permute-start.6) | collective-permute-done | bytes 2359328 | tf_op jit(solution)/shard_map/ppermute | solution.py:281
  90.4 4.2 %collective-permute-start.8 = (bf16[576,2048]{1,0:T(8,128)(2,1)S(1)}, bf16[576,2048]{1,0:T(8,128)(2,1)}, u32[]{:S(2)}, u32[]{:S(2)}) collective-permute-start(bf16[576,2048]{1,0:T(8,128)(2,1)S(1)} %collective-permute-done.6.refs_0_), channel_id=1, source_target_pairs={{1,17},{17,1},{32,48},{48,32},{3,19},{19,3},{34,50},{50,34},{5,21}... | collective-permute-start | bytes 7077896 | tf_op jit(solution)/shard_map/ppermute | solution.py:283
  94.6 1.3 collective-permute-start.10
  95.9 4.4 %collective-permute-start.7 = (bf16[576,2048]{1,0:T(8,128)(2,1)S(1)}, bf16[576,2048]{1,0:T(8,128)(2,1)}, u32[]{:S(2)}, u32[]{:S(2)}) collective-permute-start(bf16[576,2048]{1,0:T(8,128)(2,1)S(1)} %collective-permute-done.6.refs_0_), channel_id=1, source_target_pairs={{0,1},{1,0},{2,3},{3,2},{4,5},{5,4},{6,7},{7,6},{8,9},{9,8},{10,11... | collective-permute-start | bytes 7077896 | tf_op jit(solution)/shard_map/ppermute | solution.py:48
  100.3 20.9 %collective-permute-done.8.refs_4_ = bf16[576,2048]{1,0:T(8,128)(2,1)} collective-permute-done((bf16[576,2048]{1,0:T(8,128)(2,1)S(1)}, bf16[576,2048]{1,0:T(8,128)(2,1)}, u32[]{:S(2)}, u32[]{:S(2)}) %collective-permute-start.8) | collective-permute-done | bytes 2359328 | tf_op jit(solution)/shard_map/ppermute | solution.py:283
  121.2 2.7 %collective-permute-start.9 = (bf16[576,2048]{1,0:T(8,128)(2,1)}, bf16[576,2048]{1,0:T(8,128)(2,1)}, u32[]{:S(2)}, u32[]{:S(2)}) collective-permute-start(bf16[576,2048]{1,0:T(8,128)(2,1)} %collective-permute-done.8.refs_4_), channel_id=1, source_target_pairs={{1,0},{32,33},{3,2},{34,35},{5,4},{36,37},{7,6},{38,39},{9,8},{40,... | collective-permute-start | bytes 7077896 | tf_op jit(solution)/shard_map/ppermute | solution.py:285
  123.9 4.8 %all-to-all-done = bf16[32,24,2048]{2,1,0:T(8,128)(2,1)} async-done(((bf16[32,24,2048]{2,1,0:T(8,128)(2,1)}), bf16[32,24,2048]{2,1,0:T(8,128)(2,1)}, u32[]{:S(2)}, u32[]{:S(2)}) %all-to-all-start) | async-done | bytes 3145760 | tf_op jit(solution)/shard_map/all_to_all | solution.py:303
  128.7 14.6 %shard_map.65 = (bf16[32,96,128]{2,1,0:T(8,128)(2,1)}, bf16[32,288,128]{2,1,0:T(8,128)(2,1)}) custom-call(s32[1]{0:T(128)} %bitcast.5.home_ref, bf16[768,2048]{1,0:T(8,128)(2,1)} %bitcast.9.rows_ref, bf16[576,2048]{1,0:T(8,128)(2,1)} %copy-done.1, bf16[576,2048]{1,0:T(8,128)(2,1)} %collective-permute-done.7.refs_1_, ...), custom_call_target="tpu_custom_call" | custom-call | flops 7247757312 | bytes 15728640 | tf_op jit(solution)/shard_map/pallas_call | solution.py:135
  143.3 12.2 %all-to-all-start.1 = ((bf16[32,288,128]{2,1,0:T(8,128)(2,1)}), bf16[32,288,128]{2,1,0:T(8,128)(2,1)S(1)}, u32[]{:S(2)}, u32[]{:S(2)}) async-start(bf16[32,288,128]{2,1,0:T(8,128)(2,1)} %get-tuple-element.39), calls=%async_computation.1 | async-start | bytes 4718592 | tf_op jit(solution)/shard_map/all_to_all | solution.py:303
  155.5 0.1 slice_convert_fusion
  155.8 0.1 compare_reduce_fusion
  156.0 0.2 fusion.1
  156.3 0.2 fusion.2
  156.4 0.3 slice.34
  156.7 0.2 select_convert_fusion
  156.9 0.3 slice.33
  157.2 1.0 pad_maximum_fusion.1
  158.2 1.2 reshape.135.spread_ref
  159.5 50.2 %all-to-all-done.1 = bf16[32,288,128]{2,1,0:T(8,128)(2,1)S(1)} async-done(((bf16[32,288,128]{2,1,0:T(8,128)(2,1)}), bf16[32,288,128]{2,1,0:T(8,128)(2,1)S(1)}, u32[]{:S(2)}, u32[]{:S(2)}) %all-to-all-start.1) | async-done | bytes 2359328 | tf_op jit(solution)/shard_map/all_to_all | solution.py:303
  209.7 7.7 %all-to-all-start.2 = ((bf16[32,96,128]{2,1,0:T(8,128)(2,1)}), bf16[32,96,128]{2,1,0:T(8,128)(2,1)}, u32[]{:S(2)}, u32[]{:S(2)}) async-start(bf16[32,96,128]{2,1,0:T(8,128)(2,1)} %get-tuple-element.40), calls=%async_computation.2 | async-start | bytes 1572864 | tf_op jit(solution)/shard_map/all_to_all | solution.py:303
  217.4 3.4 %shard_map.66 = (bf16[64,2048]{1,0:T(8,128)(2,1)}, bf16[64,2048]{1,0:T(8,128)(2,1)S(1)}, bf16[64,2048]{1,0:T(8,128)(2,1)S(1)}) custom-call(bf16[9216,128]{1,0:T(8,128)(2,1)S(1)} %bitcast.17, bf16[576,384]{1,0:T(8,128)(2,1)S(1)} %reshape.135.spread_ref), custom_call_target="tpu_custom_call" | custom-call | flops 905969664 | bytes 2359296 | tf_op jit(solution)/shard_map/pallas_call | solution.py:234
  220.7 6.1 %collective-permute-start.11 = (bf16[64,2048]{1,0:T(8,128)(2,1)}, bf16[64,2048]{1,0:T(8,128)(2,1)S(1)}, u32[]{:S(2)}, u32[]{:S(2)}) collective-permute-start(bf16[64,2048]{1,0:T(8,128)(2,1)} %get-tuple-element.44), channel_id=1, source_target_pairs={{0,32},{32,0},{1,33},{33,1},{2,34},{34,2},{3,35},{35,3},{4,36},{36... | collective-permute-start | bytes 786440 | tf_op jit(solution)/shard_map/ppermute | solution.py:48
  226.8 3.0 %collective-permute-start.12 = (bf16[64,2048]{1,0:T(8,128)(2,1)S(1)}, bf16[64,2048]{1,0:T(8,128)(2,1)S(1)}, u32[]{:S(2)}, u32[]{:S(2)}) collective-permute-start(bf16[64,2048]{1,0:T(8,128)(2,1)S(1)} %get-tuple-element.45), channel_id=1, source_target_pairs={{0,112},{16,96},{32,80},{48,64},{64,48},{80,32},{96,16},{112,0},{1... | collective-permute-start | bytes 786440 | tf_op jit(solution)/shard_map/ppermute | solution.py:48
  229.8 4.2 %collective-permute-start.13 = (bf16[64,2048]{1,0:T(8,128)(2,1)S(1)}, bf16[64,2048]{1,0:T(8,128)(2,1)S(1)}, u32[]{:S(2)}, u32[]{:S(2)}) collective-permute-start(bf16[64,2048]{1,0:T(8,128)(2,1)S(1)} %get-tuple-element.46), channel_id=1, source_target_pairs={{0,80},{16,64},{64,16},{80,0},{1,81},{17,65},{65,17},{81,1},{2,82}... | collective-permute-start | bytes 786440 | tf_op jit(solution)/shard_map/ppermute | solution.py:48
  233.9 2.7 %all-to-all-done.2 = bf16[32,96,128]{2,1,0:T(8,128)(2,1)} async-done(((bf16[32,96,128]{2,1,0:T(8,128)(2,1)}), bf16[32,96,128]{2,1,0:T(8,128)(2,1)}, u32[]{:S(2)}, u32[]{:S(2)}) %all-to-all-start.2) | async-done | bytes 786464 | tf_op jit(solution)/shard_map/all_to_all | solution.py:303
  236.6 1.4 reshape.140
  238.0 0.3 fusion.15
  238.3 1.1 collective-permute-done.11
  239.4 1.2 collective-permute-done.12
  240.6 11.6 %collective-permute-done.13 = bf16[64,2048]{1,0:T(8,128)(2,1)S(1)} collective-permute-done((bf16[64,2048]{1,0:T(8,128)(2,1)S(1)}, bf16[64,2048]{1,0:T(8,128)(2,1)S(1)}, u32[]{:S(2)}, u32[]{:S(2)}) %collective-permute-start.13) | collective-permute-done | bytes 262176 | tf_op jit(solution)/shard_map/ppermute | solution.py:48
  252.2 1.0 add_convert_fusion
  (25 shorter events, 0.8 us)
Async XLA Ops:
  0.0 16.3 %collective-permute-start = (bf16[64,2048]{1,0:T(8,128)(2,1)}, bf16[64,2048]{1,0:T(8,128)(2,1)S(1)}, u32[]{:S(2)}, u32[]{:S(2)}) collective-permute-start(bf16[64,2048]{1,0:T(8,128)(2,1)} %refs_0_.1), channel_id=1, source_target_pairs={{0,32},{32,0},{1,33},{33,1},{2,34},{34,2},{3,35},{35,3},{4,36},{36... | collective-permute-start | bytes 786440 | tf_op jit(solution)/shard_map/ppermute | solution.py:48
  5.0 26.3 %collective-permute-start.1 = (bf16[64,2048]{1,0:T(8,128)(2,1)}, bf16[64,2048]{1,0:T(8,128)(2,1)S(1)}, u32[]{:S(2)}, u32[]{:S(2)}) collective-permute-start(bf16[64,2048]{1,0:T(8,128)(2,1)} %refs_0_.1), channel_id=1, source_target_pairs={{0,112},{16,96},{32,80},{48,64},{64,48},{80,32},{96,16},{112,0},{1... | collective-permute-start | bytes 786440 | tf_op jit(solution)/shard_map/ppermute | solution.py:48
  9.7 22.2 %collective-permute-start.2 = (bf16[64,2048]{1,0:T(8,128)(2,1)}, bf16[64,2048]{1,0:T(8,128)(2,1)S(1)}, u32[]{:S(2)}, u32[]{:S(2)}) collective-permute-start(bf16[64,2048]{1,0:T(8,128)(2,1)} %refs_0_.1), channel_id=1, source_target_pairs={{0,80},{16,64},{64,16},{80,0},{1,81},{17,65},{65,17},{81,1},{2,82}... | collective-permute-start | bytes 786440 | tf_op jit(solution)/shard_map/ppermute | solution.py:48
  16.3 15.6 %collective-permute-start.3 = (bf16[64,128]{1,0:T(8,128)(2,1)S(1)}, bf16[64,128]{1,0:T(8,128)(2,1)S(1)}, u32[]{:S(2)}, u32[]{:S(2)}) collective-permute-start(bf16[64,128]{1,0:T(8,128)(2,1)S(1)} %pad_add_fusion.refs_4_), channel_id=1, source_target_pairs={{0,32},{32,0},{1,33},{33,1},{2,34},{34,2},{3,35},{35,3},{4,36},{36... | collective-permute-start | bytes 49160 | tf_op jit(solution)/shard_map/ppermute | solution.py:48
  18.2 14.0 %collective-permute-start.4 = (bf16[64,128]{1,0:T(8,128)(2,1)S(1)}, bf16[64,128]{1,0:T(8,128)(2,1)S(1)}, u32[]{:S(2)}, u32[]{:S(2)}) collective-permute-start(bf16[64,128]{1,0:T(8,128)(2,1)S(1)} %pad_add_fusion.refs_4_), channel_id=1, source_target_pairs={{0,112},{16,96},{32,80},{48,64},{64,48},{80,32},{96,16},{112,0},{1... | collective-permute-start | bytes 49160 | tf_op jit(solution)/shard_map/ppermute | solution.py:48
  23.9 8.7 %collective-permute-start.5 = (bf16[64,128]{1,0:T(8,128)(2,1)S(1)}, bf16[64,128]{1,0:T(8,128)(2,1)S(1)}, u32[]{:S(2)}, u32[]{:S(2)}) collective-permute-start(bf16[64,128]{1,0:T(8,128)(2,1)S(1)} %pad_add_fusion.refs_4_), channel_id=1, source_target_pairs={{0,80},{16,64},{64,16},{80,0},{1,81},{17,65},{65,17},{81,1},{2,82}... | collective-permute-start | bytes 49160 | tf_op jit(solution)/shard_map/ppermute | solution.py:48
  27.9 11.7 %copy-start = (bf16[64,2048]{1,0:T(8,128)(2,1)S(1)}, bf16[64,2048]{1,0:T(8,128)(2,1)}, u32[]{:S(2)}) copy-start(bf16[64,2048]{1,0:T(8,128)(2,1)} %refs_0_.1) | copy-start | bytes 786436
  32.6 57.8 %collective-permute-start.6 = (bf16[576,2048]{1,0:T(8,128)(2,1)}, bf16[576,2048]{1,0:T(8,128)(2,1)S(1)}, u32[]{:S(2)}, u32[]{:S(2)}) collective-permute-start(bf16[576,2048]{1,0:T(8,128)(2,1)} %pad_maximum_fusion.refs_2_), channel_id=1, source_target_pairs={{32,17},{48,1},{17,32},{1,48},{0,16},{16,0},{33,49},{49,33},{34,19... | collective-permute-start | bytes 7077896 | tf_op jit(solution)/shard_map/ppermute | solution.py:281
  43.7 85.0 %all-to-all-start = ((bf16[32,24,2048]{2,1,0:T(8,128)(2,1)}), bf16[32,24,2048]{2,1,0:T(8,128)(2,1)}, u32[]{:S(2)}, u32[]{:S(2)}) async-start(bf16[32,24,2048]{2,1,0:T(8,128)(2,1)} %bitcast.8), calls=%async_computation | async-start | bytes 6291456 | tf_op jit(solution)/shard_map/all_to_all | solution.py:303
  90.4 38.3 %copy-start.1 = (bf16[576,2048]{1,0:T(8,128)(2,1)}, bf16[576,2048]{1,0:T(8,128)(2,1)S(1)}, u32[]{:S(2)}) copy-start(bf16[576,2048]{1,0:T(8,128)(2,1)S(1)} %collective-permute-done.6.refs_0_) | copy-start | bytes 7077892
  90.4 30.8 %collective-permute-start.8 = (bf16[576,2048]{1,0:T(8,128)(2,1)S(1)}, bf16[576,2048]{1,0:T(8,128)(2,1)}, u32[]{:S(2)}, u32[]{:S(2)}) collective-permute-start(bf16[576,2048]{1,0:T(8,128)(2,1)S(1)} %collective-permute-done.6.refs_0_), channel_id=1, source_target_pairs={{1,17},{17,1},{32,48},{48,32},{3,19},{19,3},{34,50},{50,34},{5,21}... | collective-permute-start | bytes 7077896 | tf_op jit(solution)/shard_map/ppermute | solution.py:283
  94.6 29.3 %collective-permute-start.10 = (bf16[576,2048]{1,0:T(8,128)(2,1)}, bf16[576,2048]{1,0:T(8,128)(2,1)}, u32[]{:S(2)}, u32[]{:S(2)}) collective-permute-start(bf16[576,2048]{1,0:T(8,128)(2,1)} %pad_maximum_fusion.refs_2_), channel_id=1, source_target_pairs={{0,1},{33,32},{2,3},{35,34},{4,5},{37,36},{6,7},{39,38},{8,9},{41,... | collective-permute-start | bytes 7077896 | tf_op jit(solution)/shard_map/ppermute | solution.py:284
  95.9 28.0 %collective-permute-start.7 = (bf16[576,2048]{1,0:T(8,128)(2,1)S(1)}, bf16[576,2048]{1,0:T(8,128)(2,1)}, u32[]{:S(2)}, u32[]{:S(2)}) collective-permute-start(bf16[576,2048]{1,0:T(8,128)(2,1)S(1)} %collective-permute-done.6.refs_0_), channel_id=1, source_target_pairs={{0,1},{1,0},{2,3},{3,2},{4,5},{5,4},{6,7},{7,6},{8,9},{9,8},{10,11... | collective-permute-start | bytes 7077896 | tf_op jit(solution)/shard_map/ppermute | solution.py:48
  121.2 7.5 %collective-permute-start.9 = (bf16[576,2048]{1,0:T(8,128)(2,1)}, bf16[576,2048]{1,0:T(8,128)(2,1)}, u32[]{:S(2)}, u32[]{:S(2)}) collective-permute-start(bf16[576,2048]{1,0:T(8,128)(2,1)} %collective-permute-done.8.refs_4_), channel_id=1, source_target_pairs={{1,0},{32,33},{3,2},{34,35},{5,4},{36,37},{7,6},{38,39},{9,8},{40,... | collective-permute-start | bytes 7077896 | tf_op jit(solution)/shard_map/ppermute | solution.py:285
  143.3 66.4 %all-to-all-start.1 = ((bf16[32,288,128]{2,1,0:T(8,128)(2,1)}), bf16[32,288,128]{2,1,0:T(8,128)(2,1)S(1)}, u32[]{:S(2)}, u32[]{:S(2)}) async-start(bf16[32,288,128]{2,1,0:T(8,128)(2,1)} %get-tuple-element.39), calls=%async_computation.1 | async-start | bytes 4718592 | tf_op jit(solution)/shard_map/all_to_all | solution.py:303
  209.7 26.9 %all-to-all-start.2 = ((bf16[32,96,128]{2,1,0:T(8,128)(2,1)}), bf16[32,96,128]{2,1,0:T(8,128)(2,1)}, u32[]{:S(2)}, u32[]{:S(2)}) async-start(bf16[32,96,128]{2,1,0:T(8,128)(2,1)} %get-tuple-element.40), calls=%async_computation.2 | async-start | bytes 1572864 | tf_op jit(solution)/shard_map/all_to_all | solution.py:303
  220.7 18.7 %collective-permute-start.11 = (bf16[64,2048]{1,0:T(8,128)(2,1)}, bf16[64,2048]{1,0:T(8,128)(2,1)S(1)}, u32[]{:S(2)}, u32[]{:S(2)}) collective-permute-start(bf16[64,2048]{1,0:T(8,128)(2,1)} %get-tuple-element.44), channel_id=1, source_target_pairs={{0,32},{32,0},{1,33},{33,1},{2,34},{34,2},{3,35},{35,3},{4,36},{36... | collective-permute-start | bytes 786440 | tf_op jit(solution)/shard_map/ppermute | solution.py:48
  226.8 13.8 %collective-permute-start.12 = (bf16[64,2048]{1,0:T(8,128)(2,1)S(1)}, bf16[64,2048]{1,0:T(8,128)(2,1)S(1)}, u32[]{:S(2)}, u32[]{:S(2)}) collective-permute-start(bf16[64,2048]{1,0:T(8,128)(2,1)S(1)} %get-tuple-element.45), channel_id=1, source_target_pairs={{0,112},{16,96},{32,80},{48,64},{64,48},{80,32},{96,16},{112,0},{1... | collective-permute-start | bytes 786440 | tf_op jit(solution)/shard_map/ppermute | solution.py:48
  229.8 22.5 %collective-permute-start.13 = (bf16[64,2048]{1,0:T(8,128)(2,1)S(1)}, bf16[64,2048]{1,0:T(8,128)(2,1)S(1)}, u32[]{:S(2)}, u32[]{:S(2)}) collective-permute-start(bf16[64,2048]{1,0:T(8,128)(2,1)S(1)} %get-tuple-element.46), channel_id=1, source_target_pairs={{0,80},{16,64},{64,16},{80,0},{1,81},{17,65},{65,17},{81,1},{2,82}... | collective-permute-start | bytes 786440 | tf_op jit(solution)/shard_map/ppermute | solution.py:48
